TPU v7x, 32 devices: a whole 2x2x4 slice. The times are simulated.
32 devices in a mesh: dp: 4 (over z), expert: 8 (over y, x, core).
Axes of the slice: x: 2, y: 2, z: 4, core: 2. Of those that a mesh axis runs over, the one named last changes fastest.
Arguments:
- tokens: bfloat16 [32768, 768], P(('dp', 'expert')), may hold values from -6 to 6
- segments: int32 [32, 1024], P(('dp', 'expert')), may hold values from 0 to 7, never falling along the last dimension, each value on 1 to 512 neighbouring positions
- routes: int32 [32768, 1], P(('dp', 'expert')), may hold values from 0 to 7; in each aligned block of 1024 rows (0 to 1023, 1024 to 2047, ...) at most 256 rows name the same one
- cotangent: bfloat16 [32768, 768], P(('dp', 'expert')), may hold values from -6 to 6
- w_qkv: bfloat16 [768, 2304], replicated, may hold values from -0.21875 to 0.21875
- w_attn_out: bfloat16 [768, 768], replicated, may hold values from -1.25 to 1.25
- gain_attn: float32 [768], replicated, may hold values from 0.5 to 1.5
- gain_ffn: float32 [768], replicated, may hold values from 0.5 to 1.5
- w_router: bfloat16 [768, 16], replicated, may hold values from -0.21875 to 0.21875
- embed: float32 [8, 16], replicated, may hold values from -5 to 5
- w_in: bfloat16 [8, 768, 3072], P('expert'), may hold values from -0.21875 to 0.21875
- w_out: bfloat16 [8, 3072, 768], P('expert'), may hold values from -0.875 to 0.875
Outputs:
- out_tokens: bfloat16 [32768, 768], P(('dp', 'expert'))
- grad_tokens: float32 [32768, 768], P(('dp', 'expert'))
- grad_w_qkv: float32 [768, 2304], replicated
- grad_w_attn_out: float32 [768, 768], replicated
- grad_gain_attn: float32 [768], replicated
- grad_gain_ffn: float32 [768], replicated
- grad_w_router: float32 [768, 16], replicated
- grad_embed: float32 [8, 16], replicated
- grad_w_in: float32 [8, 768, 3072], P('expert', None, 'dp')
- grad_w_out: float32 [8, 3072, 768], P('expert', 'dp')
Inputs may be any that keep to these rules, and one draw needn't show every extreme that they name: `routes`: among the 1024 rows of one device no expert is named more than 256 times, and in every draw some device names some expert exactly 256 times. `segments`: segment numbers never fall along a sequence; a segment has at most half of 1024 tokens, and one has exactly that many.
All inputs are finite; a program needn't handle non-finite values.
Results may differ from a plain program's by a relative error of at most 0.013.
The roundings to bfloat16 on the way count: a program that leaves them out, or rounds other values in their place, can miss the bound.
Values may be sent and summed in bfloat16 or wider, within the bound.
No kernel may reach another device: no remote copies, remote signals or barrier semaphores. Data moves between devices by JAX's collectives and lax.ppermute only.
A program may use at most 384 MiB of HBM per device.

v0:
```python
import math

import jax
import jax.numpy as jnp
from jax import lax
from jax.sharding import PartitionSpec as P

HEADS = 12
HEAD = 64


ROUTER_WARMTH = 0.3
NORM_FLOOR = 12.0
EPSILON = 1e-05
MASK_VALUE = -1e30
TOP_PRECISION = lax.Precision.HIGHEST


def rms_scale(values, gain_vec):
    return (
        values * lax.rsqrt(jnp.mean(values * values, axis=-1, keepdims=True) + EPSILON) * gain_vec
    )


def gate_from_projected(router_projected, embed, routes):
    router_projected = router_projected * lax.rsqrt(
        jnp.maximum(
            jnp.sum(router_projected * router_projected, axis=-1, keepdims=True), NORM_FLOOR
        )
    )
    expert_centroids = embed * lax.rsqrt(
        jnp.maximum(jnp.sum(embed * embed, axis=-1, keepdims=True), NORM_FLOOR)
    )
    router_logits = (
        jnp.dot(router_projected, expert_centroids.T, precision=TOP_PRECISION) / ROUTER_WARMTH
    )
    chances = jax.nn.softmax(router_logits, axis=-1)
    picked = routes == jnp.arange(embed.shape[0], dtype=jnp.int32)[None, :]
    return jnp.sum(jnp.where(picked, chances, 0.0), axis=-1, keepdims=True)


def exact_gelu(values):
    return jax.nn.gelu(values, approximate=False)


def block_scores(query_rows, keys_all, row_start, query_marks, key_marks):
    cosine_scores = jnp.einsum(
        "qhd,khd->hqk", query_rows, keys_all, preferred_element_type=jnp.float32
    ) * HEAD ** (-0.5)
    places = row_start + jnp.arange(query_rows.shape[0])
    columns = jnp.arange(keys_all.shape[0])
    allowed = (places[:, None] >= columns[None, :]) & (query_marks[:, None] == key_marks[None, :])
    return jnp.where(allowed[None], cosine_scores, MASK_VALUE)


def attend_forward(router_projected, seq_marks):
    length = seq_marks.shape[0]
    block_size = math.gcd(512, length)
    queries = router_projected[:, 0]
    keys_all = router_projected[:, 1]
    values_all = router_projected[:, 2]
    mixed_parts = []
    total_parts = []
    for row_start in range(0, length, block_size):
        cosine_scores = block_scores(
            queries[row_start : row_start + block_size],
            keys_all,
            row_start,
            seq_marks[row_start : row_start + block_size],
            seq_marks,
        )
        row_max = jnp.max(cosine_scores, axis=-1, keepdims=True)
        weights = jnp.exp(cosine_scores - row_max)
        row_total = jnp.sum(weights, axis=-1, keepdims=True)
        chances = (weights / row_total).astype(jnp.bfloat16)
        mixed_block = jnp.einsum(
            "hqk,khd->qhd", chances, values_all, preferred_element_type=jnp.float32
        )
        mixed_parts.append(mixed_block.reshape(block_size, -1).astype(jnp.bfloat16))
        total_parts.append(row_max[..., 0] + jnp.log(row_total[..., 0]))
    return (jnp.concatenate(mixed_parts, 0), jnp.concatenate(total_parts, 1))


def attend_backward(router_projected, seq_marks, log_totals, grad_heads):
    length = seq_marks.shape[0]
    block_size = math.gcd(512, length)
    scale = HEAD ** (-0.5)
    queries = router_projected[:, 0]
    keys_all = router_projected[:, 1]
    values_all = router_projected[:, 2]
    grad_keys = jnp.zeros(keys_all.shape, jnp.float32)
    grad_values = jnp.zeros(values_all.shape, jnp.float32)
    query_grads = []
    for row_start in range(0, length, block_size):
        query_rows = queries[row_start : row_start + block_size]
        grad_rows = grad_heads[row_start : row_start + block_size]
        cosine_scores = block_scores(
            query_rows,
            keys_all,
            row_start,
            seq_marks[row_start : row_start + block_size],
            seq_marks,
        )
        chances = jnp.exp(cosine_scores - log_totals[:, row_start : row_start + block_size, None])
        grad_chances = jnp.einsum(
            "qhd,khd->hqk", grad_rows, values_all, preferred_element_type=jnp.float32
        )
        row_delta = jnp.sum(chances * grad_chances, axis=-1, keepdims=True)
        grad_scores = (chances * (grad_chances - row_delta)).astype(jnp.bfloat16)
        query_grads.append(
            jnp.einsum("hqk,khd->qhd", grad_scores, keys_all, preferred_element_type=jnp.float32)
            * scale
        )
        grad_keys = (
            grad_keys
            + jnp.einsum(
                "hqk,qhd->khd", grad_scores, query_rows, preferred_element_type=jnp.float32
            )
            * scale
        )
        grad_values = grad_values + jnp.einsum(
            "hqk,qhd->khd",
            chances.astype(jnp.bfloat16),
            grad_rows,
            preferred_element_type=jnp.float32,
        )
    joined = jnp.stack([jnp.concatenate(query_grads, 0), grad_keys, grad_values], 1)
    return joined.reshape(length, -1).astype(jnp.bfloat16)


def on_device(
    tokens,
    segments,
    routes,
    cotangent,
    w_qkv,
    w_attn_out,
    gain_attn,
    gain_ffn,
    w_router,
    embed,
    w_in,
    w_out,
):
    tok_rows = tokens.shape[0]
    seq_count = segments.shape[0]
    length = segments.shape[1]
    local_experts = w_in.shape[0]
    expert_count = embed.shape[0]
    peer_count = lax.axis_size("expert")
    capacity = 2 * tok_rows // expert_count
    model_width = tokens.shape[1]
    residual_in = tokens.astype(jnp.float32)
    normed_one, norm_one_pull = jax.vjp(rms_scale, residual_in, gain_attn)
    attn_in = normed_one.astype(jnp.bfloat16)
    router_projected = jnp.dot(attn_in, w_qkv, preferred_element_type=jnp.float32).astype(
        jnp.bfloat16
    )
    qkv_seq = router_projected.reshape(seq_count, length, 3, HEADS, HEAD)
    mixed_heads, log_totals = lax.map(
        lambda packed: attend_forward(packed[0], packed[1]), (qkv_seq, segments)
    )
    mixed_heads = mixed_heads.reshape(tok_rows, model_width)
    residual = residual_in + jnp.dot(mixed_heads, w_attn_out, preferred_element_type=jnp.float32)
    normed_two, norm_two_pull = jax.vjp(rms_scale, residual, gain_ffn)
    ffn_in = normed_two.astype(jnp.bfloat16)
    router_proj = jnp.dot(ffn_in, w_router, preferred_element_type=jnp.float32)
    gate_value, gate_pull = jax.vjp(
        lambda proj_in, centers_in: gate_from_projected(proj_in, centers_in, routes),
        router_proj,
        embed,
    )
    chosen = routes[:, 0]
    onehot = (chosen[:, None] == jnp.arange(expert_count, dtype=jnp.int32)[None, :]).astype(
        jnp.int32
    )
    slot_rank = jnp.sum((jnp.cumsum(onehot, axis=0) - 1) * onehot, axis=1)
    slot_index = chosen * capacity + slot_rank

    def to_slots(rows_in):
        filled = (
            jnp.zeros((expert_count * capacity, model_width), rows_in.dtype)
            .at[slot_index]
            .set(rows_in)
        )
        return filled.reshape(peer_count, local_experts * capacity, model_width)

    def expert_rows_of(block, local):
        return block.reshape(peer_count, local_experts, capacity, -1)[:, local].reshape(
            peer_count * capacity, -1
        )

    def stack_back(pieces):
        shaped = [piece.reshape(peer_count, capacity, -1) for piece in pieces]
        return jnp.stack(shaped, 1).reshape(peer_count, local_experts * capacity, -1)

    arrived = lax.all_to_all(to_slots(ffn_in), "expert", split_axis=0, concat_axis=0, tiled=True)
    local = 0
    expert_in = expert_rows_of(arrived, local)
    hidden = jnp.dot(expert_in, w_in[local], preferred_element_type=jnp.float32)
    activated = exact_gelu(hidden).astype(jnp.bfloat16)
    output_batch = [
        jnp.dot(activated, w_out[local], preferred_element_type=jnp.float32).astype(jnp.bfloat16)
    ]
    returned = lax.all_to_all(
        stack_back(output_batch), "expert", split_axis=0, concat_axis=0, tiled=True
    )
    expert_out = returned.reshape(expert_count * capacity, model_width)[slot_index].astype(
        jnp.float32
    )
    out_tokens = (residual + gate_value * expert_out).astype(jnp.bfloat16)
    grad_out = cotangent.astype(jnp.float32)
    grad_gate = jnp.sum(grad_out * expert_out, axis=1, keepdims=True)
    grad_expert = (gate_value * grad_out).astype(jnp.bfloat16)
    grad_arrived = lax.all_to_all(
        to_slots(grad_expert), "expert", split_axis=0, concat_axis=0, tiled=True
    )
    local = 0
    expert_in = expert_rows_of(arrived, local)
    grad_rows = expert_rows_of(grad_arrived, local)
    pre_act = jnp.dot(expert_in, w_in[local], preferred_element_type=jnp.float32)
    activated, slope_pull = jax.vjp(exact_gelu, pre_act)
    out_grads = [
        jnp.dot(activated.astype(jnp.bfloat16).T, grad_rows, preferred_element_type=jnp.float32)
    ]
    grad_act = jnp.dot(grad_rows, w_out[local].T, preferred_element_type=jnp.float32)
    grad_pre = slope_pull(grad_act)[0].astype(jnp.bfloat16)
    in_grads = [jnp.dot(expert_in.T, grad_pre, preferred_element_type=jnp.float32)]
    back_rows = [
        jnp.dot(grad_pre, w_in[local].T, preferred_element_type=jnp.float32).astype(jnp.bfloat16)
    ]
    grad_w_in, grad_w_out = (
        lax.psum_scatter(jnp.stack(in_grads), "dp", scatter_dimension=2, tiled=True),
        lax.psum_scatter(jnp.stack(out_grads), "dp", scatter_dimension=1, tiled=True),
    )
    grad_back = lax.all_to_all(
        stack_back(back_rows), "expert", split_axis=0, concat_axis=0, tiled=True
    )
    grad_from_expert = grad_back.reshape(expert_count * capacity, model_width)[slot_index].astype(
        jnp.float32
    )
    grad_proj, grad_embed = gate_pull(grad_gate)
    grad_from_router = jnp.dot(grad_proj, w_router.astype(jnp.float32).T, precision=TOP_PRECISION)
    grad_router = jnp.dot(ffn_in.astype(jnp.float32).T, grad_proj, precision=TOP_PRECISION)
    grad_resid_part, grad_gain_ffn = norm_two_pull(grad_from_router + grad_from_expert)
    grad_residual = grad_out + grad_resid_part
    grad_branch = grad_residual.astype(jnp.bfloat16)
    grad_w_attn_out = jnp.dot(mixed_heads.T, grad_branch, preferred_element_type=jnp.float32)
    grad_mixed = jnp.dot(grad_branch, w_attn_out.T, preferred_element_type=jnp.float32).astype(
        jnp.bfloat16
    )
    grad_seq = grad_mixed.reshape(seq_count, length, HEADS, HEAD)
    grad_qkv = lax.map(
        lambda packed: attend_backward(packed[0], packed[1], packed[2], packed[3]),
        (qkv_seq, segments, log_totals, grad_seq),
    )
    grad_qkv = grad_qkv.reshape(tok_rows, 3 * model_width)
    grad_w_qkv = jnp.dot(attn_in.T, grad_qkv, preferred_element_type=jnp.float32)
    grad_attn_in = jnp.dot(grad_qkv, w_qkv.T, preferred_element_type=jnp.float32)
    grad_input_part, grad_gain_attn = norm_one_pull(grad_attn_in)
    grad_tokens = grad_residual + grad_input_part
    summed = lax.psum(
        (grad_w_qkv, grad_w_attn_out, grad_gain_attn, grad_gain_ffn, grad_router, grad_embed),
        ("dp", "expert"),
    )
    return (
        out_tokens,
        grad_tokens,
        summed[0],
        summed[1],
        summed[2],
        summed[3],
        summed[4],
        summed[5],
        grad_w_in,
        grad_w_out,
    )


def solution(mesh):
    return jax.shard_map(
        on_device,
        mesh=mesh,
        in_specs=(
            P(("dp", "expert"), None),
            P(("dp", "expert"), None),
            P(("dp", "expert"), None),
            P(("dp", "expert"), None),
            P(),
            P(),
            P(),
            P(),
            P(),
            P(),
            P("expert", None, None),
            P("expert", None, None),
        ),
        out_specs=(
            P(("dp", "expert"), None),
            P(("dp", "expert"), None),
            P(),
            P(),
            P(),
            P(),
            P(),
            P(),
            P("expert", None, "dp"),
            P("expert", "dp", None),
        ),
        check_vma=False,
    )
```

profile of v0, /device:TPU:0, one launch (start us, length us, event | category | flops | bytes accessed | tf_op | source)
XLA Modules:
  0.0 1114.8 jit_solution(10640059930774135630)
XLA Ops:
  40.9 14.6 %fusion.19 = (f32[12,512]{1,0:T(8,128)S(1)}, f32[12,512,1024]{2,1,0:T(8,128)}) fusion(pred[512,1024]{1,0:T(8,128)(4,1)S(1)} %get-tuple-element.82, bf16[1024,3,12,64]{0,3,2,1:T(8,128)(2,1)} %bitcast.134), kind=kOutput, calls=%fused_computation.44 | convolution fusion | flops 824174592 | bytes 28073984 | tf_op jit(solution)/shard_map/while/body/eval_jaxpr/qhd,khd->hqk/dot_general | solution.py:47
  55.6 12.3 %fusion.7 = f32[12,512]{1,0:T(8,128)S(1)} fusion(f32[12,512]{1,0:T(8,128)S(1)} %get-tuple-element.85, f32[12,512,1024]{2,1,0:T(8,128)} %get-tuple-element.86, pred[512,1024]{1,0:T(8,128)(4,1)S(1)} %get-tuple-element.82), kind=kLoop, calls=%fused_computation.34 | loop fusion | flops 25159680 | bytes 25739264 | tf_op jit(solution)/shard_map/while/body/eval_jaxpr/reduce_sum | solution.py:74
  71.0 10.0 fusion.56
  81.0 14.3 %fusion.18 = (f32[12,512]{1,0:T(8,128)S(1)}, f32[12,512,1024]{2,1,0:T(8,128)}) fusion(pred[512,1024]{1,0:T(8,128)(4,1)S(1)} %get-tuple-element.81, bf16[1024,3,12,64]{0,3,2,1:T(8,128)(2,1)} %bitcast.136), kind=kOutput, calls=%fused_computation.43 | convolution fusion | flops 824174592 | bytes 28073984 | tf_op jit(solution)/shard_map/while/body/eval_jaxpr/qhd,khd->hqk/dot_general | solution.py:47
  95.3 12.3 %fusion.6 = f32[12,512]{1,0:T(8,128)S(1)} fusion(f32[12,512]{1,0:T(8,128)S(1)} %get-tuple-element.87, f32[12,512,1024]{2,1,0:T(8,128)} %get-tuple-element.88, pred[512,1024]{1,0:T(8,128)(4,1)S(1)} %get-tuple-element.81), kind=kLoop, calls=%fused_computation.33 | loop fusion | flops 25159680 | bytes 25739264 | tf_op jit(solution)/shard_map/while/body/eval_jaxpr/reduce_sum | solution.py:74
  110.7 10.3 fusion.57
  138.0 43.3 %all_to_all.20 = bf16[8,256,768]{2,1,0:T(8,128)(2,1)S(1)} all-to-all(bf16[8,256,768]{2,1,0:T(8,128)(2,1)} %bitcast.147), channel_id=1, replica_groups=mesh['dp'=4,'expert'=8] {'expert'}, dimensions={0} | all-to-all | bytes 6291456 | tf_op jit(solution)/shard_map/all_to_all | solution.py:197
  181.3 63.4 %multiply_convert_fusion.2 = (bf16[2048,3072]{1,0:T(8,128)(2,1)S(1)}, f32[2048,3072]{1,0:T(8,128)}, f32[2048,3072]{1,0:T(8,128)}) fusion(bf16[2048,768]{1,0:T(8,128)(2,1)S(1)} %bitcast.150, bf16[1,768,3072]{2,1,0:T(8,128)(2,1)} %param.22), kind=kOutput, calls=%fused_computation.13 | convolution fusion | flops 10072621056 | bytes 70778880 | tf_op jit(solution)/shard_map/dot_general | solution.py:200
  244.7 11.2 %fusion.32 = bf16[2048,768]{1,0:T(8,128)(2,1)} fusion(bf16[2048,3072]{1,0:T(8,128)(2,1)S(1)} %get-tuple-element.75, bf16[1,3072,768]{2,1,0:T(8,128)(2,1)S(1)} %copy-done.67), kind=kOutput, calls=%fused_computation.70 | convolution fusion | flops 9665249280 | bytes 20447232 | tf_op jit(solution)/shard_map/dot_general | solution.py:203
  269.4 29.5 %all-to-all-done.1 = bf16[8,256,768]{2,1,0:T(8,128)(2,1)} async-done(((bf16[8,256,768]{2,1,0:T(8,128)(2,1)}), bf16[8,256,768]{2,1,0:T(8,128)(2,1)}, u32[]{:S(2)}, u32[]{:S(2)}) %all-to-all-start.1) | async-done | bytes 3145760 | tf_op jit(solution)/shard_map/all_to_all | solution.py:205
  328.2 42.5 %all_to_all.21 = bf16[8,256,768]{2,1,0:T(8,128)(2,1)} all-to-all(bf16[8,256,768]{2,1,0:T(8,128)(2,1)} %bitcast.146), channel_id=1, replica_groups=mesh['dp'=4,'expert'=8] {'expert'}, dimensions={0} | all-to-all | bytes 6291456 | tf_op jit(solution)/shard_map/all_to_all | solution.py:215
  370.7 32.9 %add_convert_fusion = bf16[2048,3072]{1,0:T(8,128)(2,1)} fusion(f32[2048,3072]{1,0:T(8,128)} %get-tuple-element.76, f32[2048,3072]{1,0:T(8,128)} %get-tuple-element.91, bf16[2048,768]{1,0:T(8,128)(2,1)} %bitcast.152, bf16[1,3072,768]{2,1,0:T(8,128)(2,1)} %param.23), kind=kOutput, calls=%fused_computation.12 | convolution fusion | flops 9751756800 | bytes 70778880 | tf_op jit(solution)/shard_map/dot_general | solution.py:226
  403.5 15.4 %fusion.29 = bf16[2048,768]{1,0:T(8,128)(2,1)} fusion(bf16[2048,3072]{1,0:T(8,128)(2,1)} %add_convert_fusion, bf16[1,768,3072]{2,1,0:T(8,128)(2,1)} %param.22), kind=kOutput, calls=%fused_computation.69 | convolution fusion | flops 9665249280 | bytes 20447232 | tf_op jit(solution)/shard_map/dot_general | solution.py:230
  428.8 32.5 %all-to-all-done.3 = bf16[8,256,768]{2,1,0:T(8,128)(2,1)} async-done(((bf16[8,256,768]{2,1,0:T(8,128)(2,1)}), bf16[8,256,768]{2,1,0:T(8,128)(2,1)}, u32[]{:S(2)}, u32[]{:S(2)}) %all-to-all-start.3) | async-done | bytes 3145760 | tf_op jit(solution)/shard_map/all_to_all | solution.py:236
  486.7 13.1 %fusion.10 = f32[12,64,1024]{2,1,0:T(8,128)} fusion(bf16[512,12,64]{0,2,1:T(8,128)(2,1)S(1)} %bitcast.158, f32[12,512]{1,0:T(8,128)S(1)} %copy-done.28, f32[12,512,1024]{2,1,0:T(8,128)} %get-tuple-element.86, pred[512,1024]{1,0:T(8,128)(4,1)S(1)} %copy-done.13), kind=kOutput, calls=%fused_computation.37 | convolution fusion | flops 830472192 | bytes 29646848 | tf_op jit(solution)/shard_map/while/body/eval_jaxpr/hqk,qhd->khd/dot_general | solution.py:121
  499.7 19.3 %multiply_reduce_fusion = (f32[12,512]{1,0:T(8,128)}, f32[12,512,1024]{2,1,0:T(8,128)}) fusion(f32[12,512]{1,0:T(8,128)} %log_add_fusion, f32[12,512,1024]{2,1,0:T(8,128)} %get-tuple-element.86, pred[512,1024]{1,0:T(8,128)(4,1)} %copy-done.12, bf16[512,12,64]{0,2,1:T(8,128)(2,1)} %bitcast.159, bf16[1024,3,12,64]{0,3,2,1:T(8,128)(2,1)} %bitcast.138), kind=kOutput, calls=%fused_computation.7 | convolution fusion | flops 836757504 | bytes 53272576 | tf_op jit(solution)/shard_map/while/body/eval_jaxpr/qhd,khd->hqk/dot_general | solution.py:105
  519.0 18.8 %multiply_reduce_fusion.1 = (f32[12,512]{1,0:T(8,128)}, f32[12,512,1024]{2,1,0:T(8,128)}) fusion(f32[12,512]{1,0:T(8,128)} %log_add_fusion.1, f32[12,512,1024]{2,1,0:T(8,128)} %get-tuple-element.88, pred[512,1024]{1,0:T(8,128)(4,1)} %copy-done.10, bf16[512,12,64]{0,2,1:T(8,128)(2,1)} %bitcast.156, bf16[1024,3,12,64]{0,3,2,1:T(8,128)(2,1)} %bitcast.139), kind=kOutput, calls=%fused_computation.10 | convolution fusion | flops 836757504 | bytes 53272576 | tf_op jit(solution)/shard_map/while/body/eval_jaxpr/qhd,khd->hqk/dot_general | solution.py:105
  537.8 42.8 %multiply_convert_fusion = (bf16[12,512,1024]{2,1,0:T(8,128)(2,1)}, bf16[12,512,1024]{2,1,0:T(8,128)(2,1)}) fusion(f32[12,512,1024]{2,1,0:T(8,128)} %get-tuple-element.102, f32[12,512]{1,0:T(8,128)} %get-tuple-element.101, f32[12,512]{1,0:T(8,128)} %log_add_fusion, f32[12,512,1024]{2,1,0:T(8,128)} %get-tuple-element.86, pred[512,1024]{1,0:T(8,128)(4,1)} %copy-done.12, ...), kind=kLoop, calls=%fused_computation.6 | loop fusion | flops 75497472 | bytes 126976000 | tf_op jit(solution)/shard_map/while/body/eval_jaxpr/convert_element_type | solution.py:109
  580.6 9.9 fusion.58
  597.8 14.0 %fusion.52 = bf16[1024,1,12,64]{0,3,2,1:T(8,128)(2,1)} fusion(f32[12,64,1024]{2,1,0:T(8,128)} %fusion.10, bf16[512,12,64]{0,2,1:T(8,128)(2,1)S(1)} %bitcast.157, f32[12,512]{1,0:T(8,128)S(1)} %copy-done.27, f32[12,512,1024]{2,1,0:T(8,128)} %get-tuple-element.88, pred[512,1024]{1,0:T(8,128)(4,1)S(1)} %copy-done.11), kind=kOutput, calls=%fused_computation.102 | convolution fusion | flops 832045056 | bytes 31219712 | tf_op jit(solution)/shard_map/while/body/eval_jaxpr/hqk,qhd->khd/dot_general | solution.py:121
  637.7 16.2 %convolution_bitcast_fusion = f32[1,3072,768]{2,1,0:T(8,128)} fusion(bf16[2048,3072]{1,0:T(8,128)(2,1)} %copy-done.71, bf16[2048,768]{1,0:T(8,128)(2,1)} %bitcast.153), kind=kOutput, calls=%fused_computation.50 | convolution fusion | flops 9663676416 | bytes 25165824 | tf_op jit(solution)/shard_map/dot_general | solution.py:224
  653.9 16.5 %convolution_bitcast_fusion.1 = f32[1,768,3072]{2,1,0:T(8,128)} fusion(bf16[2048,768]{1,0:T(8,128)(2,1)} %bitcast.151, bf16[2048,3072]{1,0:T(8,128)(2,1)} %add_convert_fusion), kind=kOutput, calls=%fused_computation.52 | convolution fusion | flops 9663676416 | bytes 25165824 | tf_op jit(solution)/shard_map/dot_general | solution.py:228
  694.1 43.7 %all-reduce = (f32[768]{0:T(1024)}, f32[768]{0:T(1024)}, f32[768,16]{0,1:T(8,128)}, f32[8,16]{1,0:T(8,128)}) all-reduce(f32[768]{0:T(1024)S(1)} %copy-done.64, f32[768]{0:T(1024)S(1)} %copy-done.55, f32[768,16]{0,1:T(8,128)} %fusion.85, f32[8,16]{1,0:T(8,128)S(1)} %copy-done.59), channel_id=1, replica_groups=mesh['dp'=4,'expert'=8] {'dp','expert'}, use_global_device_ids=true, to_apply=%region_26.27 | all-reduce | flops 13952 | bytes 111616 | tf_op jit(solution)/shard_map/psum | solution.py:262
  737.9 361.1 %all-reduce.4.cloned.1.call-done = (f32[768,2304]{1,0:T(8,128)}, f32[768,768]{1,0:T(8,128)}) async-done(((f32[768,2304]{1,0:T(8,128)}, f32[768,768]{1,0:T(8,128)}), (f32[768,2304]{1,0:T(8,128)}, f32[768,768]{1,0:T(8,128)})) %all-reduce.4.cloned.1.call-update) | async-done | bytes 9437200 | tf_op jit(solution)/shard_map/psum | solution.py:262
  (225 shorter events, 198.3 us)
Async XLA Ops:
  8.0 16.8 %copy-start = (bf16[768,2304]{1,0:T(8,128)(2,1)S(1)}, bf16[768,2304]{1,0:T(8,128)(2,1)}, u32[]{:S(2)}) copy-start(bf16[768,2304]{1,0:T(8,128)(2,1)} %param.16) | copy-start | bytes 10616836
  19.3 110.9 %copy-start.58 = (s32[1024,1]{0,1:T(1,128)}, s32[1024,1]{0,1:T(1,128)S(1)}, u32[]{:S(2)}) copy-start(s32[1024,1]{0,1:T(1,128)S(1)} %compare_select_fusion) | copy-start | bytes 12292
  40.9 27.0 %copy-start.12 = (pred[512,1024]{1,0:T(8,128)(4,1)}, pred[512,1024]{1,0:T(8,128)(4,1)S(1)}, u32[]{:S(2)}) copy-start(pred[512,1024]{1,0:T(8,128)(4,1)S(1)} %get-tuple-element.82) | copy-start | bytes 1572868
  40.9 54.3 %copy-start.10 = (pred[512,1024]{1,0:T(8,128)(4,1)}, pred[512,1024]{1,0:T(8,128)(4,1)S(1)}, u32[]{:S(2)}) copy-start(pred[512,1024]{1,0:T(8,128)(4,1)S(1)} %get-tuple-element.81) | copy-start | bytes 1572868
  55.6 12.3 %copy-start.25 = (f32[12,512]{1,0:T(8,128)}, f32[12,512]{1,0:T(8,128)S(1)}, u32[]{:S(2)}) copy-start(f32[12,512]{1,0:T(8,128)S(1)} %get-tuple-element.85) | copy-start | bytes 73732
  55.6 15.4 %copy-start.2 = (f32[12,512,1024]{2,1,0:T(8,128)S(1)}, f32[12,512,1024]{2,1,0:T(8,128)}, u32[]{:S(2)}) copy-start(f32[12,512,1024]{2,1,0:T(8,128)} %get-tuple-element.86) | copy-start | bytes 75497472
  95.3 12.3 %copy-start.26 = (f32[12,512]{1,0:T(8,128)}, f32[12,512]{1,0:T(8,128)S(1)}, u32[]{:S(2)}) copy-start(f32[12,512]{1,0:T(8,128)S(1)} %get-tuple-element.87) | copy-start | bytes 73732
  95.3 15.4 %copy-start.1 = (f32[12,512,1024]{2,1,0:T(8,128)S(1)}, f32[12,512,1024]{2,1,0:T(8,128)}, u32[]{:S(2)}) copy-start(f32[12,512,1024]{2,1,0:T(8,128)} %get-tuple-element.88) | copy-start | bytes 75497472
  110.7 10.3 copy-start.6
  181.3 63.4 %copy-start.19 = (bf16[8,256,768]{2,1,0:T(8,128)(2,1)}, bf16[8,256,768]{2,1,0:T(8,128)(2,1)S(1)}, u32[]{:S(2)}) copy-start(bf16[8,256,768]{2,1,0:T(8,128)(2,1)S(1)} %all_to_all.20) | copy-start | bytes 9437188
  181.3 63.4 %copy-start.67 = (bf16[1,3072,768]{2,1,0:T(8,128)(2,1)S(1)}, bf16[1,3072,768]{2,1,0:T(8,128)(2,1)}, u32[]{:S(2)}) copy-start(bf16[1,3072,768]{2,1,0:T(8,128)(2,1)} %param.23) | copy-start | bytes 14155780
  244.7 11.3 %copy-start.71 = (bf16[2048,3072]{1,0:T(8,128)(2,1)}, bf16[2048,3072]{1,0:T(8,128)(2,1)S(1)}, u32[]{:S(2)}) copy-start(bf16[2048,3072]{1,0:T(8,128)(2,1)S(1)} %get-tuple-element.75) | copy-start | bytes 37748740
  256.0 43.0 %all-to-all-start.1 = ((bf16[8,256,768]{2,1,0:T(8,128)(2,1)}), bf16[8,256,768]{2,1,0:T(8,128)(2,1)}, u32[]{:S(2)}, u32[]{:S(2)}) async-start(bf16[8,256,768]{2,1,0:T(8,128)(2,1)} %bitcast.155), calls=%async_computation.1 | async-start | bytes 6291456 | tf_op jit(solution)/shard_map/all_to_all | solution.py:205
  266.1 206.2 %copy-start.32 = (f32[1024]{0:T(1024)}, f32[1024]{0:T(1024)S(1)}, u32[]{:S(2)}) copy-start(f32[1024]{0:T(1024)S(1)} %maximum_rsqrt_fusion) | copy-start | bytes 12292
  266.9 32.0 %copy-start.44 = (f32[1024]{0:T(1024)}, f32[1024]{0:T(1024)S(1)}, u32[]{:S(2)}) copy-start(f32[1024]{0:T(1024)S(1)} %get-tuple-element.94) | copy-start | bytes 12292
  419.0 42.4 %all-to-all-start.3 = ((bf16[8,256,768]{2,1,0:T(8,128)(2,1)}), bf16[8,256,768]{2,1,0:T(8,128)(2,1)}, u32[]{:S(2)}, u32[]{:S(2)}) async-start(bf16[8,256,768]{2,1,0:T(8,128)(2,1)} %bitcast.154), calls=%async_computation.3 | async-start | bytes 6291456 | tf_op jit(solution)/shard_map/all_to_all | solution.py:236
  423.4 675.5 %all-reduce.4.cloned.1.call-start = ((), (), s32[]{:S(2)}) async-start(), calls=%async_computation.8 | async-start | bytes 18874368 | tf_op jit(solution)/shard_map/psum | solution.py:262
  428.8 43.5 %copy-start.38 = (f32[1024]{0:T(1024)}, f32[1024]{0:T(1024)S(1)}, u32[]{:S(2)}) copy-start(f32[1024]{0:T(1024)S(1)} %select_multiply_fusion.1) | copy-start | bytes 12292
  461.3 11.0 copy-start.37
  461.3 11.0 copy-start.47
  590.5 21.3 %slice-start = ((s8[4718592]{0:T(1024)(128)(4,1)}), s8[4194304]{0:T(1024)(128)(4,1)S(1)}, s32[]{:S(2)}) async-start(s8[4718592]{0:T(1024)(128)(4,1)} %bitcast.142), calls=%async_computation.9 | async-start | bytes 8388608
  597.8 14.0 %slice-start.1 = ((s8[4718592]{0:T(1024)(128)(4,1)}), s8[524288]{0:T(1024)(128)(4,1)S(1)}, s32[]{:S(2)}) async-start(s8[4718592]{0:T(1024)(128)(4,1)} %bitcast.142), calls=%async_computation.10 | async-start | bytes 1048576
  637.6 461.4 %reduce-scatter.5.cloned.1.call-start = ((), (), s32[]{:S(2)}) async-start(), calls=%async_computation.7 | async-start | bytes 11796480 | tf_op jit(solution)/shard_map/reduce_scatter | solution.py:234
  653.9 445.1 %reduce-scatter.3.cloned.1.call-start = ((), (), s32[]{:S(2)}) async-start(), calls=%async_computation.6 | async-start | bytes 11796480 | tf_op jit(solution)/shard_map/reduce_scatter | solution.py:233
  (55 other events, 229.0 us)
Sparse Core Ops, SparseCore 0:
  637.7 461.2 all-reduce.3
Sparse Core Ops, SparseCore 1:
  653.9 192.4 reduce-scatter.4
  849.3 170.3 reduce-scatter.2
where the time goes:
time: 1120 us; the launch traced here: 1110 us
  waiting for transfers between devices  423 us (38%)
  matrix products  347 us (31%)
  blocking collectives  129 us (12%)
  other arithmetic  102 us (9%)
  local copies, waits for them, and re-layouts  87.8 us (8%)
  between operations  16.6 us (1%)
    psum x1, waiting for transfers between devices, on_device(): lax.psum((grad_w_qkv, grad_w_attn_out, grad_gain_attn, grad_gain_ffn, gra...  361 us
    dot_general x1, matrix products, on_device(): hidden = jnp.dot(expert_in, w_in[local], preferred_element_type=jnp.float32)  63.4 us
    psum x1, blocking collectives, on_device(): lax.psum((grad_w_qkv, grad_w_attn_out, grad_gain_attn, grad_gain_ffn, gra...  43.7 us
    all_to_all x1, blocking collectives, on_device(): lax.all_to_all(to_slots(ffn_in), 'expert', split_axis=0, concat_axis=0, t...  43.3 us
    convert_element_type x1, other arithmetic, attend_backward(): grad_scores = (chances * (grad_chances - row_delta)).astype(jnp.bfloat16)  42.8 us
    all_to_all x1, blocking collectives, on_device(): lax.all_to_all(to_slots(grad_expert), 'expert', split_axis=0, concat_axis...  42.5 us
    dot_general x2, matrix products, attend_backward(): jnp.einsum('qhd,khd->hqk', grad_rows, values_all, preferred_element_type=...  38.1 us
    unnamed x154, local copies, waits for them, and re-layouts  35.2 us
  transfers between devices with their start and end apart: 5, of which 3 were waited for; matrix products, arithmetic and copies ran while one was open for 6% of the time, Pallas kernels for 0%

commit v1 on v0

v1 whole, which is shorter than its diff:
```python
import functools

import jax
import jax.numpy as jnp
from jax import lax
from jax.experimental import pallas as pl
from jax.experimental.pallas import tpu as pltpu
from jax.sharding import PartitionSpec as P

HEADS = 12
HEAD = 64
PAIRS = HEADS // 2
PAIR = 2 * HEAD
QB = 256
LANES = 128
ROUTER_WARMTH = 0.3
NORM_FLOOR = 12.0
EPSILON = 1e-05
MASK_VALUE = -1e30
F32 = jnp.float32
BF16 = jnp.bfloat16
I32 = jnp.int32
NN = (((1,), (0,)), ((), ()))
NT = (((1,), (1,)), ((), ()))
TN = (((0,), (0,)), ((), ()))
HIGHEST = lax.Precision.HIGHEST
MIB = 1 << 20


def mm(a, b, dims=NN, precision=None):
    return lax.dot_general(a, b, dims, precision=precision, preferred_element_type=F32)


def params(mib):
    return pltpu.CompilerParams(vmem_limit_bytes=mib * MIB)


def cost(flops, nbytes):
    return pl.CostEstimate(flops=int(flops), bytes_accessed=int(nbytes), transcendentals=0)


def whole(shape):
    return pl.BlockSpec(
        shape, lambda *_: (0,) * len(shape), pipeline_mode=pl.Buffered(buffer_count=1)
    )


def smem():
    return pl.BlockSpec(memory_space=pltpu.SMEM)


def ones_where(mask):
    return jnp.where(mask, 1.0, 0.0).astype(BF16)


def dispatch(me, key_row, rows, out_refs):
    cap = out_refs[0].shape[0]
    slot = lax.broadcasted_iota(I32, (cap, key_row.shape[1]), 0)
    for d, ref in enumerate(out_refs):
        target = slot + (me ^ d) * cap
        ref[...] = mm(ones_where(key_row == target), rows).astype(BF16)


def place_kernel(me_ref, rr_ref, rc_ref, cot_ref, keyr_ref, keyc_ref, *out_refs):
    toks = cot_ref.shape[0]
    peers = len(out_refs)
    cap = out_refs[0].shape[0]
    rr, rc = rr_ref[...], rc_ref[...]
    before = ones_where(
        lax.broadcasted_iota(I32, (toks, toks), 0) <= lax.broadcasted_iota(I32, (toks, toks), 1)
    )
    hot_row = jnp.where(lax.broadcasted_iota(I32, (peers, toks), 0) == rr, 1.0, 0.0)
    upto = mm(hot_row.astype(BF16), before)
    rank = jnp.sum(hot_row * upto, axis=0, keepdims=True) - 1.0
    key_row = rr * cap + rank.astype(I32)
    keyr_ref[...] = key_row
    after = ones_where(
        lax.broadcasted_iota(I32, (toks, toks), 0) >= lax.broadcasted_iota(I32, (toks, toks), 1)
    )
    hot_col = jnp.where(lax.broadcasted_iota(I32, (toks, LANES), 1) == rc, 1.0, 0.0)
    upto_col = mm(after, hot_col.astype(BF16))
    rank_col = jnp.sum(hot_col * upto_col, axis=1, keepdims=True) - 1.0
    keyc_ref[...] = rc * cap + rank_col.astype(I32)
    dispatch(me_ref[0], key_row, cot_ref[...], out_refs)


def place(me, routes, cot, peers, cap):
    toks, width = cot.shape
    block = jax.ShapeDtypeStruct((cap, width), BF16)
    return pl.pallas_call(
        place_kernel,
        out_shape=[
            jax.ShapeDtypeStruct((1, toks), I32),
            jax.ShapeDtypeStruct((toks, 1), I32),
        ]
        + [block] * peers,
        in_specs=[smem()] + [pl.BlockSpec(memory_space=pltpu.VMEM)] * 3,
        compiler_params=params(40),
        cost_estimate=cost(2 * peers * cap * toks * width, 3 * toks * width * 2),
        name="place",
    )(me, routes.reshape(1, toks), routes, cot)


def band(i):
    return max(0, i - 2) * QB, (i + 1) * QB


def fill_bias(bias_ref, segr, segc, count):
    for i in range(count):
        low, high = band(i)
        keys = lax.broadcasted_iota(I32, (high - low, QB), 0) + low
        queries = lax.broadcasted_iota(I32, (high - low, QB), 1) + i * QB
        same = segc[low:high] == segr[:, i * QB : (i + 1) * QB]
        bias_ref[i, : high - low, :] = jnp.where((keys <= queries) & same, 0.0, MASK_VALUE)


def head_mask(values, h):
    lane = lax.broadcasted_iota(I32, values.shape, 1)
    return jnp.where((lane >= h * HEAD) & (lane < (h + 1) * HEAD), values, jnp.zeros_like(values))


def attend_kernel(
    peers,
    me_ref,
    tok_ref,
    segr_ref,
    segc_ref,
    keyr_ref,
    wq_ref,
    wk_ref,
    wv_ref,
    wo_ref,
    ga_ref,
    gf_ref,
    q_ref,
    k_ref,
    v_ref,
    lse_ref,
    mixt_ref,
    attn_ref,
    res_ref,
    *rest,
):
    out_refs, (bias_ref, mix_ref) = rest[:peers], rest[peers:]
    p = pl.program_id(0)
    toks, width = tok_ref.shape
    count = toks // QB

    @pl.when(p == 0)
    def _():
        fill_bias(bias_ref, segr_ref[...], segc_ref[...], count)
        x = tok_ref[...].astype(F32)
        inv = lax.rsqrt(jnp.mean(x * x, axis=1, keepdims=True) + EPSILON)
        attn_ref[...] = (x * inv * ga_ref[...]).astype(BF16)

    attn_in = attn_ref[...]
    q_ref[...] = mm(attn_in, wq_ref[...]).astype(BF16)
    k_ref[...] = mm(attn_in, wk_ref[...]).astype(BF16)
    v = mm(attn_in, wv_ref[...])
    v_ref[...] = v.astype(BF16)
    vt = v.T.astype(BF16)
    for i in range(count):
        low, high = band(i)
        cols = slice(i * QB, (i + 1) * QB)
        q = q_ref[cols, :] * HEAD**-0.5
        keys = k_ref[low:high, :]
        parts = []
        for h in range(2):
            s = mm(keys, head_mask(q, h), NT) + bias_ref[i, : high - low, :]
            top = jnp.max(s, axis=0, keepdims=True)
            w = jnp.exp(s - top)
            total = jnp.sum(w, axis=0, keepdims=True)
            lse_ref[0, h : h + 1, cols] = top + jnp.log(total)
            chances = (w * (1.0 / total)).astype(BF16)
            parts.append(mm(vt[h * HEAD : (h + 1) * HEAD, low:high], chances))
        mixt_ref[:, cols] = jnp.concatenate(parts, axis=0).astype(BF16)
    mix_ref[pl.ds(pl.multiple_of(p * PAIR, PAIR), PAIR), :] = mixt_ref[...]

    @pl.when(p == pl.num_programs(0) - 1)
    def _():
        res = tok_ref[...].astype(F32) + mm(mix_ref[...], wo_ref[...], TN)
        res_ref[...] = res
        inv = lax.rsqrt(jnp.mean(res * res, axis=1, keepdims=True) + EPSILON)
        ffn_in = (res * inv * gf_ref[...]).astype(BF16)
        dispatch(me_ref[0], keyr_ref[...], ffn_in, out_refs)


def attend(me, tokens, segr, segc, keyr, w_qkv, w_o, ga, gf, peers, cap):
    toks, width = tokens.shape
    pair_cols = pl.BlockSpec((toks, PAIR), lambda p: (0, p))
    heads = jax.ShapeDtypeStruct((toks, width), BF16)
    block = jax.ShapeDtypeStruct((cap, width), BF16)
    weights = [
        pl.BlockSpec((width, PAIR), lambda p, part=part: (0, part * PAIRS + p)) for part in range(3)
    ]
    return pl.pallas_call(
        functools.partial(attend_kernel, peers),
        grid=(PAIRS,),
        in_specs=[
            smem(),
            whole((toks, width)),
            whole((1, toks)),
            whole((toks, 1)),
            whole((1, toks)),
            *weights,
            whole((width, width)),
            whole((1, width)),
            whole((1, width)),
        ],
        out_specs=[
            pair_cols,
            pair_cols,
            pair_cols,
            pl.BlockSpec((1, 2, toks), lambda p: (p, 0, 0)),
            pl.BlockSpec((PAIR, toks), lambda p: (p, 0)),
            whole((toks, width)),
            whole((toks, width)),
        ]
        + [whole((cap, width))] * peers,
        out_shape=[
            heads,
            heads,
            heads,
            jax.ShapeDtypeStruct((PAIRS, 2, toks), F32),
            jax.ShapeDtypeStruct((width, toks), BF16),
            heads,
            jax.ShapeDtypeStruct((toks, width), F32),
        ]
        + [block] * peers,
        scratch_shapes=[
            pltpu.VMEM((toks // QB, 3 * QB, QB), F32),
            pltpu.VMEM((width, toks), BF16),
        ],
        compiler_params=params(56),
        cost_estimate=cost(20e9, 20e6),
        name="attend",
    )(me, tokens, segr, segc, keyr, w_qkv, w_qkv, w_qkv, w_o, ga, gf)


def attend_back_kernel(
    segr_ref,
    segc_ref,
    q_ref,
    k_ref,
    v_ref,
    lse_ref,
    mixt_ref,
    gb_ref,
    attnt_ref,
    wo_ref,
    wq_ref,
    wk_ref,
    wv_ref,
    gin_ref,
    gwo_ref,
    gwq_ref,
    gwk_ref,
    gwv_ref,
    gatt_ref,
    bias_ref,
    dqt_ref,
    dk_ref,
    dv_ref,
    do_ref,
):
    p = pl.program_id(0)
    toks, width = gb_ref.shape
    count = toks // QB
    scale = HEAD**-0.5

    @pl.when(p == 0)
    def _():
        fill_bias(bias_ref, segr_ref[...], segc_ref[...], count)
        gatt_ref[...] = gin_ref[...]

    gb = gb_ref[...]
    do_ref[...] = mm(gb, wo_ref[...], NT).astype(BF16)
    dot_ = mm(wo_ref[...], gb, NT).astype(BF16).astype(F32)
    mixt = mixt_ref[...]
    gwo_ref[...] = mm(mixt, gb).astype(BF16)
    weighted = dot_ * mixt.astype(F32)
    delta = [
        jnp.sum(weighted[h * HEAD : (h + 1) * HEAD], axis=0, keepdims=True) for h in range(2)
    ]
    kt = k_ref[...].astype(F32).T.astype(BF16)
    dk_ref[...] = jnp.zeros_like(dk_ref)
    dv_ref[...] = jnp.zeros_like(dv_ref)
    for i in range(count):
        low, high = band(i)
        cols = slice(i * QB, (i + 1) * QB)
        q = q_ref[cols, :] * scale
        do = do_ref[cols, :]
        keys = k_ref[low:high, :]
        values = v_ref[low:high, :]
        dk_add, dv_add, dqs = [], [], []
        for h in range(2):
            qm, dom = head_mask(q, h), head_mask(do, h)
            s = mm(keys, qm, NT) + bias_ref[i, : high - low, :]
            pr = jnp.exp(s - lse_ref[0, h : h + 1, cols])
            dpr = mm(values, dom, NT)
            ds = (pr * (dpr - delta[h][:, cols])).astype(BF16)
            dv_add.append(mm(pr.astype(BF16), dom))
            dk_add.append(mm(ds, qm))
            dqs.append(mm(kt[h * HEAD : (h + 1) * HEAD, low:high], ds))
        dk_ref[low:high, :] += dk_add[0] + dk_add[1]
        dv_ref[low:high, :] += dv_add[0] + dv_add[1]
        dqt_ref[:, cols] = jnp.concatenate(dqs, axis=0) * scale
    grads = [
        dqt_ref[...].T.astype(BF16),
        dk_ref[...].astype(BF16),
        dv_ref[...].astype(BF16),
    ]
    attnt = attnt_ref[...]
    for grad, ref in zip(grads, (gwq_ref, gwk_ref, gwv_ref)):
        ref[...] = mm(attnt, grad).astype(BF16)
    joined = jnp.concatenate(grads, axis=1)
    weights = jnp.concatenate([wq_ref[...], wk_ref[...], wv_ref[...]], axis=1)
    gatt_ref[...] += mm(joined, weights, NT)


def attend_back(first, pairs, segr, segc, q, k, v, lse, mixt, gb, attnt, w_o, w_qkv, gin):
    toks, width = gb.shape
    pair_cols = pl.BlockSpec((toks, PAIR), lambda p: (0, first + p))
    weights = [
        pl.BlockSpec((width, PAIR), lambda p, part=part: (0, part * PAIRS + first + p))
        for part in range(3)
    ]
    grad_cols = pl.BlockSpec((width, PAIR), lambda p: (0, p))
    grad_w = jax.ShapeDtypeStruct((width, pairs * PAIR), BF16)
    return pl.pallas_call(
        attend_back_kernel,
        grid=(pairs,),
        in_specs=[
            whole((1, toks)),
            whole((toks, 1)),
            pair_cols,
            pair_cols,
            pair_cols,
            pl.BlockSpec((1, 2, toks), lambda p: (first + p, 0, 0)),
            pl.BlockSpec((PAIR, toks), lambda p: (first + p, 0)),
            whole((toks, width)),
            whole((width, toks)),
            pl.BlockSpec((PAIR, width), lambda p: (first + p, 0)),
            *weights,
            whole((toks, width)),
        ],
        out_specs=[
            pl.BlockSpec((PAIR, width), lambda p: (p, 0)),
            grad_cols,
            grad_cols,
            grad_cols,
            whole((toks, width)),
        ],
        out_shape=[
            jax.ShapeDtypeStruct((pairs * PAIR, width), BF16),
            grad_w,
            grad_w,
            grad_w,
            jax.ShapeDtypeStruct((toks, width), F32),
        ],
        scratch_shapes=[
            pltpu.VMEM((toks // QB, 3 * QB, QB), F32),
            pltpu.VMEM((PAIR, toks), F32),
            pltpu.VMEM((toks, PAIR), F32),
            pltpu.VMEM((toks, PAIR), F32),
            pltpu.VMEM((toks, PAIR), BF16),
        ],
        compiler_params=params(56),
        cost_estimate=cost(pairs * 5e9, 20e6),
        name="attend_back",
    )(segr, segc, q, k, v, lse, mixt, gb, attnt, w_o, w_qkv, w_qkv, w_qkv, gin)


def unit_rows(values):
    total = jnp.sum(values * values, axis=1, keepdims=True)
    return lax.rsqrt(jnp.maximum(total, NORM_FLOOR)), total


def unit_rows_back(values, inv, total, grad):
    passed = jnp.where(total > NORM_FLOOR, 1.0, jnp.where(total == NORM_FLOOR, 0.5, 0.0))
    inner = jnp.sum(grad * values, axis=1, keepdims=True)
    return inv * grad - passed * inv * inv * inv * inner * values


def gelu_and_slope(h):
    cdf = 0.5 + 0.5 * lax.erf(h * 0.7071067811865476)
    pdf = 0.3989422804014327 * jnp.exp(-0.5 * h * h)
    return h * cdf, cdf + h * pdf


def expert_kernel(peers, experts, me_ref, wr_ref, emb_ref, win_ref, wout_ref, *rest):
    x_refs, rest = rest[:peers], rest[peers:]
    g_refs, rest = rest[:peers], rest[peers:]
    gwin_ref, gwout_ref, gwr_ref, gemb_ref = rest[:4]
    rest = rest[4:]
    fout_refs, rest = rest[:peers], rest[peers:]
    gout_refs, rest = rest[:peers], rest[peers:]
    x_s, xt_s, g_s, act_s, gp_s, out_s, gin_s, acc_s = rest
    c = pl.program_id(0)
    rows = x_s.shape[0]
    cap = x_refs[0].shape[0]
    me = me_ref[0]
    step = min(QB, rows)

    def route(block):
        z = mm(block, wr_ref[...])
        inv, total = unit_rows(z)
        zn = z * inv
        einv, _ = unit_rows(emb_ref[...])
        en = emb_ref[...] * einv
        logits = mm(zn, en, NT, HIGHEST) / ROUTER_WARMTH
        lane = lax.broadcasted_iota(I32, logits.shape, 1)
        logits = jnp.where(lane < experts, logits, MASK_VALUE)
        w = jnp.exp(logits - jnp.max(logits, axis=1, keepdims=True))
        chances = w / jnp.sum(w, axis=1, keepdims=True)
        mine = lane == me
        gate = jnp.sum(jnp.where(mine, chances, 0.0), axis=1, keepdims=True)
        return z, inv, total, zn, en, chances, mine, gate

    @pl.when(c == 0)
    def _():
        for d in range(peers):
            x_s[d * cap : (d + 1) * cap, :] = x_refs[d][...]
            g_s[d * cap : (d + 1) * cap, :] = g_refs[d][...]
        for r in range(0, rows, step):
            block = x_s[r : r + step, :]
            xt_s[:, r : r + step] = block.T
            gate = route(block)[-1]
            g_s[r : r + step, :] = (gate * g_s[r : r + step, :].astype(F32)).astype(BF16)
        out_s[...] = jnp.zeros_like(out_s)
        gin_s[...] = jnp.zeros_like(gin_s)
        acc_s[...] = jnp.zeros_like(acc_s)

    w_in, w_out = win_ref[0], wout_ref[0]
    for r in range(0, rows, step):
        part = slice(r, r + step)
        h = mm(x_s[part, :], w_in)
        act, slope = gelu_and_slope(h)
        act_s[part, :] = act.astype(BF16)
        ga = mm(g_s[part, :], w_out, NT)
        gp_s[part, :] = (ga * slope).astype(BF16)
        prod = act * ga
        folded = prod[:, :LANES]
        for j in range(LANES, prod.shape[1], LANES):
            folded = folded + prod[:, j : j + LANES]
        acc_s[part, :] += folded
    act16, gp16 = act_s[...], gp_s[...]
    out_s[...] += mm(act16, w_out)
    gin_s[...] += mm(gp16, w_in, NT)
    gwout_ref[...] = mm(act16, g_s[...], TN).astype(BF16)
    gwin_ref[0] = mm(xt_s[...], gp16).astype(BF16)

    @pl.when(c == pl.num_programs(0) - 1)
    def _():
        gwr = jnp.zeros(gwr_ref.shape, F32)
        gen = jnp.zeros(gemb_ref.shape, F32)
        for r in range(0, rows, step):
            part = slice(r, r + step)
            z, inv, total, zn, en, chances, mine, gate = route(x_s[part, :])
            weight = jnp.sum(acc_s[part, :], axis=1, keepdims=True)
            dl = weight * (jnp.where(mine, 1.0, 0.0) - chances) / ROUTER_WARMTH
            gen = gen + mm(dl, zn, TN, HIGHEST)
            dz = unit_rows_back(z, inv, total, mm(dl, en, NN, HIGHEST))
            dz_top = dz.astype(BF16)
            dz_low = (dz - dz_top.astype(F32)).astype(BF16)
            back = gin_s[part, :].astype(BF16).astype(F32)
            back = back + mm(dz_top, wr_ref[...], NT) + mm(dz_low, wr_ref[...], NT)
            gin_s[part, :] = back
            xt = xt_s[:, part]
            gwr = gwr + mm(xt, dz_top) + mm(xt, dz_low)
            out_s[part, :] = gate * out_s[part, :].astype(BF16).astype(F32)
        for d in range(peers):
            gout_refs[d][...] = gin_s[d * cap : (d + 1) * cap, :].astype(BF16)
            fout_refs[d][...] = out_s[d * cap : (d + 1) * cap, :].astype(BF16)
        gwr_ref[...] = gwr
        einv, etotal = unit_rows(emb_ref[...])
        gemb_ref[...] = unit_rows_back(emb_ref[...], einv, etotal, gen)


def expert(me, wr, emb, w_in, w_out, xs, gs, experts, shards):
    peers = len(xs)
    cap, width = xs[0].shape
    hidden = w_in.shape[2]
    share = hidden // shards
    wide = 256 if share % 256 == 0 else 128
    per = share // wide
    rows = peers * cap
    block = jax.ShapeDtypeStruct((cap, width), BF16)
    return pl.pallas_call(
        functools.partial(expert_kernel, peers, experts),
        grid=(hidden // wide,),
        in_specs=[
            smem(),
            whole(wr.shape),
            whole(emb.shape),
            pl.BlockSpec((1, width, wide), lambda c: (0, 0, c)),
            pl.BlockSpec((1, wide, width), lambda c: (0, c, 0)),
        ]
        + [whole((cap, width))] * (2 * peers),
        out_specs=[
            pl.BlockSpec((1, width, wide), lambda c: (c // per, 0, c % per)),
            pl.BlockSpec((wide, width), lambda c: (c, 0)),
            whole((width, LANES)),
            whole(emb.shape),
        ]
        + [whole((cap, width))] * (2 * peers),
        out_shape=[
            jax.ShapeDtypeStruct((shards, width, share), BF16),
            jax.ShapeDtypeStruct((hidden, width), BF16),
            jax.ShapeDtypeStruct((width, LANES), F32),
            jax.ShapeDtypeStruct(emb.shape, F32),
        ]
        + [block] * (2 * peers),
        scratch_shapes=[
            pltpu.VMEM((rows, width), BF16),
            pltpu.VMEM((width, rows), BF16),
            pltpu.VMEM((rows, width), BF16),
            pltpu.VMEM((rows, wide), BF16),
            pltpu.VMEM((rows, wide), BF16),
            pltpu.VMEM((rows, width), F32),
            pltpu.VMEM((rows, width), F32),
            pltpu.VMEM((rows, LANES), F32),
        ],
        compiler_params=params(60),
        cost_estimate=cost(12 * rows * width * hidden, 50e6),
        name="expert",
    )(me, wr, emb, w_in, w_out, *xs, *gs)


def gather_rows(me, keys, rows_ref, peers):
    total = rows_ref.shape[0]
    cap = total // peers
    column = lax.broadcasted_iota(I32, (keys.shape[0], total), 1)
    target = ((column // cap) ^ me) * cap + column % cap
    return mm(ones_where(keys == target), rows_ref[...])


def stage_rows(block_refs, rows_ref):
    cap = block_refs[0].shape[0]

    @pl.when(pl.program_id(0) == 0)
    def _():
        for d, ref in enumerate(block_refs):
            rows_ref[d * cap : (d + 1) * cap, :] = ref[...]


def combine_back_kernel(peers, me_ref, keyc_ref, res_ref, cot_ref, gf_ref, *rest):
    gres_ref, gb_ref, gain_ref, rows_ref = rest[peers:]
    stage_rows(rest[:peers], rows_ref)
    dy = gather_rows(me_ref[0], keyc_ref[...], rows_ref, peers)
    x = res_ref[...]
    inv = lax.rsqrt(jnp.mean(x * x, axis=1, keepdims=True) + EPSILON)

    @pl.when(pl.program_id(0) == 0)
    def _():
        gain_ref[...] = jnp.zeros_like(gain_ref)

    gain_ref[...] += jnp.sum(dy * x * inv, axis=0, keepdims=True)
    dn = dy * gf_ref[...]
    dx = inv * dn - x * (inv * inv * inv * jnp.mean(x * dn, axis=1, keepdims=True))
    grad = cot_ref[...].astype(F32) + dx
    gres_ref[...] = grad
    gb_ref[...] = grad.astype(BF16)


def combine_back(me, keyc, res, cot, gf, blocks):
    toks, width = res.shape
    peers = len(blocks)
    cap = blocks[0].shape[0]
    tile = pl.BlockSpec((QB, width), lambda i: (i, 0))
    return pl.pallas_call(
        functools.partial(combine_back_kernel, peers),
        grid=(toks // QB,),
        in_specs=[smem(), pl.BlockSpec((QB, 1), lambda i: (i, 0)), tile, tile, whole((1, width))]
        + [whole((cap, width))] * peers,
        out_specs=[tile, tile, whole((1, width))],
        out_shape=[
            jax.ShapeDtypeStruct((toks, width), F32),
            jax.ShapeDtypeStruct((toks, width), BF16),
            jax.ShapeDtypeStruct((1, width), F32),
        ],
        scratch_shapes=[pltpu.VMEM((peers * cap, width), BF16)],
        compiler_params=params(40),
        cost_estimate=cost(2 * toks * peers * cap * width, 15e6),
        name="combine_back",
    )(me, keyc, res, cot, gf, *blocks)


def combine_kernel(peers, me_ref, keyc_ref, res_ref, *rest):
    out_ref, rows_ref = rest[peers:]
    stage_rows(rest[:peers], rows_ref)
    back = gather_rows(me_ref[0], keyc_ref[...], rows_ref, peers)
    out_ref[...] = (res_ref[...] + back).astype(BF16)


def combine(me, keyc, res, blocks):
    toks, width = res.shape
    peers = len(blocks)
    cap = blocks[0].shape[0]
    tile = pl.BlockSpec((QB, width), lambda i: (i, 0))
    return pl.pallas_call(
        functools.partial(combine_kernel, peers),
        grid=(toks // QB,),
        in_specs=[smem(), pl.BlockSpec((QB, 1), lambda i: (i, 0)), tile]
        + [whole((cap, width))] * peers,
        out_specs=tile,
        out_shape=jax.ShapeDtypeStruct((toks, width), BF16),
        scratch_shapes=[pltpu.VMEM((peers * cap, width), BF16)],
        compiler_params=params(40),
        cost_estimate=cost(2 * toks * peers * cap * width, 10e6),
        name="combine",
    )(me, keyc, res, *blocks)


def norm_back_kernel(gatt_ref, tok_ref, gres_ref, ga_ref, out_ref, gain_ref):
    dy = gatt_ref[...]
    x = tok_ref[...].astype(F32)
    inv = lax.rsqrt(jnp.mean(x * x, axis=1, keepdims=True) + EPSILON)

    @pl.when(pl.program_id(0) == 0)
    def _():
        gain_ref[...] = jnp.zeros_like(gain_ref)

    gain_ref[...] += jnp.sum(dy * x * inv, axis=0, keepdims=True)
    dn = dy * ga_ref[...]
    dx = inv * dn - x * (inv * inv * inv * jnp.mean(x * dn, axis=1, keepdims=True))
    out_ref[...] = gres_ref[...] + dx


def norm_back(gatt, tokens, gres, ga):
    toks, width = tokens.shape
    tile = pl.BlockSpec((QB, width), lambda i: (i, 0))
    return pl.pallas_call(
        norm_back_kernel,
        grid=(toks // QB,),
        in_specs=[tile, tile, tile, whole((1, width))],
        out_specs=[tile, whole((1, width))],
        out_shape=[
            jax.ShapeDtypeStruct((toks, width), F32),
            jax.ShapeDtypeStruct((1, width), F32),
        ],
        compiler_params=params(32),
        cost_estimate=cost(20 * toks * width, 12 * toks * width),
        name="norm_back",
    )(gatt, tokens, gres, ga)


def exchange(blocks):
    peers = len(blocks)
    return [blocks[0]] + [
        lax.ppermute(blocks[d], "expert", [(j, j ^ d) for j in range(peers)])
        for d in range(1, peers)
    ]


def halve(value, axis, bit):
    size = lax.axis_size(axis)
    half = value.shape[0] // 2
    up = (lax.axis_index(axis) >> bit) & 1
    keep = lax.dynamic_slice_in_dim(value, up * half, half, 0)
    send = lax.dynamic_slice_in_dim(value, (1 - up) * half, half, 0)
    got = lax.ppermute(send, axis, [(j, j ^ (1 << bit)) for j in range(size)])
    return (keep.astype(F32) + got.astype(F32)).astype(BF16)


def double(value, axis, bit):
    size = lax.axis_size(axis)
    up = (lax.axis_index(axis) >> bit) & 1
    got = lax.ppermute(value, axis, [(j, j ^ (1 << bit)) for j in range(size)])
    return jnp.where(
        up == 1, jnp.concatenate([got, value], 0), jnp.concatenate([value, got], 0)
    )


def total_over_all(value, flip):
    bits = list(range((lax.axis_size("expert") - 1).bit_length()))
    if flip:
        bits = bits[:1] + bits[1:][::-1]
    for bit in bits:
        value = halve(value, "expert", bit)
    groups = lax.axis_size("dp")
    total = value.astype(F32)
    for d in range(1, groups):
        total = total + lax.ppermute(value, "dp", [(j, j ^ d) for j in range(groups)]).astype(F32)
    value = total.astype(BF16)
    for bit in bits[::-1]:
        value = double(value, "expert", bit)
    return value


def sum_shared(parts):
    sizes = [part.shape[0] for part in parts]
    joined = jnp.concatenate(parts, axis=0)
    half = joined.shape[0] // 2
    total = jnp.concatenate(
        [total_over_all(joined[:half], False), total_over_all(joined[half:], True)], axis=0
    ).astype(F32)
    outs, at = [], 0
    for size in sizes:
        outs.append(total[at : at + size])
        at += size
    return outs


def on_device(
    tokens,
    segments,
    routes,
    cotangent,
    w_qkv,
    w_attn_out,
    gain_attn,
    gain_ffn,
    w_router,
    embed,
    w_in,
    w_out,
):
    toks, width = tokens.shape
    experts, rdim = embed.shape
    peers = lax.axis_size("expert")
    shards = lax.axis_size("dp")
    cap = 2 * toks // experts
    me = lax.axis_index("expert").astype(I32).reshape(1)
    ga, gf = gain_attn.reshape(1, width), gain_ffn.reshape(1, width)
    segr, segc = segments.reshape(1, toks), segments.reshape(toks, 1)
    wr = jnp.pad(w_router, ((0, 0), (0, LANES - rdim)))
    emb = jnp.pad(embed, ((0, LANES - experts), (0, LANES - rdim)))

    keyr, keyc, *g_blocks = place(me, routes, cotangent, peers, cap)
    g_rows = exchange(g_blocks)
    q, k, v, lse, mixt, attn_in, res, *x_blocks = attend(
        me, tokens, segr, segc, keyr, w_qkv, w_attn_out, ga, gf, peers, cap
    )
    x_rows = exchange(x_blocks)
    attnt = attn_in.T
    gwin, gwout, gwr, gemb, *outs = expert(
        me, wr, emb, w_in, w_out, x_rows, g_rows, experts, shards
    )
    fouts, gouts = outs[:peers], outs[peers:]
    grad_w_out = lax.psum_scatter(gwout, "dp", scatter_dimension=0, tiled=True)
    grad_w_in = lax.psum_scatter(gwin, "dp", scatter_dimension=0, tiled=True)
    gback = exchange(gouts)
    gres, gb, ggf = combine_back(me, keyc, res, cotangent, gf, gback)
    fback = exchange(fouts)
    out_tokens = combine(me, keyc, res, fback)

    half = PAIRS // 2
    gatt = jnp.zeros((toks, width), F32)
    sums = []
    for first in (0, half):
        gwo, gwq, gwk, gwv, gatt = attend_back(
            first, half, segr, segc, q, k, v, lse, mixt, gb, attnt, w_attn_out, w_qkv, gatt
        )
        sums.append(sum_shared([gwo.reshape(width, -1), gwq, gwk, gwv]))
    grad_tokens, gga = norm_back(gatt, tokens, gres, ga)
    small = lax.psum(
        jnp.concatenate([gga.reshape(-1), ggf.reshape(-1), gwr[:, :rdim].reshape(-1), gemb[:experts, :rdim].reshape(-1)]),
        ("dp", "expert"),
    )
    grad_gain_attn = small[:width]
    grad_gain_ffn = small[width : 2 * width]
    grad_router = small[2 * width : (2 + rdim) * width].reshape(width, rdim)
    grad_embed = small[(2 + rdim) * width :].reshape(experts, rdim)
    grad_w_qkv = jnp.concatenate([sums[s][1 + part] for part in range(3) for s in range(2)], axis=1)
    grad_w_attn_out = jnp.concatenate(
        [sums[s][0].reshape(-1, width) for s in range(2)], axis=0
    )
    return (
        out_tokens,
        grad_tokens,
        grad_w_qkv,
        grad_w_attn_out,
        grad_gain_attn,
        grad_gain_ffn,
        grad_router,
        grad_embed,
        grad_w_in.astype(F32),
        grad_w_out.astype(F32)[None],
    )


def solution(mesh):
    rows = P(("dp", "expert"), None)
    return jax.shard_map(
        on_device,
        mesh=mesh,
        in_specs=(
            rows,
            rows,
            rows,
            rows,
            P(),
            P(),
            P(),
            P(),
            P(),
            P(),
            P("expert", None, None),
            P("expert", None, None),
        ),
        out_specs=(
            rows,
            rows,
            P(),
            P(),
            P(),
            P(),
            P(),
            P(),
            P("expert", None, "dp"),
            P("expert", "dp", None),
        ),
        check_vma=False,
    )
```

time: 1120 us -> 551 us (0.49)
  matrix products: 347 us -> 0 us
  waiting for transfers between devices: 423 us -> 112 us
  Pallas kernels: 0 us -> 209 us
  other arithmetic: 102 us -> 16.4 us
  blocking collectives: 129 us -> 51.5 us
  starting transfers between devices: 9.64 us -> 76.3 us
  local copies, waits for them, and re-layouts: 87.8 us -> 64.8 us
    psum x1 -> x0, waiting for transfers between devices: 361 us -> none  [on_device(): lax.psum((grad_w_qkv, grad_w_attn_out, grad_gain_attn, grad_gain_ffn, gra...]
    dot_general x30 -> x0, matrix products: 347 us -> none  [the longest x1 63.4 us: on_device(): hidden = jnp.dot(expert_in, w_in[local], preferred_element_type=jnp.float32)]
    pallas_call x0 -> x8, Pallas kernels: none -> 209 us  [the longest x1 89.4 us: expert(): pl.pallas_call(functools.partial(expert_kernel, peers, experts), grid=(hi...]
    ppermute x0 -> x64, waiting for transfers between devices: none -> 112 us  [the longest x28 64.2 us: exchange(): lax.ppermute(blocks[d], 'expert', [(j, j ^ d) for j in range(peers)])]
    all_to_all x2 -> x0, blocking collectives: 85.8 us -> none  [the longest x1 43.3 us: on_device(): lax.all_to_all(to_slots(ffn_in), 'expert', split_axis=0, concat_axis=0, t...]
    ppermute x0 -> x64, starting transfers between devices: none -> 76.3 us  [the longest x28 31.8 us: exchange(): lax.ppermute(blocks[d], 'expert', [(j, j ^ d) for j in range(peers)])]
    all_to_all x2 -> x0, waiting for transfers between devices: 62 us -> none  [the longest x1 32.5 us: on_device(): lax.all_to_all(stack_back(back_rows), 'expert', split_axis=0, concat_axis...]
    convert_element_type x4 -> x19, other arithmetic: 48.6 us -> 7.17 us  [the longest x12 3.4 us: halve(): return (keep.astype(F32) + got.astype(F32)).astype(BF16)]
  transfers between devices with their start and end apart: 5 -> 66, of which waited for: 3 -> 25; matrix products, arithmetic and copies ran while one was open for 6% -> 8% of each run, Pallas kernels for 0% -> 21%
where the time goes in v1:
time: 551 us; the launch traced here: 546 us
  Pallas kernels  209 us (38%)
  waiting for transfers between devices  112 us (20%)
  starting transfers between devices  76.3 us (14%)
  local copies, waits for them, and re-layouts  64.8 us (12%)
  blocking collectives  51.5 us (9%)
  other arithmetic  16.4 us (3%)
  between operations  15.1 us (3%)
    pallas_call x1, Pallas kernels, expert(): pl.pallas_call(functools.partial(expert_kernel, peers, experts), grid=(hi...  89.4 us
    ppermute x28, waiting for transfers between devices, exchange(): lax.ppermute(blocks[d], 'expert', [(j, j ^ d) for j in range(peers)])  64.2 us
    pallas_call x2, Pallas kernels, attend_back(): pl.pallas_call(attend_back_kernel, grid=(pairs,), in_specs=[whole((1, tok...  54.9 us
    psum x1, blocking collectives, on_device(): lax.psum(jnp.concatenate([gga.reshape(-1), ggf.reshape(-1), gwr[:, :rdim]...  51.5 us
    pallas_call x1, Pallas kernels, attend(): pl.pallas_call(functools.partial(attend_kernel, peers), grid=(PAIRS,), in...  44.5 us
    unnamed x129, local copies, waits for them, and re-layouts  39.2 us
    ppermute x28, starting transfers between devices, exchange(): lax.ppermute(blocks[d], 'expert', [(j, j ^ d) for j in range(peers)])  31.8 us
    ppermute x12, waiting for transfers between devices, total_over_all(): lax.ppermute(value, 'dp', [(j, j ^ d) for j in range(groups)]).astype(F32)  26.1 us
  transfers between devices with their start and end apart: 66, of which 25 were waited for; matrix products, arithmetic and copies ran while one was open for 8% of the time, Pallas kernels for 21%

profile of v1, /device:TPU:0, one launch (start us, length us, event | category | flops | bytes accessed | tf_op | source)
XLA Modules:
  0.0 545.8 jit_solution(5797741669604167538)
XLA Ops:
  10.2 4.3 place.1
  23.3 44.5 %attend.1 = (bf16[1024,768]{1,0:T(8,128)(2,1)}, bf16[1024,768]{1,0:T(8,128)(2,1)}, bf16[1024,768]{1,0:T(8,128)(2,1)}, f32[6,2,1024]{2,1,0:T(2,128)}, bf16[768,10...) custom-call(s32[1]{0:T(128)} %bitcast.me_ref, ...), custom_call_target="tpu_custom_call" | custom-call | flops 20000000000 | bytes 20000000 | tf_op jit(solution)/shard_map/attend/pallas_call | solution.py:196
  72.5 8.2 %collective-permute-done.12.rest_14_ = bf16[256,768]{1,0:T(8,128)(2,1)S(1)} collective-permute-done((bf16[256,768]{1,0:T(8,128)(2,1)S(1)}, bf16[256,768]{1,0:T(8,128)(2,1)S(1)}, u32[]{:S(2)}, u32[]{:S(2)}) %collective-permute-start.12) | collective-permute-done | bytes 393248 | tf_op jit(solution)/shard_map/ppermute | solution.py:651
  82.3 6.0 %collective-permute-done.13.rest_15_ = bf16[256,768]{1,0:T(8,128)(2,1)S(1)} collective-permute-done((bf16[256,768]{1,0:T(8,128)(2,1)S(1)}, bf16[256,768]{1,0:T(8,128)(2,1)S(1)}, u32[]{:S(2)}, u32[]{:S(2)}) %collective-permute-start.13) | collective-permute-done | bytes 393248 | tf_op jit(solution)/shard_map/ppermute | solution.py:651
  91.6 6.1 %collective-permute-done.1.rest_2_ = bf16[256,768]{1,0:T(8,128)(2,1)S(1)} collective-permute-done((bf16[256,768]{1,0:T(8,128)(2,1)}, bf16[256,768]{1,0:T(8,128)(2,1)S(1)}, u32[]{:S(2)}, u32[]{:S(2)}) %collective-permute-start.1) | collective-permute-done | bytes 393248 | tf_op jit(solution)/shard_map/ppermute | solution.py:651
  99.6 5.7 %collective-permute-done.2.rest_3_ = bf16[256,768]{1,0:T(8,128)(2,1)S(1)} collective-permute-done((bf16[256,768]{1,0:T(8,128)(2,1)}, bf16[256,768]{1,0:T(8,128)(2,1)S(1)}, u32[]{:S(2)}, u32[]{:S(2)}) %collective-permute-start.2) | collective-permute-done | bytes 393248 | tf_op jit(solution)/shard_map/ppermute | solution.py:651
  105.9 8.7 %collective-permute-done.5.rest_6_ = bf16[256,768]{1,0:T(8,128)(2,1)} collective-permute-done((bf16[256,768]{1,0:T(8,128)(2,1)}, bf16[256,768]{1,0:T(8,128)(2,1)}, u32[]{:S(2)}, u32[]{:S(2)}) %collective-permute-start.5) | collective-permute-done | bytes 393248 | tf_op jit(solution)/shard_map/ppermute | solution.py:651
  114.6 7.4 %collective-permute-done.6.rest_7_ = bf16[256,768]{1,0:T(8,128)(2,1)} collective-permute-done((bf16[256,768]{1,0:T(8,128)(2,1)}, bf16[256,768]{1,0:T(8,128)(2,1)}, u32[]{:S(2)}, u32[]{:S(2)}) %collective-permute-start.6) | collective-permute-done | bytes 393248 | tf_op jit(solution)/shard_map/ppermute | solution.py:651
  122.0 89.4 %expert.1 = (bf16[4,768,768]{2,1,0:T(8,128)(2,1)}, bf16[3072,768]{1,0:T(8,128)(2,1)}, f32[768,128]{1,0:T(8,128)}, f32[128,128]{1,0:T(8,128)}, bf16[256,768]{1,0:...) custom-call(s32[1]{0:T(128)} %bitcast.me_ref, ...), custom_call_target="tpu_custom_call" | custom-call | flops 57982058496 | bytes 50000000 | tf_op jit(solution)/shard_map/expert/pallas_call | solution.py:489
  218.9 5.8 %collective-permute-done.22.rest_2_ = bf16[256,768]{1,0:T(8,128)(2,1)S(1)} collective-permute-done((bf16[256,768]{1,0:T(8,128)(2,1)S(1)}, bf16[256,768]{1,0:T(8,128)(2,1)S(1)}, u32[]{:S(2)}, u32[]{:S(2)}) %collective-permute-start.22) | collective-permute-done | bytes 393248 | tf_op jit(solution)/shard_map/ppermute | solution.py:651
  236.5 14.2 %collective-permute-done.25.rest_5_ = bf16[256,768]{1,0:T(8,128)(2,1)S(1)} collective-permute-done((bf16[256,768]{1,0:T(8,128)(2,1)}, bf16[256,768]{1,0:T(8,128)(2,1)S(1)}, u32[]{:S(2)}, u32[]{:S(2)}) %collective-permute-start.25) | collective-permute-done | bytes 393248 | tf_op jit(solution)/shard_map/ppermute | solution.py:651
  268.0 5.9 %combine_back.1 = (f32[1024,768]{1,0:T(8,128)S(1)}, bf16[1024,768]{1,0:T(8,128)(2,1)S(1)}, f32[1,768]{1,0:T(1,128)S(1)}) custom-call(s32[1]{0:T(128)} %bitcast.me_ref, s32[1024,1]{1,0:T(8,128)S(1)} %copy-done.23, f32[1024,768]{1,0:T(8,128)S(1)} %copy-done.19, bf16[1024,768]{1,0:T(8,128)(2,1)S(1)} %copy-done.6, f32[1,768]{1,0:T(1,128)S(1)} %copy-done.4, ...), custom_call_target="tpu_custom_call" | custom-call | flops 3221225472 | bytes 15000000 | tf_op jit(solution)/shard_map/combine_back/pallas_call | solution.py:571
  277.0 27.0 %attend_back.2 = (bf16[384,768]{1,0:T(8,128)(2,1)}, bf16[768,384]{1,0:T(8,128)(2,1)}, bf16[768,384]{1,0:T(8,128)(2,1)}, bf16[768,384]{1,0:T(8,128)(2,1)}, f32[1024,768]{1,0:T(8,128)}) custom-call(s32[1,1024]{1,0:T(1,128)} %segr_ref.5, s32[1024,1]{1,0:T(8,128)} %copy.26.segc_ref, bf16[1024,768]{1,0:T(8,128)(2,1)} %get-tuple-element.97.q_ref, ...), custom_call_target="tpu_custom_call" | custom-call | flops 15000000512 | bytes 20000000 | tf_op jit(solution)/shard_map/attend_back/pallas_call | solution.py:330
  304.0 27.9 %attend_back.3 = (bf16[384,768]{1,0:T(8,128)(2,1)}, bf16[768,384]{1,0:T(8,128)(2,1)}, bf16[768,384]{1,0:T(8,128)(2,1)}, bf16[768,384]{1,0:T(8,128)(2,1)}, f32[1024,768]{1,0:T(8,128)}) custom-call(s32[1,1024]{1,0:T(1,128)} %segr_ref.5, s32[1024,1]{1,0:T(8,128)} %copy.26.segc_ref, bf16[1024,768]{1,0:T(8,128)(2,1)} %get-tuple-element.97.q_ref, ...), custom_call_target="tpu_custom_call" | custom-call | flops 15000000512 | bytes 20000000 | tf_op jit(solution)/shard_map/attend_back/pallas_call | solution.py:330
  356.6 51.5 %psum.7 = f32[13952]{0:T(1024)S(1)} all-reduce(f32[13952]{0:T(1024)S(1)} %pad_maximum_fusion.1), channel_id=1, replica_groups=mesh['dp'=4,'expert'=8] {'dp','expert'}, use_global_device_ids=true, to_apply=%region_0.1 | all-reduce | flops 13952 | bytes 111616 | tf_op jit(solution)/shard_map/psum | solution.py:757
  412.1 6.9 %combine.1 = bf16[1024,768]{1,0:T(8,128)(2,1)} custom-call(s32[1]{0:T(128)} %bitcast.me_ref, s32[1024,1]{1,0:T(8,128)S(1)} %copy-done.24, f32[1024,768]{1,0:T(8,128)S(1)} %copy-done.20, bf16[256,768]{1,0:T(8,128)(2,1)S(1)} %copy-done.26, bf16[256,768]{1,0:T(8,128)(2,1)} %collective-permute-done.14.rest_1_, bf16[256,768]{1,0:T(8,128)(2,1)} %collective-permute-done.15.rest_2_, ...), custom_call_target="tpu_custom_call" | custom-call | flops 3221225472 | bytes 10000000 | tf_op jit(solution)/shard_map/combine/pallas_call | solution.py:601
  426.7 3.9 collective-permute-done.29
  432.7 3.9 collective-permute-done.47
  452.4 6.8 %collective-permute-start.49 = (bf16[192,384]{1,0:T(8,128)(2,1)S(1)}, bf16[192,384]{1,0:T(8,128)(2,1)S(1)}, u32[]{:S(2)}, u32[]{:S(2)}) collective-permute-start(bf16[192,384]{1,0:T(8,128)(2,1)S(1)} %add_convert_fusion.11), channel_id=1, source_target_pairs={{0,8},{8,0},{16,24},{24,16},{1,9},{9,1},{17,25},{25,17},{2,10},{10... | collective-permute-start | bytes 442376 | tf_op jit(solution)/shard_map/ppermute | solution.py:684
  459.2 8.9 %collective-permute-done.32 = bf16[192,384]{1,0:T(8,128)(2,1)S(1)} collective-permute-done((bf16[192,384]{1,0:T(8,128)(2,1)S(1)}, bf16[192,384]{1,0:T(8,128)(2,1)S(1)}, u32[]{:S(2)}, u32[]{:S(2)}) %collective-permute-start.32) | collective-permute-done | bytes 147488 | tf_op jit(solution)/shard_map/ppermute | solution.py:684
  472.6 8.9 %collective-permute-done.50 = bf16[192,384]{1,0:T(8,128)(2,1)S(1)} collective-permute-done((bf16[192,384]{1,0:T(8,128)(2,1)S(1)}, bf16[192,384]{1,0:T(8,128)(2,1)S(1)}, u32[]{:S(2)}, u32[]{:S(2)}) %collective-permute-start.50) | collective-permute-done | bytes 147488 | tf_op jit(solution)/shard_map/ppermute | solution.py:684
  486.1 4.9 collective-permute-done.59
  504.7 4.7 collective-permute-done.35
  509.7 4.4 collective-permute-done.53
  (321 shorter events, 164.5 us)
Async XLA Ops:
  7.2 525.8 %reduce-scatter.5.cloned.1.call-start = ((), (), s32[]{:S(2)}) async-start(), calls=%async_computation.3 | async-start | bytes 5898240 | tf_op jit(solution)/shard_map/reduce_scatter | solution.py:741
  16.2 51.6 %collective-permute-start.7 = (bf16[256,768]{1,0:T(8,128)(2,1)S(1)}, bf16[256,768]{1,0:T(8,128)(2,1)S(1)}, u32[]{:S(2)}, u32[]{:S(2)}) collective-permute-start(bf16[256,768]{1,0:T(8,128)(2,1)S(1)} %get-tuple-element.82), channel_id=1, source_target_pairs={{0,1},{1,0},{2,3},{3,2},{4,5},{5,4},{6,7},{7,6},{8,9},{9,8},{10,11... | collective-permute-start | bytes 1179656 | tf_op jit(solution)/shard_map/ppermute | solution.py:651
  16.6 53.8 %collective-permute-start.8 = (bf16[256,768]{1,0:T(8,128)(2,1)S(1)}, bf16[256,768]{1,0:T(8,128)(2,1)}, u32[]{:S(2)}, u32[]{:S(2)}) collective-permute-start(bf16[256,768]{1,0:T(8,128)(2,1)S(1)} %get-tuple-element.83), channel_id=1, source_target_pairs={{0,2},{1,3},{2,0},{3,1},{4,6},{5,7},{6,4},{7,5},{8,10},{9,11},{10,... | collective-permute-start | bytes 1179656 | tf_op jit(solution)/shard_map/ppermute | solution.py:651
  19.1 51.5 %collective-permute-start.9 = (bf16[256,768]{1,0:T(8,128)(2,1)S(1)}, bf16[256,768]{1,0:T(8,128)(2,1)}, u32[]{:S(2)}, u32[]{:S(2)}) collective-permute-start(bf16[256,768]{1,0:T(8,128)(2,1)S(1)} %get-tuple-element.84), channel_id=1, source_target_pairs={{0,3},{1,2},{2,1},{3,0},{4,7},{5,6},{6,5},{7,4},{8,11},{9,10},{10,... | collective-permute-start | bytes 1179656 | tf_op jit(solution)/shard_map/ppermute | solution.py:651
  19.3 51.7 %collective-permute-start.10 = (bf16[256,768]{1,0:T(8,128)(2,1)S(1)}, bf16[256,768]{1,0:T(8,128)(2,1)}, u32[]{:S(2)}, u32[]{:S(2)}) collective-permute-start(bf16[256,768]{1,0:T(8,128)(2,1)S(1)} %get-tuple-element.85), channel_id=1, source_target_pairs={{0,4},{1,5},{2,6},{3,7},{4,0},{5,1},{6,2},{7,3},{8,12},{9,13},{10,... | collective-permute-start | bytes 1179656 | tf_op jit(solution)/shard_map/ppermute | solution.py:651
  21.0 51.5 %collective-permute-start.11 = (bf16[256,768]{1,0:T(8,128)(2,1)S(1)}, bf16[256,768]{1,0:T(8,128)(2,1)}, u32[]{:S(2)}, u32[]{:S(2)}) collective-permute-start(bf16[256,768]{1,0:T(8,128)(2,1)S(1)} %get-tuple-element.86), channel_id=1, source_target_pairs={{0,5},{1,4},{2,7},{3,6},{4,1},{5,0},{6,3},{7,2},{8,13},{9,12},{10,... | collective-permute-start | bytes 1179656 | tf_op jit(solution)/shard_map/ppermute | solution.py:651
  71.0 26.8 %collective-permute-start.1 = (bf16[256,768]{1,0:T(8,128)(2,1)}, bf16[256,768]{1,0:T(8,128)(2,1)S(1)}, u32[]{:S(2)}, u32[]{:S(2)}) collective-permute-start(bf16[256,768]{1,0:T(8,128)(2,1)} %get-tuple-element.75), channel_id=1, source_target_pairs={{0,2},{1,3},{2,0},{3,1},{4,6},{5,7},{6,4},{7,5},{8,10},{9,11},{10,... | collective-permute-start | bytes 1179656 | tf_op jit(solution)/shard_map/ppermute | solution.py:651
  72.5 32.8 %collective-permute-start.2 = (bf16[256,768]{1,0:T(8,128)(2,1)}, bf16[256,768]{1,0:T(8,128)(2,1)S(1)}, u32[]{:S(2)}, u32[]{:S(2)}) collective-permute-start(bf16[256,768]{1,0:T(8,128)(2,1)} %get-tuple-element.76), channel_id=1, source_target_pairs={{0,3},{1,2},{2,1},{3,0},{4,7},{5,6},{6,5},{7,4},{8,11},{9,10},{10,... | collective-permute-start | bytes 1179656 | tf_op jit(solution)/shard_map/ppermute | solution.py:651
  80.7 24.6 %collective-permute-start.3 = (bf16[256,768]{1,0:T(8,128)(2,1)}, bf16[256,768]{1,0:T(8,128)(2,1)S(1)}, u32[]{:S(2)}, u32[]{:S(2)}) collective-permute-start(bf16[256,768]{1,0:T(8,128)(2,1)} %get-tuple-element.77), channel_id=1, source_target_pairs={{0,4},{1,5},{2,6},{3,7},{4,0},{5,1},{6,2},{7,3},{8,12},{9,13},{10,... | collective-permute-start | bytes 1179656 | tf_op jit(solution)/shard_map/ppermute | solution.py:651
  90.2 24.4 %collective-permute-start.5 = (bf16[256,768]{1,0:T(8,128)(2,1)}, bf16[256,768]{1,0:T(8,128)(2,1)}, u32[]{:S(2)}, u32[]{:S(2)}) collective-permute-start(bf16[256,768]{1,0:T(8,128)(2,1)} %get-tuple-element.79), channel_id=1, source_target_pairs={{0,6},{1,7},{2,4},{3,5},{4,2},{5,3},{6,0},{7,1},{8,14},{9,15},{10,... | collective-permute-start | bytes 1179656 | tf_op jit(solution)/shard_map/ppermute | solution.py:651
  211.4 324.4 %reduce-scatter.3.cloned.1.call-start = ((), (), s32[]{:S(2)}) async-start(), calls=%async_computation.2 | async-start | bytes 5898240 | tf_op jit(solution)/shard_map/reduce_scatter | solution.py:742
  216.1 34.6 %collective-permute-start.25 = (bf16[256,768]{1,0:T(8,128)(2,1)}, bf16[256,768]{1,0:T(8,128)(2,1)S(1)}, u32[]{:S(2)}, u32[]{:S(2)}) collective-permute-start(bf16[256,768]{1,0:T(8,128)(2,1)} %get-tuple-element.107), channel_id=1, source_target_pairs={{0,5},{1,4},{2,7},{3,6},{4,1},{5,0},{6,3},{7,2},{8,13},{9,12},{10,... | collective-permute-start | bytes 1179656 | tf_op jit(solution)/shard_map/ppermute | solution.py:651
  216.2 37.4 %collective-permute-start.26 = (bf16[256,768]{1,0:T(8,128)(2,1)S(1)}, bf16[256,768]{1,0:T(8,128)(2,1)S(1)}, u32[]{:S(2)}, u32[]{:S(2)}) collective-permute-start(bf16[256,768]{1,0:T(8,128)(2,1)S(1)} %copy-done.49), channel_id=1, source_target_pairs={{0,6},{1,7},{2,4},{3,5},{4,2},{5,3},{6,0},{7,1},{8,14},{9,15},{10,... | collective-permute-start | bytes 1179656 | tf_op jit(solution)/shard_map/ppermute | solution.py:651
  225.4 30.5 %collective-permute-start.27 = (bf16[256,768]{1,0:T(8,128)(2,1)S(1)}, bf16[256,768]{1,0:T(8,128)(2,1)S(1)}, u32[]{:S(2)}, u32[]{:S(2)}) collective-permute-start(bf16[256,768]{1,0:T(8,128)(2,1)S(1)} %copy-done.48), channel_id=1, source_target_pairs={{0,7},{1,6},{2,5},{3,4},{4,3},{5,2},{6,1},{7,0},{8,15},{9,14},{10,... | collective-permute-start | bytes 1179656 | tf_op jit(solution)/shard_map/ppermute | solution.py:651
  233.1 119.2 %collective-permute-start.14 = (bf16[256,768]{1,0:T(8,128)(2,1)}, bf16[256,768]{1,0:T(8,128)(2,1)}, u32[]{:S(2)}, u32[]{:S(2)}) collective-permute-start(bf16[256,768]{1,0:T(8,128)(2,1)} %get-tuple-element.90), channel_id=1, source_target_pairs={{0,1},{1,0},{2,3},{3,2},{4,5},{5,4},{6,7},{7,6},{8,9},{9,8},{10,11... | collective-permute-start | bytes 1179656 | tf_op jit(solution)/shard_map/ppermute | solution.py:651
  234.8 117.8 %collective-permute-start.15 = (bf16[256,768]{1,0:T(8,128)(2,1)}, bf16[256,768]{1,0:T(8,128)(2,1)}, u32[]{:S(2)}, u32[]{:S(2)}) collective-permute-start(bf16[256,768]{1,0:T(8,128)(2,1)} %get-tuple-element.91), channel_id=1, source_target_pairs={{0,2},{1,3},{2,0},{3,1},{4,6},{5,7},{6,4},{7,5},{8,10},{9,11},{10,... | collective-permute-start | bytes 1179656 | tf_op jit(solution)/shard_map/ppermute | solution.py:651
  251.5 103.9 %collective-permute-start.16 = (bf16[256,768]{1,0:T(8,128)(2,1)}, bf16[256,768]{1,0:T(8,128)(2,1)}, u32[]{:S(2)}, u32[]{:S(2)}) collective-permute-start(bf16[256,768]{1,0:T(8,128)(2,1)} %get-tuple-element.92), channel_id=1, source_target_pairs={{0,3},{1,2},{2,1},{3,0},{4,7},{5,6},{6,5},{7,4},{8,11},{9,10},{10,... | collective-permute-start | bytes 1179656 | tf_op jit(solution)/shard_map/ppermute | solution.py:651
  254.4 155.1 %collective-permute-start.17 = (bf16[256,768]{1,0:T(8,128)(2,1)}, bf16[256,768]{1,0:T(8,128)(2,1)}, u32[]{:S(2)}, u32[]{:S(2)}) collective-permute-start(bf16[256,768]{1,0:T(8,128)(2,1)} %get-tuple-element.93), channel_id=1, source_target_pairs={{0,4},{1,5},{2,6},{3,7},{4,0},{5,1},{6,2},{7,3},{8,12},{9,13},{10,... | collective-permute-start | bytes 1179656 | tf_op jit(solution)/shard_map/ppermute | solution.py:651
  256.7 152.9 %collective-permute-start.18 = (bf16[256,768]{1,0:T(8,128)(2,1)}, bf16[256,768]{1,0:T(8,128)(2,1)}, u32[]{:S(2)}, u32[]{:S(2)}) collective-permute-start(bf16[256,768]{1,0:T(8,128)(2,1)} %get-tuple-element.94), channel_id=1, source_target_pairs={{0,5},{1,4},{2,7},{3,6},{4,1},{5,0},{6,3},{7,2},{8,13},{9,12},{10,... | collective-permute-start | bytes 1179656 | tf_op jit(solution)/shard_map/ppermute | solution.py:651
  352.3 57.7 %collective-permute-start.19 = (bf16[256,768]{1,0:T(8,128)(2,1)}, bf16[256,768]{1,0:T(8,128)(2,1)S(1)}, u32[]{:S(2)}, u32[]{:S(2)}) collective-permute-start(bf16[256,768]{1,0:T(8,128)(2,1)} %get-tuple-element.95), channel_id=1, source_target_pairs={{0,6},{1,7},{2,4},{3,5},{4,2},{5,3},{6,0},{7,1},{8,14},{9,15},{10,... | collective-permute-start | bytes 1179656 | tf_op jit(solution)/shard_map/ppermute | solution.py:651
  352.6 57.5 %collective-permute-start.20 = (bf16[256,768]{1,0:T(8,128)(2,1)}, bf16[256,768]{1,0:T(8,128)(2,1)S(1)}, u32[]{:S(2)}, u32[]{:S(2)}) collective-permute-start(bf16[256,768]{1,0:T(8,128)(2,1)} %get-tuple-element.96), channel_id=1, source_target_pairs={{0,7},{1,6},{2,5},{3,4},{4,3},{5,2},{6,1},{7,0},{8,15},{9,14},{10,... | collective-permute-start | bytes 1179656 | tf_op jit(solution)/shard_map/ppermute | solution.py:651
  355.4 63.6 %collective-permute-start.28 = (bf16[768,384]{1,0:T(8,128)(2,1)S(1)}, bf16[768,384]{1,0:T(8,128)(2,1)}, u32[]{:S(2)}, u32[]{:S(2)}) collective-permute-start(bf16[768,384]{1,0:T(8,128)(2,1)S(1)} %copy-done.36), channel_id=1, source_target_pairs={{0,1},{1,0},{2,3},{3,2},{4,5},{5,4},{6,7},{7,6},{8,9},{9,8},{10,11... | collective-permute-start | bytes 1769480 | tf_op jit(solution)/shard_map/ppermute | solution.py:662
  449.9 31.6 %collective-permute-start.50 = (bf16[192,384]{1,0:T(8,128)(2,1)S(1)}, bf16[192,384]{1,0:T(8,128)(2,1)S(1)}, u32[]{:S(2)}, u32[]{:S(2)}) collective-permute-start(bf16[192,384]{1,0:T(8,128)(2,1)S(1)} %add_convert_fusion.11), channel_id=1, source_target_pairs={{0,16},{8,24},{16,0},{24,8},{1,17},{9,25},{17,1},{25,9},{2,18},{10... | collective-permute-start | bytes 442376 | tf_op jit(solution)/shard_map/ppermute | solution.py:684
  452.4 30.6 %collective-permute-start.49 = (bf16[192,384]{1,0:T(8,128)(2,1)S(1)}, bf16[192,384]{1,0:T(8,128)(2,1)S(1)}, u32[]{:S(2)}, u32[]{:S(2)}) collective-permute-start(bf16[192,384]{1,0:T(8,128)(2,1)S(1)} %add_convert_fusion.11), channel_id=1, source_target_pairs={{0,8},{8,0},{16,24},{24,16},{1,9},{9,1},{17,25},{25,17},{2,10},{10... | collective-permute-start | bytes 442376 | tf_op jit(solution)/shard_map/ppermute | solution.py:684
  (101 other events, 1082.3 us)
Sparse Core Ops, SparseCore 0:
  211.5 86.8 reduce-scatter.4
  300.7 85.7 reduce-scatter.2

commit v2 on v1

v2 whole, which is shorter than its diff:
```python
import functools

import jax
import jax.numpy as jnp
from jax import lax
from jax.experimental import pallas as pl
from jax.experimental.pallas import tpu as pltpu
from jax.sharding import PartitionSpec as P

HEADS = 12
HEAD = 64
PAIRS = HEADS // 2
PAIR = 2 * HEAD
QB = 256
LANES = 128
ROUTER_WARMTH = 0.3
NORM_FLOOR = 12.0
EPSILON = 1e-05
MASK_VALUE = -1e30
F32 = jnp.float32
BF16 = jnp.bfloat16
I32 = jnp.int32
NN = (((1,), (0,)), ((), ()))
NT = (((1,), (1,)), ((), ()))
TN = (((0,), (0,)), ((), ()))
HIGHEST = lax.Precision.HIGHEST
MIB = 1 << 20


def mm(a, b, dims=NN, precision=None):
    return lax.dot_general(a, b, dims, precision=precision, preferred_element_type=F32)


def params(mib):
    return pltpu.CompilerParams(vmem_limit_bytes=mib * MIB)


def cost(micros, nbytes=0):
    return pl.CostEstimate(
        flops=int(micros * 1.15e9), bytes_accessed=int(nbytes), transcendentals=0
    )


def whole(shape):
    return pl.BlockSpec(
        shape, lambda *_: (0,) * len(shape), pipeline_mode=pl.Buffered(buffer_count=1)
    )


def smem():
    return pl.BlockSpec(memory_space=pltpu.SMEM)


def norm_back(x, gain, dy):
    inv = lax.rsqrt(jnp.mean(x * x, axis=1, keepdims=True) + EPSILON)
    dn = dy * gain
    dx = inv * dn - x * (inv * inv * inv * jnp.mean(x * dn, axis=1, keepdims=True))
    return dx, jnp.sum(dy * x * inv, axis=0, keepdims=True)


def column_of(row):
    return jnp.broadcast_to(row.astype(F32), (8, row.shape[1])).T[:, :1].astype(row.dtype)


def ones_where(mask):
    return jnp.where(mask, 1.0, 0.0).astype(BF16)


def dispatch(key_row, rows, out_refs):
    at = 0
    for ref in out_refs:
        step = min(2 * QB, ref.shape[0])
        for r in range(0, ref.shape[0], step):
            slot = lax.broadcasted_iota(I32, (step, key_row.shape[1]), 0) + at
            ref[r : r + step, :] = mm(ones_where(key_row == slot), rows).astype(BF16)
            at += step


def place_kernel(peers, rr_ref, cot_ref, keyr_ref, g_ref):
    toks = cot_ref.shape[0]
    cap = g_ref.shape[0] // peers
    half = cap // 2
    rr = rr_ref[...]
    before = ones_where(
        lax.broadcasted_iota(I32, (toks, toks), 0) <= lax.broadcasted_iota(I32, (toks, toks), 1)
    )
    hot_row = jnp.where(lax.broadcasted_iota(I32, (peers, toks), 0) == rr, 1.0, 0.0)
    upto = mm(hot_row.astype(BF16), before)
    rank = (jnp.sum(hot_row * upto, axis=0, keepdims=True) - 1.0).astype(I32)
    keyr_ref[...] = rr * half + jnp.where(rank < half, rank, rank + (peers - 1) * half)
    dispatch(rr * cap + rank, cot_ref[...], (g_ref,))


def place(routes, cot, peers, slots):
    toks, width = cot.shape
    return pl.pallas_call(
        functools.partial(place_kernel, peers),
        out_shape=[
            jax.ShapeDtypeStruct((1, toks), I32),
            jax.ShapeDtypeStruct((slots, width), BF16),
        ],
        in_specs=[pl.BlockSpec(memory_space=pltpu.VMEM)] * 2,
        compiler_params=params(40),
        cost_estimate=cost(5),
        name="place",
    )(routes, cot)


def band(i):
    return max(0, i - 2) * QB, (i + 1) * QB


def fill_bias(bias_ref, segr, count):
    segc = column_of(segr)
    for i in range(count):
        low, high = band(i)
        keys = lax.broadcasted_iota(I32, (high - low, QB), 0) + low
        queries = lax.broadcasted_iota(I32, (high - low, QB), 1) + i * QB
        same = segc[low:high] == segr[:, i * QB : (i + 1) * QB]
        bias_ref[i, : high - low, :] = jnp.where((keys <= queries) & same, 0.0, MASK_VALUE)


def head_mask(values, h):
    lane = lax.broadcasted_iota(I32, values.shape, 1)
    return jnp.where((lane >= h * HEAD) & (lane < (h + 1) * HEAD), values, jnp.zeros_like(values))


def attend_kernel(
    tok_ref,
    segr_ref,
    keyr_ref,
    wq_ref,
    wk_ref,
    wv_ref,
    wo_ref,
    ga_ref,
    gf_ref,
    q_ref,
    k_ref,
    v_ref,
    lse_ref,
    mixt_ref,
    attn_ref,
    res_ref,
    xa_ref,
    xb_ref,
    bias_ref,
    mix_ref,
):
    p = pl.program_id(0)
    toks, width = tok_ref.shape
    count = toks // QB

    @pl.when(p == 0)
    def _():
        fill_bias(bias_ref, segr_ref[...], count)
        x = tok_ref[...].astype(F32)
        inv = lax.rsqrt(jnp.mean(x * x, axis=1, keepdims=True) + EPSILON)
        attn_ref[...] = (x * inv * ga_ref[...]).astype(BF16)

    attn_in = attn_ref[...]
    weights = jnp.concatenate([wq_ref[...], wk_ref[...], wv_ref[...]], axis=1)
    qkv = mm(attn_in, weights)
    q_ref[...] = qkv[:, :PAIR].astype(BF16)
    k_ref[...] = qkv[:, PAIR : 2 * PAIR].astype(BF16)
    v = qkv[:, 2 * PAIR :]
    v_ref[...] = v.astype(BF16)
    vt = v.T.astype(BF16)
    for i in range(count):
        low, high = band(i)
        cols = slice(i * QB, (i + 1) * QB)
        q = q_ref[cols, :] * HEAD**-0.5
        keys = k_ref[low:high, :]
        parts = []
        for h in range(2):
            s = mm(keys, head_mask(q, h), NT) + bias_ref[i, : high - low, :]
            top = jnp.max(s, axis=0, keepdims=True)
            w = jnp.exp(s - top)
            total = jnp.sum(w, axis=0, keepdims=True)
            lse_ref[0, h : h + 1, cols] = top + jnp.log(total)
            chances = (w * (1.0 / total)).astype(BF16)
            parts.append(mm(vt[h * HEAD : (h + 1) * HEAD, low:high], chances))
        mixt_ref[:, cols] = jnp.concatenate(parts, axis=0).astype(BF16)
    mix_ref[pl.ds(pl.multiple_of(p * PAIR, PAIR), PAIR), :] = mixt_ref[...]

    @pl.when(p == pl.num_programs(0) - 1)
    def _():
        res = tok_ref[...].astype(F32) + mm(mix_ref[...], wo_ref[...], TN)
        res_ref[...] = res
        inv = lax.rsqrt(jnp.mean(res * res, axis=1, keepdims=True) + EPSILON)
        ffn_in = (res * inv * gf_ref[...]).astype(BF16)
        dispatch(keyr_ref[...], ffn_in, (xa_ref, xb_ref))


def attend(tokens, segr, keyr, w_qkv, w_o, ga, gf):
    toks, width = tokens.shape
    pair_cols = pl.BlockSpec((toks, PAIR), lambda p: (0, p))
    heads = jax.ShapeDtypeStruct((toks, width), BF16)
    weights = [
        pl.BlockSpec((width, PAIR), lambda p, part=part: (0, part * PAIRS + p)) for part in range(3)
    ]
    return pl.pallas_call(
        attend_kernel,
        grid=(PAIRS,),
        in_specs=[
            whole((toks, width)),
            whole((1, toks)),
            whole((1, toks)),
            *weights,
            whole((width, width)),
            whole((1, width)),
            whole((1, width)),
        ],
        out_specs=[
            pair_cols,
            pair_cols,
            pair_cols,
            pl.BlockSpec((1, 2, toks), lambda p: (p, 0, 0)),
            pl.BlockSpec((PAIR, toks), lambda p: (p, 0)),
            whole((toks, width)),
            whole((toks, width)),
            whole((toks, width)),
            whole((toks, width)),
        ],
        out_shape=[
            heads,
            heads,
            heads,
            jax.ShapeDtypeStruct((PAIRS, 2, toks), F32),
            jax.ShapeDtypeStruct((width, toks), BF16),
            heads,
            jax.ShapeDtypeStruct((toks, width), F32),
            heads,
            heads,
        ],
        scratch_shapes=[
            pltpu.VMEM((toks // QB, 3 * QB, QB), F32),
            pltpu.VMEM((width, toks), BF16),
        ],
        compiler_params=params(56),
        cost_estimate=cost(42),
        name="attend",
    )(tokens, segr, keyr, w_qkv, w_qkv, w_qkv, w_o, ga, gf)


def attend_back_kernel(
    last,
    core_ref,
    segr_ref,
    q_ref,
    k_ref,
    v_ref,
    lse_ref,
    mixt_ref,
    gb_ref,
    attnt_ref,
    wo_ref,
    wq_ref,
    wk_ref,
    wv_ref,
    *rest,
):
    if last:
        gin_ref, tok_ref, gres_ref, ga_ref, send_ref, keep_ref, gtok_ref, gain_ref, gatt_ref = rest[:9]
    else:
        gin_ref, send_ref, keep_ref, gatt_ref = rest[:4]
    bias_ref, dqt_ref, dk_ref, dv_ref, do_ref = rest[-5:]
    p = pl.program_id(0)
    toks, width = gb_ref.shape
    count = toks // QB
    scale = HEAD**-0.5

    @pl.when(p == 0)
    def _():
        fill_bias(bias_ref, segr_ref[...], count)
        gatt_ref[...] = gin_ref[...]

    gb = gb_ref[...]
    do_ref[...] = mm(gb, wo_ref[...], NT).astype(BF16)
    dot_ = mm(wo_ref[...], gb, NT).astype(BF16).astype(F32)
    mixt = mixt_ref[...]
    gwo = mm(mixt, gb).astype(BF16)
    weighted = dot_ * mixt.astype(F32)
    delta = [
        jnp.sum(weighted[h * HEAD : (h + 1) * HEAD], axis=0, keepdims=True) for h in range(2)
    ]
    kt = k_ref[...].astype(F32).T.astype(BF16)
    dk_ref[...] = jnp.zeros_like(dk_ref)
    dv_ref[...] = jnp.zeros_like(dv_ref)
    for i in range(count):
        low, high = band(i)
        cols = slice(i * QB, (i + 1) * QB)
        q = q_ref[cols, :] * scale
        do = do_ref[cols, :]
        keys = k_ref[low:high, :]
        values = v_ref[low:high, :]
        dk_add, dv_add, dqs = [], [], []
        for h in range(2):
            qm, dom = head_mask(q, h), head_mask(do, h)
            s = mm(keys, qm, NT) + bias_ref[i, : high - low, :]
            pr = jnp.exp(s - lse_ref[0, h : h + 1, cols])
            dpr = mm(values, dom, NT)
            ds = (pr * (dpr - delta[h][:, cols])).astype(BF16)
            dv_add.append(mm(pr.astype(BF16), dom))
            dk_add.append(mm(ds, qm))
            dqs.append(mm(kt[h * HEAD : (h + 1) * HEAD, low:high], ds))
        dk_ref[low:high, :] += dk_add[0] + dk_add[1]
        dv_ref[low:high, :] += dv_add[0] + dv_add[1]
        dqt_ref[:, cols] = jnp.concatenate(dqs, axis=0) * scale
    grads = [
        dqt_ref[...].T.astype(BF16),
        dk_ref[...].astype(BF16),
        dv_ref[...].astype(BF16),
    ]
    joined = jnp.concatenate(grads, axis=1)
    gw = mm(attnt_ref[...], joined).astype(BF16)
    for turn, ref in enumerate((send_ref, keep_ref)):

        @pl.when(p == turn)
        def _(ref=ref):
            for part in range(3):
                ref[part] = gw[:, part * PAIR : (part + 1) * PAIR]
            for j in range(width // PAIR):
                ref[3, j * PAIR : (j + 1) * PAIR, :] = gwo[:, j * PAIR : (j + 1) * PAIR]

    weights = jnp.concatenate([wq_ref[...], wk_ref[...], wv_ref[...]], axis=1)
    gatt_ref[...] += mm(joined, weights, NT)

    if last:

        @pl.when(p == pl.num_programs(0) - 1)
        def _():
            gain = jnp.zeros(gain_ref.shape, F32)
            for i in range(count):
                part = slice(i * QB, (i + 1) * QB)
                dx, dgain = norm_back(tok_ref[part, :].astype(F32), ga_ref[...], gatt_ref[part, :])
                gtok_ref[part, :] = gres_ref[part, :] + dx
                gain = gain + dgain
            gain_ref[...] = gain


def attend_back(first, core, segr, q, k, v, lse, mixt, gb, attnt, w_o, w_qkv, gin, final):
    toks, width = gb.shape

    def pair(p, core_ref):
        return first + jnp.where(p == 0, 1 - core_ref[0], core_ref[0])

    def fixed(shape):
        return pl.BlockSpec(
            shape, lambda p, c: (0,) * len(shape), pipeline_mode=pl.Buffered(buffer_count=1)
        )

    pair_cols = pl.BlockSpec((toks, PAIR), lambda p, c: (0, pair(p, c)))
    weights = [
        pl.BlockSpec((width, PAIR), lambda p, c, part=part: (0, part * PAIRS + pair(p, c)))
        for part in range(3)
    ]
    full = fixed((toks, width))
    row = fixed((1, width))
    f32_full = jax.ShapeDtypeStruct((toks, width), F32)
    gw_spec = fixed((4, width, PAIR))
    gw_shape = jax.ShapeDtypeStruct((4, width, PAIR), BF16)
    scratch = [
        pltpu.VMEM((toks // QB, 3 * QB, QB), F32),
        pltpu.VMEM((PAIR, toks), F32),
        pltpu.VMEM((toks, PAIR), F32),
        pltpu.VMEM((toks, PAIR), F32),
        pltpu.VMEM((toks, PAIR), BF16),
    ]
    if final:
        out_specs = [gw_spec, gw_spec, full, row]
        out_shape = [gw_shape, gw_shape, f32_full, jax.ShapeDtypeStruct((1, width), F32)]
        scratch = [pltpu.VMEM((toks, width), F32)] + scratch
    else:
        out_specs, out_shape = [gw_spec, gw_spec, full], [gw_shape, gw_shape, f32_full]
    return pl.pallas_call(
        functools.partial(attend_back_kernel, bool(final)),
        grid_spec=pltpu.PrefetchScalarGridSpec(
            num_scalar_prefetch=1,
            grid=(2,),
            in_specs=[
                fixed((1, toks)),
                pair_cols,
                pair_cols,
                pair_cols,
                pl.BlockSpec((1, 2, toks), lambda p, c: (pair(p, c), 0, 0)),
                pl.BlockSpec((PAIR, toks), lambda p, c: (pair(p, c), 0)),
                full,
                fixed((width, toks)),
                pl.BlockSpec((PAIR, width), lambda p, c: (pair(p, c), 0)),
                *weights,
                full,
            ]
            + ([full, full, row] if final else []),
            out_specs=out_specs,
            scratch_shapes=scratch,
        ),
        out_shape=out_shape,
        compiler_params=params(56),
        cost_estimate=cost(19),
        name="attend_back",
    )(core, segr, q, k, v, lse, mixt, gb, attnt, w_o, w_qkv, w_qkv, w_qkv, gin, *final)


def unit_scale(values, axis):
    total = jnp.sum(values * values, axis=axis, keepdims=True)
    return lax.rsqrt(jnp.maximum(total, NORM_FLOOR)), total


def unit_back(values, inv, total, grad, axis):
    passed = jnp.where(total > NORM_FLOOR, 1.0, jnp.where(total == NORM_FLOOR, 0.5, 0.0))
    inner = jnp.sum(grad * values, axis=axis, keepdims=True)
    return inv * grad - passed * inv * inv * inv * inner * values


def gelu_and_slope(h):
    cdf = 0.5 + 0.5 * lax.erf(h * 0.7071067811865476)
    pdf = 0.3989422804014327 * jnp.exp(-0.5 * h * h)
    return h * cdf, cdf + h * pdf


def route(me, x, wrt, emb):
    z = mm(wrt, x, NT)
    inv, total = unit_scale(z, 0)
    zn = z * inv
    en = emb * unit_scale(emb, 1)[0]
    logits = mm(en, zn, NN, HIGHEST) / ROUTER_WARMTH
    w = jnp.exp(logits - jnp.max(logits, axis=0, keepdims=True))
    chances = w / jnp.sum(w, axis=0, keepdims=True)
    mine = jnp.where(lax.broadcasted_iota(I32, logits.shape, 0) == me, 1.0, 0.0)
    return z, inv, total, zn, en, chances, mine


def expert_kernel(grads, me_ref, wrt_ref, emb_ref, x_ref, win_ref, ga_ref, *rest):
    if grads:
        acta_ref, gpa_ref, xta_ref, gta_ref, gtb_ref, gw_ref, act_ref, *rest = rest
    else:
        act_ref, gp_ref, xt_ref, *rest = rest
    gout_ref, gwrt_ref, gemb_ref, gin_s, acc_s, gate_s, *rest = rest
    if grads:
        gp_ref, xt_ref = rest
    c = pl.program_id(0)
    rows, width = x_ref.shape
    me = me_ref[0]

    @pl.when(c == 0)
    def _():
        chances, mine = route(me, x_ref[...], wrt_ref[...], emb_ref[...])[-2:]
        gate = column_of(jnp.sum(chances * mine, axis=0, keepdims=True))
        gate_s[...] = jnp.broadcast_to(gate, (rows, LANES))
        for r in range(0, rows, QB):
            xt_ref[:, r : r + QB] = x_ref[r : r + QB, :].T
        gin_s[...] = jnp.zeros_like(gin_s)
        acc_s[...] = jnp.zeros_like(acc_s)

    w_in = win_ref[0]
    wide = w_in.shape[1]
    step = min(2 * QB, rows)
    for r in range(0, rows, step):
        part = slice(r, r + step)
        h = mm(x_ref[part, :], w_in)
        act, slope = gelu_and_slope(h)
        gate = jnp.concatenate([gate_s[part, :]] * (wide // LANES), axis=1)
        ga = ga_ref[part, :].astype(F32)
        act = act * gate
        act_ref[part, :] = act.astype(BF16)
        gp = (ga * (slope * gate)).astype(BF16)
        gp_ref[part, :] = gp
        prod = act * ga
        folded = prod[:, :LANES]
        for j in range(LANES, wide, LANES):
            folded = folded + prod[:, j : j + LANES]
        acc_s[part, :] += folded
        gin_s[part, :] += mm(gp, w_in, NT)
    if grads:
        gw_ref[0, 0] = (mm(xta_ref[...], gpa_ref[...]) + mm(xt_ref[...], gp_ref[...])).astype(BF16)
        gw_ref[0, 1] = (mm(gta_ref[...], acta_ref[...]) + mm(gtb_ref[...], act_ref[...])).astype(
            BF16
        )

    @pl.when(c == pl.num_programs(0) - 1)
    def _():
        x, wrt, emb = x_ref[...], wrt_ref[...], emb_ref[...]
        z, inv, total, zn, en, chances, mine = route(me, x, wrt, emb)
        weight = jnp.sum(acc_s[...].T, axis=0, keepdims=True)
        dl = weight * (mine - chances) / ROUTER_WARMTH
        gen = mm(dl, zn, NT, HIGHEST)
        dz = unit_back(z, inv, total, mm(en, dl, TN, HIGHEST), 0)
        dz_top = dz.astype(BF16)
        dz_low = (dz - dz_top.astype(F32)).astype(BF16)
        gwrt_ref[...] = mm(dz_top, x) + mm(dz_low, x)
        einv, etotal = unit_scale(emb, 1)
        gemb_ref[...] = unit_back(emb, einv, etotal, gen, 1)
        dz_top, dz_low = dz_top.astype(F32).T.astype(BF16), dz_low.astype(F32).T.astype(BF16)
        for r in range(0, rows, QB):
            part = slice(r, r + QB)
            back = gin_s[part, :].astype(BF16).astype(F32)
            back = back + mm(dz_top[part], wrt) + mm(dz_low[part], wrt)
            gout_ref[part, :] = back.astype(BF16)


def expert(me, wrt, emb, x, w_in, ga, wide, other=None):
    rows, width = x.shape
    hidden = w_in.shape[2]
    steps = hidden // wide
    grads = other is not None
    cols = pl.BlockSpec((rows, wide), lambda c: (0, c))
    hid = jax.ShapeDtypeStruct((rows, hidden), BF16)
    xt_spec = whole((width, rows))
    operands = [me, wrt, emb, x, w_in, ga]
    in_specs = [
        smem(),
        whole(wrt.shape),
        whole(emb.shape),
        whole((rows, width)),
        pl.BlockSpec((1, width, wide), lambda c: (0, 0, c)),
        cols,
    ]
    scratch = [
        pltpu.VMEM((rows, width), F32),
        pltpu.VMEM((rows, LANES), F32),
        pltpu.VMEM((rows, LANES), F32),
    ]
    if grads:
        operands += list(other)
        in_specs += [cols, cols, xt_spec, xt_spec, xt_spec]
        out_specs = [pl.BlockSpec((1, 2, width, wide), lambda c: (c, 0, 0, 0)), cols]
        out_shape = [jax.ShapeDtypeStruct((steps, 2, width, wide), BF16), hid]
        scratch += [pltpu.VMEM((rows, wide), BF16), pltpu.VMEM((width, rows), BF16)]
    else:
        out_specs = [cols, cols, xt_spec]
        out_shape = [hid, hid, jax.ShapeDtypeStruct((width, rows), BF16)]
    out_specs += [whole((rows, width)), whole(wrt.shape), whole(emb.shape)]
    out_shape += [
        jax.ShapeDtypeStruct((rows, width), BF16),
        jax.ShapeDtypeStruct(wrt.shape, F32),
        jax.ShapeDtypeStruct(emb.shape, F32),
    ]
    return pl.pallas_call(
        functools.partial(expert_kernel, grads),
        grid=(steps,),
        in_specs=in_specs,
        out_specs=out_specs,
        out_shape=out_shape,
        scratch_shapes=scratch,
        compiler_params=params(60),
        cost_estimate=cost(45 if grads else 24),
        name="expert",
    )(*operands)


def grad_act_kernel(g_ref, wout_ref, out_ref, gt_ref):
    g = g_ref[...].reshape(out_ref.shape[0], g_ref.shape[-1])

    @pl.when(pl.program_id(0) == 0)
    def _():
        gt_ref[...] = g.T

    out_ref[...] = mm(g, wout_ref[0], NT).astype(BF16)


def grad_act(g, half, w_out, wide):
    peers, _, slots, width = g.shape
    rows = peers * slots
    hidden = w_out.shape[1]
    return pl.pallas_call(
        grad_act_kernel,
        grid=(hidden // wide,),
        in_specs=[
            pl.BlockSpec((peers, 1, slots, width), lambda c: (0, half, 0, 0)),
            pl.BlockSpec((1, wide, width), lambda c: (0, c, 0)),
        ],
        out_specs=[pl.BlockSpec((rows, wide), lambda c: (0, c)), whole((width, rows))],
        out_shape=[
            jax.ShapeDtypeStruct((rows, hidden), BF16),
            jax.ShapeDtypeStruct((width, rows), BF16),
        ],
        compiler_params=params(40),
        cost_estimate=cost(7),
        name="grad_act",
    )(g, w_out)


def expert_out_kernel(acta_ref, actb_ref, wout_ref, outa_ref, outb_ref, acc_ref):
    c = pl.program_id(0)
    rows = acta_ref.shape[0]

    @pl.when(c == 0)
    def _():
        acc_ref[...] = jnp.zeros_like(acc_ref)

    w_out = wout_ref[0]
    acc_ref[:rows, :] += mm(acta_ref[...], w_out)
    acc_ref[rows:, :] += mm(actb_ref[...], w_out)

    @pl.when(c == pl.num_programs(0) - 1)
    def _():
        outa_ref[...] = acc_ref[:rows, :].astype(BF16)
        outb_ref[...] = acc_ref[rows:, :].astype(BF16)


def expert_out_of(acta, actb, w_out, wide):
    rows, hidden = acta.shape
    width = w_out.shape[2]
    block = jax.ShapeDtypeStruct((rows, width), BF16)
    cols = pl.BlockSpec((rows, wide), lambda c: (0, c))
    return pl.pallas_call(
        expert_out_kernel,
        grid=(hidden // wide,),
        in_specs=[cols, cols, pl.BlockSpec((1, wide, width), lambda c: (0, c, 0))],
        out_specs=[whole((rows, width))] * 2,
        out_shape=[block] * 2,
        scratch_shapes=[pltpu.VMEM((2 * rows, width), F32)],
        compiler_params=params(50),
        cost_estimate=cost(14),
        name="expert_out",
    )(acta, actb, w_out)


def expert_sums_kernel(sum_ref, win_ref, wout_ref):
    win_ref[0] = sum_ref[0].astype(F32)
    wout_ref[0] = sum_ref[1].astype(F32).T


def expert_sums(total):
    _, width, share = total.shape
    wide = LANES
    return pl.pallas_call(
        expert_sums_kernel,
        grid=(share // wide,),
        in_specs=[pl.BlockSpec((2, width, wide), lambda k: (0, 0, k))],
        out_specs=[
            pl.BlockSpec((1, width, wide), lambda k: (0, 0, k)),
            pl.BlockSpec((1, wide, width), lambda k: (0, k, 0)),
        ],
        out_shape=[
            jax.ShapeDtypeStruct((1, width, share), F32),
            jax.ShapeDtypeStruct((1, share, width), F32),
        ],
        compiler_params=params(32),
        cost_estimate=cost(3),
        name="expert_sums",
    )(total)


def gather_rows(key_row, row_refs):
    keys = column_of(key_row)
    total, at = None, 0
    for ref in row_refs:
        column = lax.broadcasted_iota(I32, (keys.shape[0], ref.shape[0]), 1) + at
        part = mm(ones_where(keys == column), ref[...])
        total = part if total is None else total + part
        at += ref.shape[0]
    return total


def combine_back_kernel(
    keyr_ref, res_ref, cot_ref, gf_ref, ra_ref, rb_ref, gres_ref, gb_ref, gain_ref
):
    dy = gather_rows(keyr_ref[...], (ra_ref, rb_ref))

    @pl.when(pl.program_id(0) == 0)
    def _():
        gain_ref[...] = jnp.zeros_like(gain_ref)

    dx, dgain = norm_back(res_ref[...], gf_ref[...], dy)
    gain_ref[...] += dgain
    grad = cot_ref[...].astype(F32) + dx
    gres_ref[...] = grad
    gb_ref[...] = grad.astype(BF16)


def combine_back(keyr, res, cot, gf, rows):
    toks, width = res.shape
    tile = pl.BlockSpec((QB, width), lambda i: (i, 0))
    return pl.pallas_call(
        combine_back_kernel,
        grid=(toks // QB,),
        in_specs=[
            pl.BlockSpec((1, QB), lambda i: (0, i)),
            tile,
            tile,
            whole((1, width)),
            *[whole(r.shape) for r in rows],
        ],
        out_specs=[tile, tile, whole((1, width))],
        out_shape=[
            jax.ShapeDtypeStruct((toks, width), F32),
            jax.ShapeDtypeStruct((toks, width), BF16),
            jax.ShapeDtypeStruct((1, width), F32),
        ],
        compiler_params=params(40),
        cost_estimate=cost(8),
        name="combine_back",
    )(keyr, res, cot, gf, *rows)


def combine_kernel(keyr_ref, res_ref, ra_ref, rb_ref, out_ref):
    out_ref[...] = (res_ref[...] + gather_rows(keyr_ref[...], (ra_ref, rb_ref))).astype(BF16)


def combine(keyr, res, rows):
    toks, width = res.shape
    tile = pl.BlockSpec((QB, width), lambda i: (i, 0))
    return pl.pallas_call(
        combine_kernel,
        grid=(toks // QB,),
        in_specs=[
            pl.BlockSpec((1, QB), lambda i: (0, i)),
            tile,
            *[whole(r.shape) for r in rows],
        ],
        out_specs=tile,
        out_shape=jax.ShapeDtypeStruct((toks, width), BF16),
        compiler_params=params(40),
        cost_estimate=cost(5),
        name="combine",
    )(keyr, res, *rows)


def shared_sums_kernel(
    me_ref, mine_ref, other_ref, mine_tail, other_tail, qkv_ref, o_ref, small_ref
):
    pair, part = pl.program_id(0), pl.program_id(1)
    chips, extra = mine_tail.shape[:2]
    quarter = chips // 4
    chip = me_ref[0] >> 1
    is_mine = (me_ref[0] & 1) == pair % 2

    def piece(ref, index):
        blocks = [ref[(index * quarter + t) ^ chip] for t in range(quarter)]
        return jnp.concatenate(blocks, axis=0).astype(F32)

    for ref, chosen in ((mine_ref, is_mine), (other_ref, jnp.logical_not(is_mine))):

        @pl.when(chosen)
        def _(ref=ref):
            qkv_ref[...] = piece(ref, part)

        @pl.when(chosen & (part == 0))
        def _(ref=ref):
            block = piece(ref, 3)
            for j in range(block.shape[0] // PAIR):
                o_ref[:, j * PAIR : (j + 1) * PAIR] = block[j * PAIR : (j + 1) * PAIR]

    @pl.when((pair == 0) & (part == 0))
    def _():
        for t in range(chips):
            both = mine_tail[t ^ chip].astype(F32) + other_tail[t ^ chip].astype(F32)
            small_ref[t * extra : (t + 1) * extra, :] = both


def shared_sums(me, mine, other, width):
    chips = mine.shape[0]
    rows = 4 * width // chips
    count = PAIRS // 2 * rows
    extra = mine.shape[1] - count
    block = pl.BlockSpec((chips, rows, PAIR), lambda pair, part: (0, pair // 2, 0))
    tail = pl.BlockSpec((chips, extra, PAIR), lambda pair, part: (0, count // extra, 0))
    return pl.pallas_call(
        shared_sums_kernel,
        grid=(PAIRS, 3),
        in_specs=[smem(), block, block, tail, tail],
        out_specs=[
            pl.BlockSpec((width, PAIR), lambda pair, part: (0, part * PAIRS + pair)),
            pl.BlockSpec((PAIR, width), lambda pair, part: (pair, 0)),
            whole((chips * extra, PAIR)),
        ],
        out_shape=[
            jax.ShapeDtypeStruct((width, 3 * width), F32),
            jax.ShapeDtypeStruct((width, width), F32),
            jax.ShapeDtypeStruct((chips * extra, PAIR), F32),
        ],
        compiler_params=params(32),
        cost_estimate=cost(8),
        name="shared_sums",
    )(me, mine, other, mine, other)


def exchange(rows):
    peers = lax.axis_size("expert")
    width = rows.shape[1]
    out = lax.all_to_all(
        rows.reshape(peers, -1, width), "expert", split_axis=0, concat_axis=0, tiled=True
    )
    return out.reshape(-1, width)


def core_groups():
    return [[core + 2 * chip for chip in range(lax.axis_size("expert") // 2)] for core in range(2)]


def swap_cores(value):
    peers = lax.axis_size("expert")
    return lax.ppermute(value, "expert", [(j, j ^ 1) for j in range(peers)])


def sum_blocks(blocks):
    return jnp.sum(blocks.astype(F32), axis=0).astype(BF16)


def sum_over_chips(blocks):
    return sum_blocks(
        lax.all_to_all(blocks, "expert", 0, 0, axis_index_groups=core_groups(), tiled=True)
    )


def finish_sums(shares):
    peers = lax.axis_size("expert")
    groups = lax.axis_size("dp")
    joined = jnp.concatenate(shares, axis=0)
    blocks = joined.reshape(groups, joined.shape[0] // groups, -1)
    total = sum_blocks(lax.all_to_all(blocks, "dp", 0, 0, tiled=True))
    total = lax.all_gather(total, "dp", axis=0, tiled=True)
    pieces = [total] + [
        lax.ppermute(total, "expert", [(j, j ^ (2 * d)) for j in range(peers)])
        for d in range(1, peers // 2)
    ]
    mine = jnp.stack(pieces)
    return mine, swap_cores(mine)


def on_device(
    tokens,
    segments,
    routes,
    cotangent,
    w_qkv,
    w_attn_out,
    gain_attn,
    gain_ffn,
    w_router,
    embed,
    w_in,
    w_out,
):
    toks, width = tokens.shape
    experts, rdim = embed.shape
    peers = lax.axis_size("expert")
    shards = lax.axis_size("dp")
    chips = peers // 2
    wide = w_in.shape[2] // shards
    me = lax.axis_index("expert").astype(I32).reshape(1)
    core = me & 1
    ga, gf = gain_attn.reshape(1, width), gain_ffn.reshape(1, width)
    segr = segments.reshape(1, toks)
    wrt = w_router.T
    hold = lax.optimization_barrier

    keyr, g_slots = place(routes.reshape(1, toks), cotangent, peers, 2 * toks)
    g_rows = exchange(g_slots).reshape(peers, 2, toks // peers, width)
    q, k, v, lse, mixt, attn_in, res, xa_slots, xb_slots = attend(
        tokens, segr, keyr, w_qkv, w_attn_out, ga, gf
    )
    x_a = exchange(xa_slots)
    gact_a, gt_a = grad_act(g_rows, 0, w_out, wide)
    gact_b, gt_b = grad_act(g_rows, 1, w_out, wide)
    x_a, xb_slots, gact_b, gt_b = hold((x_a, xb_slots, gact_b, gt_b))
    x_b = exchange(xb_slots)
    act_a, gp_a, xt_a, gout_a, gwr_a, gemb_a = expert(me, wrt, embed, x_a, w_in, gact_a, wide)
    gback_a = exchange(gout_a)
    gw, act_b, gout_b, gwr_b, gemb_b = expert(
        me, wrt, embed, x_b, w_in, gact_b, wide, (act_a, gp_a, xt_a, gt_a, gt_b)
    )
    expert_total = lax.psum_scatter(gw, "dp", scatter_dimension=0, tiled=True)[0]
    gout_b, gback_a = hold((gout_b, gback_a))
    gback_b = exchange(gout_b)
    attnt = attn_in.T
    fout_a, fout_b = expert_out_of(act_a, act_b, w_out, wide)
    gback_b, fout_a, fout_b, attnt = hold((gback_b, fout_a, fout_b, attnt))
    gres, gb, ggf = combine_back(keyr, res, cotangent, gf, (gback_a, gback_b))

    gatt = jnp.zeros((toks, width), F32)
    fback, both, shares = [], [], []
    for turn in range(PAIRS // 2):
        final = (tokens, gres, ga) if turn + 1 == PAIRS // 2 else ()
        send, keep, gatt, *gga = attend_back(
            2 * turn, core, segr, q, k, v, lse, mixt, gb, attnt, w_attn_out, w_qkv, gatt, final
        )
        got = swap_cores(send)
        both.append((keep.astype(F32) + got.astype(F32)).astype(BF16).reshape(chips, -1, PAIR))
        if turn == 0:
            fback.append(exchange(fout_a))
            gatt, fout_b, *fback = hold((gatt, fout_b, *fback))
        elif not final:
            fback.append(exchange(fout_b))
            gatt, both, fback = hold((gatt, both, fback))
            shares.append(sum_over_chips(jnp.concatenate(both, axis=1)))
            both = []
    grad_tokens = gatt
    gemb = (gemb_a + gemb_b).reshape(-1)
    small = jnp.concatenate(
        [
            gga[0].reshape(-1, LANES),
            ggf.reshape(-1, LANES),
            (gwr_a + gwr_b).reshape(-1, LANES),
            jnp.pad(gemb, (0, -experts * rdim % LANES)).reshape(-1, LANES),
        ],
        axis=0,
    )
    small = jnp.pad(small, ((0, -small.shape[0] % (16 * chips)), (0, 0))).astype(BF16)
    small = small.reshape(chips, -1, LANES)
    shares.append(sum_over_chips(jnp.concatenate([*both, small], axis=1)))
    mine, others = finish_sums(shares)
    grad_w_qkv, grad_w_attn_out, small = shared_sums(me, mine, others, width)
    small = small.reshape(-1)
    grad_gain_attn = small[:width]
    grad_gain_ffn = small[width : 2 * width]
    grad_router = small[2 * width : (2 + rdim) * width].reshape(rdim, width).T
    at = (2 + rdim) * width
    grad_embed = small[at : at + experts * rdim].reshape(experts, rdim)
    out_tokens = combine(keyr, res, fback)
    grad_w_in, grad_w_out = expert_sums(expert_total)
    return (
        out_tokens,
        grad_tokens,
        grad_w_qkv,
        grad_w_attn_out,
        grad_gain_attn,
        grad_gain_ffn,
        grad_router,
        grad_embed,
        grad_w_in,
        grad_w_out,
    )


def solution(mesh):
    rows = P(("dp", "expert"), None)
    return jax.shard_map(
        on_device,
        mesh=mesh,
        in_specs=(
            rows,
            rows,
            rows,
            rows,
            P(),
            P(),
            P(),
            P(),
            P(),
            P(),
            P("expert", None, None),
            P("expert", None, None),
        ),
        out_specs=(
            rows,
            rows,
            P(),
            P(),
            P(),
            P(),
            P(),
            P(),
            P("expert", None, "dp"),
            P("expert", "dp", None),
        ),
        check_vma=False,
    )
```

time: 551 us -> 427 us (0.77)
  waiting for transfers between devices: 112 us -> 41.5 us
  local copies, waits for them, and re-layouts: 64.8 us -> 31.3 us
  starting transfers between devices: 76.3 us -> 44.4 us
  Pallas kernels: 209 us -> 236 us
  blocking collectives: 51.5 us -> 39.3 us
    ppermute x64 -> x7, waiting for transfers between devices: 112 us -> 24.6 us  [the longest x3 23 us: finish_sums(): lax.ppermute(total, 'expert', [(j, j ^ 2 * d) for j in range(peers)])]
    ppermute x64 -> x7, starting transfers between devices: 76.3 us -> 4.66 us  [the longest x3 3.49 us: finish_sums(): lax.ppermute(total, 'expert', [(j, j ^ 2 * d) for j in range(peers)])]
    psum x1 -> x0, blocking collectives: 51.5 us -> none  [on_device(): lax.psum(jnp.concatenate([gga.reshape(-1), ggf.reshape(-1), gwr[:, :rdim]...]
    all_to_all x0 -> x9, starting transfers between devices: none -> 39.3 us  [the longest x7 30.4 us: exchange(): lax.all_to_all(rows.reshape(peers, -1, width), 'expert', split_axis=0, co...]
    pallas_call x8 -> x14, Pallas kernels: 209 us -> 236 us  [the longest x2 71.3 us: expert(): pl.pallas_call(functools.partial(expert_kernel, grads), grid=(steps,), in...]
    all_to_all x0 -> x1, blocking collectives: none -> 22.9 us  [finish_sums(): total = sum_blocks(lax.all_to_all(blocks, 'dp', 0, 0, tiled=True))]
    all_to_all x0 -> x9, waiting for transfers between devices: none -> 16.9 us  [the longest x2 10.2 us: sum_over_chips(): lax.all_to_all(blocks, 'expert', 0, 0, axis_index_groups=core_groups(), t...]
    all_gather x0 -> x1, blocking collectives: none -> 16.5 us  [finish_sums(): total = lax.all_gather(total, 'dp', axis=0, tiled=True)]
  transfers between devices with their start and end apart: 66 -> 17, of which waited for: 25 -> 6; matrix products, arithmetic and copies ran while one was open for 8% -> 5% of each run, Pallas kernels for 21% -> 54%
where the time goes in v2:
time: 427 us; the launch traced here: 423 us
  Pallas kernels  236 us (55%)
  starting transfers between devices  44.4 us (10%)
  waiting for transfers between devices  41.5 us (10%)
  blocking collectives  39.3 us (9%)
  local copies, waits for them, and re-layouts  31.3 us (7%)
  other arithmetic  15.6 us (4%)
  between operations  14.7 us (3%)
    pallas_call x2, Pallas kernels, expert(): pl.pallas_call(functools.partial(expert_kernel, grads), grid=(steps,), in...  71.3 us
    pallas_call x3, Pallas kernels, attend_back(): pl.pallas_call(functools.partial(attend_back_kernel, bool(final)), grid_s...  61.2 us
    pallas_call x1, Pallas kernels, attend(): pl.pallas_call(attend_kernel, grid=(PAIRS,), in_specs=[whole((toks, width...  44.3 us
    all_to_all x7, starting transfers between devices, exchange(): lax.all_to_all(rows.reshape(peers, -1, width), 'expert', split_axis=0, co...  30.4 us
    unnamed x58, local copies, waits for them, and re-layouts  24.6 us
    ppermute x3, waiting for transfers between devices, finish_sums(): lax.ppermute(total, 'expert', [(j, j ^ 2 * d) for j in range(peers)])  23 us
    all_to_all x1, blocking collectives, finish_sums(): total = sum_blocks(lax.all_to_all(blocks, 'dp', 0, 0, tiled=True))  22.9 us
    all_gather x1, blocking collectives, finish_sums(): total = lax.all_gather(total, 'dp', axis=0, tiled=True)  16.5 us
  transfers between devices with their start and end apart: 17, of which 6 were waited for; matrix products, arithmetic and copies ran while one was open for 5% of the time, Pallas kernels for 54%

profile of v2, /device:TPU:0, one launch (start us, length us, event | category | flops | bytes accessed | tf_op | source)
XLA Modules:
  0.0 423.1 jit_solution(12613577813657839492)
XLA Ops:
  15.3 5.5 %all-to-all-start.1 = ((bf16[8,256,768]{2,1,0:T(8,128)(2,1)}), bf16[8,256,768]{2,1,0:T(8,128)(2,1)S(1)}, u32[]{:S(2)}, u32[]{:S(2)}) async-start(bf16[8,256,768]{2,1,0:T(8,128)(2,1)} %bitcast.34), calls=%async_computation.1 | async-start | bytes 6291456 | tf_op jit(solution)/shard_map/all_to_all | solution.py:783
  22.0 44.3 %attend.1 = (bf16[1024,768]{1,0:T(8,128)(2,1)}, bf16[1024,768]{1,0:T(8,128)(2,1)}, bf16[1024,768]{1,0:T(8,128)(2,1)}, f32[6,2,1024]{2,1,0:T(2,128)}, bf16[768,10...) custom-call(bf16[1024,768]{1,0:T(8,128)(2,1)} %rest_1_.1, ...), custom_call_target="tpu_custom_call" | custom-call | flops 48299999232 | tf_op jit(solution)/shard_map/attend/pallas_call | solution.py:202
  66.4 4.5 %all-to-all-start = ((bf16[8,128,768]{2,1,0:T(8,128)(2,1)}), bf16[8,128,768]{2,1,0:T(8,128)(2,1)}, u32[]{:S(2)}, u32[]{:S(2)}) async-start(bf16[8,128,768]{2,1,0:T(8,128)(2,1)} %bitcast.51), calls=%async_computation | async-start | bytes 3145728 | tf_op jit(solution)/shard_map/all_to_all | solution.py:783
  73.3 8.1 %grad_act.2 = (bf16[1024,3072]{1,0:T(8,128)(2,1)}, bf16[768,1024]{1,0:T(8,128)(2,1)S(1)}) custom-call(bf16[8,2,128,768]{3,2,1,0:T(8,128)(2,1)S(1)} %bitcast.32, bf16[1,3072,768]{2,1,0:T(8,128)(2,1)S(1)} %copy-done.6), custom_call_target="tpu_custom_call" | custom-call | flops 8049999872 | tf_op jit(solution)/shard_map/grad_act/pallas_call | solution.py:566
  82.6 8.0 %grad_act.3 = (bf16[1024,3072]{1,0:T(8,128)(2,1)}, bf16[768,1024]{1,0:T(8,128)(2,1)S(1)}) custom-call(bf16[8,2,128,768]{3,2,1,0:T(8,128)(2,1)S(1)} %bitcast.33, bf16[1,3072,768]{2,1,0:T(8,128)(2,1)S(1)} %copy-done.6), custom_call_target="tpu_custom_call" | custom-call | flops 8049999872 | tf_op jit(solution)/shard_map/grad_act/pallas_call | solution.py:566
  95.9 24.7 %expert.2 = (bf16[1024,3072]{1,0:T(8,128)(2,1)}, bf16[1024,3072]{1,0:T(8,128)(2,1)}, bf16[768,1024]{1,0:T(8,128)(2,1)}, bf16[1024,768]{1,0:T(8,128)(2,1)}, f32[16,768]{1,0:T(8,128)}, /*index=5*/f32[8,16]{1,0:T(8,128)}) custom-call(s32[1]{0:T(128)} %bitcast.1.me_ref, bf16[16,768]{1,0:T(8,128)(2,1)} %bitcast.59, f32[8,16]{1,0:T(8,128)} %emb_ref.3, ...), custom_call_target="tpu_custom_call" | custom-call | flops 27599998976 | tf_op jit(solution)/shard_map/expert/pallas_call | solution.py:539
  121.8 4.2 all-to-all-start.3
  126.4 46.5 %expert.3 = (bf16[4,2,768,768]{3,2,1,0:T(8,128)(2,1)}, bf16[1024,3072]{1,0:T(8,128)(2,1)}, bf16[1024,768]{1,0:T(8,128)(2,1)}, f32[16,768]{1,0:T(8,128)}, f32[8,16]{1,0:T(8,128)}) custom-call(s32[1]{0:T(128)} %bitcast.1.me_ref, bf16[16,768]{1,0:T(8,128)(2,1)} %bitcast.60, f32[8,16]{1,0:T(8,128)} %emb_ref.3, bf16[1024,768]{1,0:T(8,128)(2,1)} %bitcast.50, ...), custom_call_target="tpu_custom_call" | custom-call | flops 51749998592 | tf_op jit(solution)/shard_map/expert/pallas_call | solution.py:539
  177.1 4.5 %all-to-all-start.4 = ((bf16[8,128,768]{2,1,0:T(8,128)(2,1)}), bf16[8,128,768]{2,1,0:T(8,128)(2,1)}, u32[]{:S(2)}, u32[]{:S(2)}) async-start(bf16[8,128,768]{2,1,0:T(8,128)(2,1)} %bitcast.49), calls=%async_computation.4 | async-start | bytes 3145728 | tf_op jit(solution)/shard_map/all_to_all | solution.py:783
  181.6 13.5 %expert_out.1 = (bf16[1024,768]{1,0:T(8,128)(2,1)S(1)}, bf16[1024,768]{1,0:T(8,128)(2,1)S(1)}) custom-call(bf16[1024,3072]{1,0:T(8,128)(2,1)} %get-tuple-element.90.rest_0_.acta_ref, bf16[1024,3072]{1,0:T(8,128)(2,1)} %get-tuple-element.99.actb_ref, bf16[1,3072,768]{2,1,0:T(8,128)(2,1)} %wout_ref.5), custom_call_target="tpu_custom_call" | custom-call | flops 16099999744 | tf_op jit(solution)/shard_map/expert_out/pallas_call | solution.py:607
  196.3 6.4 %all-to-all-done.4 = bf16[8,128,768]{2,1,0:T(8,128)(2,1)} async-done(((bf16[8,128,768]{2,1,0:T(8,128)(2,1)}), bf16[8,128,768]{2,1,0:T(8,128)(2,1)}, u32[]{:S(2)}, u32[]{:S(2)}) %all-to-all-start.4) | async-done | bytes 1572896 | tf_op jit(solution)/shard_map/all_to_all | solution.py:783
  211.1 8.1 %combine_back.1 = (f32[1024,768]{1,0:T(8,128)S(1)}, bf16[1024,768]{1,0:T(8,128)(2,1)S(1)}, f32[1,768]{1,0:T(1,128)S(1)}) custom-call(s32[1,1024]{1,0:T(1,128)S(1)} %copy-done.18, f32[1024,768]{1,0:T(8,128)S(1)} %copy-done.11, bf16[1024,768]{1,0:T(8,128)(2,1)S(1)} %copy-done.9, f32[1,768]{1,0:T(1,128)S(1)} %copy-done.5, bf16[1024,768]{1,0:T(8,128)(2,1)S(1)} %bitcast.38, ...), custom_call_target="tpu_custom_call" | custom-call | flops 9200000000 | tf_op jit(solution)/shard_map/combine_back/pallas_call | solution.py:676
  223.9 19.3 %attend_back.3 = (bf16[4,768,128]{2,1,0:T(8,128)(2,1)}, bf16[4,768,128]{2,1,0:T(8,128)(2,1)}, f32[1024,768]{1,0:T(8,128)}) custom-call(s32[1]{0:T(128)S(6)} %and.4.core_ref, s32[1,1024]{1,0:T(1,128)} %segr_ref.7, bf16[1024,768]{1,0:T(8,128)(2,1)} %get-tuple-element.76.q_ref, bf16[1024,768]{1,0:T(8,128)(2,1)} %get-tuple-element.77.k_ref, ...), custom_call_target="tpu_custom_call" | custom-call | flops 21849999360 | tf_op jit(solution)/shard_map/attend_back/pallas_call | solution.py:376
  247.8 19.3 %attend_back.4 = (bf16[4,768,128]{2,1,0:T(8,128)(2,1)}, bf16[4,768,128]{2,1,0:T(8,128)(2,1)}, f32[1024,768]{1,0:T(8,128)}) custom-call(s32[1]{0:T(128)S(6)} %and.4.core_ref, s32[1,1024]{1,0:T(1,128)} %segr_ref.7, bf16[1024,768]{1,0:T(8,128)(2,1)} %get-tuple-element.76.q_ref, bf16[1024,768]{1,0:T(8,128)(2,1)} %get-tuple-element.77.k_ref, ...), custom_call_target="tpu_custom_call" | custom-call | flops 21849999360 | tf_op jit(solution)/shard_map/attend_back/pallas_call | solution.py:376
  273.6 4.6 %all-to-all-start.7 = ((bf16[4,1536,128]{2,1,0:T(8,128)(2,1)}), bf16[4,1536,128]{2,1,0:T(8,128)(2,1)}, u32[]{:S(2)}, u32[]{:S(2)}) async-start(bf16[4,1536,128]{2,1,0:T(8,128)(2,1)} %pad_maximum_fusion.1), calls=%async_computation.7 | async-start | bytes 3145728 | tf_op jit(solution)/shard_map/all_to_all | solution.py:804
  278.3 22.7 %attend_back.5 = (bf16[4,768,128]{2,1,0:T(8,128)(2,1)}, bf16[4,768,128]{2,1,0:T(8,128)(2,1)}, f32[1024,768]{1,0:T(8,128)}, f32[1,768]{1,0:T(1,128)}) custom-call(s32[1]{0:T(128)S(6)} %and.4.core_ref, s32[1,1024]{1,0:T(1,128)} %segr_ref.7, bf16[1024,768]{1,0:T(8,128)(2,1)} %get-tuple-element.76.q_ref, bf16[1024,768]{1,0:T(8,128)(2,1)} %get-tuple-element.77.k_ref, ...), custom_call_target="tpu_custom_call" | custom-call | flops 21849999360 | tf_op jit(solution)/shard_map/attend_back/pallas_call | solution.py:376
  306.2 4.2 %all-to-all-start.8 = ((bf16[4,800,128]{2,1,0:T(8,128)(2,1)}), bf16[4,800,128]{2,1,0:T(8,128)(2,1)}, u32[]{:S(2)}, u32[]{:S(2)}) async-start(bf16[4,800,128]{2,1,0:T(8,128)(2,1)} %pad_maximum_fusion.2), calls=%async_computation.8 | async-start | bytes 1638400 | tf_op jit(solution)/shard_map/all_to_all | solution.py:804
  312.3 10.2 %all-to-all-done.8 = bf16[4,800,128]{2,1,0:T(8,128)(2,1)} async-done(((bf16[4,800,128]{2,1,0:T(8,128)(2,1)}), bf16[4,800,128]{2,1,0:T(8,128)(2,1)}, u32[]{:S(2)}, u32[]{:S(2)}) %all-to-all-start.8) | async-done | bytes 819232 | tf_op jit(solution)/shard_map/all_to_all | solution.py:804
  325.4 22.9 %all_to_all.50 = bf16[4,584,128]{2,1,0:T(8,128)(2,1)} all-to-all(bf16[4,584,128]{2,1,0:T(8,128)(2,1)S(1)} %bitcast.43), channel_id=1, replica_groups=mesh['dp'=4,'expert'=8] {'dp'}, dimensions={0} | all-to-all | bytes 1196032 | tf_op jit(solution)/shard_map/all_to_all | solution.py:813
  349.5 16.5 %all_gather.3 = bf16[2336,128]{1,0:T(8,128)(2,1)S(1)} all-gather(bf16[584,128]{1,0:T(8,128)(2,1)S(1)} %reduce_sum.38), channel_id=1, replica_groups=mesh['dp'=4,'expert'=8] {'dp'}, dimensions={0}, use_global_device_ids=true | all-gather | bytes 747520 | tf_op jit(solution)/shard_map/all_gather | solution.py:814
  369.4 13.0 %collective-permute-done.3 = bf16[2336,128]{1,0:T(8,128)(2,1)S(1)} collective-permute-done((bf16[2336,128]{1,0:T(8,128)(2,1)S(1)}, bf16[2336,128]{1,0:T(8,128)(2,1)S(1)}, u32[]{:S(2)}, u32[]{:S(2)}) %collective-permute-start.3) | collective-permute-done | bytes 598048 | tf_op jit(solution)/shard_map/ppermute | solution.py:816
  382.4 10.1 %collective-permute-done.4 = bf16[2336,128]{1,0:T(8,128)(2,1)S(1)} collective-permute-done((bf16[2336,128]{1,0:T(8,128)(2,1)S(1)}, bf16[2336,128]{1,0:T(8,128)(2,1)S(1)}, u32[]{:S(2)}, u32[]{:S(2)}) %collective-permute-start.4) | collective-permute-done | bytes 598048 | tf_op jit(solution)/shard_map/ppermute | solution.py:816
  394.3 5.6 %combine.1 = bf16[1024,768]{1,0:T(8,128)(2,1)} custom-call(s32[1,1024]{1,0:T(1,128)S(1)} %copy-done.18, f32[1024,768]{1,0:T(8,128)S(1)} %copy-done.12, bf16[1024,768]{1,0:T(8,128)(2,1)S(1)} %bitcast.35, bf16[1024,768]{1,0:T(8,128)(2,1)S(1)} %bitcast.36), custom_call_target="tpu_custom_call" | custom-call | flops 5750000128 | tf_op jit(solution)/shard_map/combine/pallas_call | solution.py:705
  400.0 9.0 %shared_sums.1 = (f32[768,2304]{1,0:T(8,128)}, f32[768,768]{1,0:T(8,128)}, f32[128,128]{1,0:T(8,128)S(1)}) custom-call(s32[1]{0:T(128)} %bitcast.1.me_ref, bf16[4,2336,128]{2,1,0:T(8,128)(2,1)S(1)} %pad_maximum_fusion.mine_ref.mine_tail, bf16[4,2336,128]{2,1,0:T(8,128)(2,1)S(1)} %collective-permute-done.6.other_ref.other_tail, ...), custom_call_target="tpu_custom_call" | custom-call | flops 9200000000 | tf_op jit(solution)/shard_map/shared_sums/pallas_call | solution.py:760
  (111 shorter events, 72.9 us)
Async XLA Ops:
  15.3 6.1 %copy-start.26 = (f32[768]{0:T(1024)S(1)}, f32[768]{0:T(1024)}, u32[]{:S(2)}) copy-start(f32[768]{0:T(1024)} %param.19) | copy-start | bytes 9220
  15.3 51.1 %all-to-all-start.1 = ((bf16[8,256,768]{2,1,0:T(8,128)(2,1)}), bf16[8,256,768]{2,1,0:T(8,128)(2,1)S(1)}, u32[]{:S(2)}, u32[]{:S(2)}) async-start(bf16[8,256,768]{2,1,0:T(8,128)(2,1)} %bitcast.34), calls=%async_computation.1 | async-start | bytes 6291456 | tf_op jit(solution)/shard_map/all_to_all | solution.py:783
  66.4 25.6 %all-to-all-start = ((bf16[8,128,768]{2,1,0:T(8,128)(2,1)}), bf16[8,128,768]{2,1,0:T(8,128)(2,1)}, u32[]{:S(2)}, u32[]{:S(2)}) async-start(bf16[8,128,768]{2,1,0:T(8,128)(2,1)} %bitcast.51), calls=%async_computation | async-start | bytes 3145728 | tf_op jit(solution)/shard_map/all_to_all | solution.py:783
  92.0 28.6 %all-to-all-start.2 = ((bf16[8,128,768]{2,1,0:T(8,128)(2,1)}), bf16[8,128,768]{2,1,0:T(8,128)(2,1)S(1)}, u32[]{:S(2)}, u32[]{:S(2)}) async-start(bf16[8,128,768]{2,1,0:T(8,128)(2,1)} %bitcast.47), calls=%async_computation.2 | async-start | bytes 3145728 | tf_op jit(solution)/shard_map/all_to_all | solution.py:783
  121.8 54.2 %all-to-all-start.3 = ((bf16[8,128,768]{2,1,0:T(8,128)(2,1)}), bf16[8,128,768]{2,1,0:T(8,128)(2,1)S(1)}, u32[]{:S(2)}, u32[]{:S(2)}) async-start(bf16[8,128,768]{2,1,0:T(8,128)(2,1)} %bitcast.48), calls=%async_computation.3 | async-start | bytes 3145728 | tf_op jit(solution)/shard_map/all_to_all | solution.py:783
  126.0 284.9 %reduce-scatter.2.cloned.1.call-start = ((), (), s32[]{:S(2)}) async-start(), calls=%async_computation.11 | async-start | bytes 11796480 | tf_op jit(solution)/shard_map/reduce_scatter | solution.py:865
  177.1 25.5 %all-to-all-start.4 = ((bf16[8,128,768]{2,1,0:T(8,128)(2,1)}), bf16[8,128,768]{2,1,0:T(8,128)(2,1)}, u32[]{:S(2)}, u32[]{:S(2)}) async-start(bf16[8,128,768]{2,1,0:T(8,128)(2,1)} %bitcast.49), calls=%async_computation.4 | async-start | bytes 3145728 | tf_op jit(solution)/shard_map/all_to_all | solution.py:783
  196.3 6.4 %copy-start.1 = (bf16[1024,768]{1,0:T(8,128)(2,1)}, bf16[1024,768]{1,0:T(8,128)(2,1)S(1)}, u32[]{:S(2)}) copy-start(bf16[1024,768]{1,0:T(8,128)(2,1)S(1)} %get-tuple-element.116) | copy-start | bytes 4718596
  202.7 41.0 %all-to-all-start.5 = ((bf16[8,128,768]{2,1,0:T(8,128)(2,1)}), bf16[8,128,768]{2,1,0:T(8,128)(2,1)S(1)}, u32[]{:S(2)}, u32[]{:S(2)}) async-start(bf16[8,128,768]{2,1,0:T(8,128)(2,1)} %bitcast.39), calls=%async_computation.5 | async-start | bytes 3145728 | tf_op jit(solution)/shard_map/all_to_all | solution.py:783
  243.2 24.4 %collective-permute-start = (bf16[4,768,128]{2,1,0:T(8,128)(2,1)}, bf16[4,768,128]{2,1,0:T(8,128)(2,1)}, u32[]{:S(2)}, u32[]{:S(2)}) collective-permute-start(bf16[4,768,128]{2,1,0:T(8,128)(2,1)} %get-tuple-element.112), channel_id=1, source_target_pairs={{0,1},{1,0},{2,3},{3,2},{4,5},{5,4},{6,7},{7,6},{8,9},{9,8},{10,11... | collective-permute-start | bytes 2359304 | tf_op jit(solution)/shard_map/ppermute | solution.py:795
  243.6 27.4 %all-to-all-start.6 = ((bf16[8,128,768]{2,1,0:T(8,128)(2,1)}), bf16[8,128,768]{2,1,0:T(8,128)(2,1)S(1)}, u32[]{:S(2)}, u32[]{:S(2)}) async-start(bf16[8,128,768]{2,1,0:T(8,128)(2,1)} %bitcast.37), calls=%async_computation.6 | async-start | bytes 3145728 | tf_op jit(solution)/shard_map/all_to_all | solution.py:783
  247.8 19.8 %copy-start.21 = (bf16[4,768,128]{2,1,0:T(8,128)(2,1)S(1)}, bf16[4,768,128]{2,1,0:T(8,128)(2,1)}, u32[]{:S(2)}) copy-start(bf16[4,768,128]{2,1,0:T(8,128)(2,1)} %get-tuple-element.111) | copy-start | bytes 2359300
  267.1 2.9 collective-permute-start.1
  273.6 32.6 %all-to-all-start.7 = ((bf16[4,1536,128]{2,1,0:T(8,128)(2,1)}), bf16[4,1536,128]{2,1,0:T(8,128)(2,1)}, u32[]{:S(2)}, u32[]{:S(2)}) async-start(bf16[4,1536,128]{2,1,0:T(8,128)(2,1)} %pad_maximum_fusion.1), calls=%async_computation.7 | async-start | bytes 3145728 | tf_op jit(solution)/shard_map/all_to_all | solution.py:804
  278.2 22.9 %copy-start.23 = (f32[16,768]{1,0:T(8,128)S(1)}, f32[16,768]{1,0:T(8,128)}, u32[]{:S(2)}) copy-start(f32[16,768]{1,0:T(8,128)} %get-tuple-element.128) | copy-start | bytes 147460
  278.2 22.9 %copy-start.24 = (f32[16,768]{1,0:T(8,128)S(1)}, f32[16,768]{1,0:T(8,128)}, u32[]{:S(2)}) copy-start(f32[16,768]{1,0:T(8,128)} %get-tuple-element.129) | copy-start | bytes 147460
  278.3 23.0 %copy-start.27 = (f32[8,16]{1,0:T(8,128)S(1)}, f32[8,16]{1,0:T(8,128)}, u32[]{:S(2)}) copy-start(f32[8,16]{1,0:T(8,128)} %get-tuple-element.130) | copy-start | bytes 1540
  278.3 23.0 %copy-start.28 = (f32[8,16]{1,0:T(8,128)S(1)}, f32[8,16]{1,0:T(8,128)}, u32[]{:S(2)}) copy-start(f32[8,16]{1,0:T(8,128)} %get-tuple-element.131) | copy-start | bytes 1540
  301.0 2.7 collective-permute-start.2
  306.2 16.2 %all-to-all-start.8 = ((bf16[4,800,128]{2,1,0:T(8,128)(2,1)}), bf16[4,800,128]{2,1,0:T(8,128)(2,1)}, u32[]{:S(2)}, u32[]{:S(2)}) async-start(bf16[4,800,128]{2,1,0:T(8,128)(2,1)} %pad_maximum_fusion.2), calls=%async_computation.8 | async-start | bytes 1638400 | tf_op jit(solution)/shard_map/all_to_all | solution.py:804
  365.9 16.4 %collective-permute-start.3 = (bf16[2336,128]{1,0:T(8,128)(2,1)S(1)}, bf16[2336,128]{1,0:T(8,128)(2,1)S(1)}, u32[]{:S(2)}, u32[]{:S(2)}) collective-permute-start(bf16[2336,128]{1,0:T(8,128)(2,1)S(1)} %all_gather.3), channel_id=1, source_target_pairs={{0,2},{1,3},{2,0},{3,1},{4,6},{5,7},{6,4},{7,5},{8,10},{9,11},{10,... | collective-permute-start | bytes 1794056 | tf_op jit(solution)/shard_map/ppermute | solution.py:816
  367.4 25.0 %collective-permute-start.4 = (bf16[2336,128]{1,0:T(8,128)(2,1)S(1)}, bf16[2336,128]{1,0:T(8,128)(2,1)S(1)}, u32[]{:S(2)}, u32[]{:S(2)}) collective-permute-start(bf16[2336,128]{1,0:T(8,128)(2,1)S(1)} %all_gather.3), channel_id=1, source_target_pairs={{0,4},{1,5},{2,6},{3,7},{4,0},{5,1},{6,2},{7,3},{8,12},{9,13},{10,... | collective-permute-start | bytes 1794056 | tf_op jit(solution)/shard_map/ppermute | solution.py:816
  369.1 23.4 %collective-permute-start.5 = (bf16[2336,128]{1,0:T(8,128)(2,1)S(1)}, bf16[2336,128]{1,0:T(8,128)(2,1)S(1)}, u32[]{:S(2)}, u32[]{:S(2)}) collective-permute-start(bf16[2336,128]{1,0:T(8,128)(2,1)S(1)} %all_gather.3), channel_id=1, source_target_pairs={{0,6},{1,7},{2,4},{3,5},{4,2},{5,3},{6,0},{7,1},{8,14},{9,15},{10,... | collective-permute-start | bytes 1794056 | tf_op jit(solution)/shard_map/ppermute | solution.py:816
  392.8 7.2 %collective-permute-start.6 = (bf16[4,2336,128]{2,1,0:T(8,128)(2,1)S(1)}, bf16[4,2336,128]{2,1,0:T(8,128)(2,1)S(1)}, u32[]{:S(2)}, u32[]{:S(2)}) collective-permute-start(bf16[4,2336,128]{2,1,0:T(8,128)(2,1)S(1)} %pad_maximum_fusion.mine_ref.mine_tail), channel_id=1, source_target_pairs={{0,1},{1,0},{2,3},{3,2},{4,5},{5,4},{6,7},{7,6},{8,9},{9,8},{10,11... | collective-permute-start | bytes 7176200 | tf_op jit(solution)/shard_map/ppermute | solution.py:795
  (22 other events, 40.9 us)
Sparse Core Ops, SparseCore 0:
  173.1 164.3 reduce-scatter.1

commit v3 on v2

--- a/solution.py
+++ b/solution.py
@@ -1,4 +1,5 @@
 import functools
+import math
 
 import jax
 import jax.numpy as jnp
@@ -31,8 +32,8 @@
     return lax.dot_general(a, b, dims, precision=precision, preferred_element_type=F32)
 
 
-def params(mib):
-    return pltpu.CompilerParams(vmem_limit_bytes=mib * MIB)
+def params():
+    return pltpu.CompilerParams(vmem_limit_bytes=62 * MIB)
 
 
 def cost(micros, nbytes=0):
@@ -76,7 +77,7 @@
             at += step
 
 
-def place_kernel(peers, rr_ref, cot_ref, keyr_ref, g_ref):
+def place_kernel(peers, rr_ref, cot_ref, keyr_ref, keyn_ref, g_ref):
     toks = cot_ref.shape[0]
     cap = g_ref.shape[0] // peers
     half = cap // 2
@@ -88,7 +89,8 @@
     upto = mm(hot_row.astype(BF16), before)
     rank = (jnp.sum(hot_row * upto, axis=0, keepdims=True) - 1.0).astype(I32)
     keyr_ref[...] = rr * half + jnp.where(rank < half, rank, rank + (peers - 1) * half)
-    dispatch(rr * cap + rank, cot_ref[...], (g_ref,))
+    keyn_ref[...] = rr * cap + rank
+    dispatch(keyn_ref[...], cot_ref[...], (g_ref,))
 
 
 def place(routes, cot, peers, slots):
@@ -97,10 +99,11 @@
         functools.partial(place_kernel, peers),
         out_shape=[
             jax.ShapeDtypeStruct((1, toks), I32),
+            jax.ShapeDtypeStruct((1, toks), I32),
             jax.ShapeDtypeStruct((slots, width), BF16),
         ],
         in_specs=[pl.BlockSpec(memory_space=pltpu.VMEM)] * 2,
-        compiler_params=params(40),
+        compiler_params=params(),
         cost_estimate=cost(5),
         name="place",
     )(routes, cot)
@@ -237,14 +240,13 @@
             pltpu.VMEM((toks // QB, 3 * QB, QB), F32),
             pltpu.VMEM((width, toks), BF16),
         ],
-        compiler_params=params(56),
+        compiler_params=params(),
         cost_estimate=cost(42),
         name="attend",
     )(tokens, segr, keyr, w_qkv, w_qkv, w_qkv, w_o, ga, gf)
 
 
 def attend_back_kernel(
-    last,
     core_ref,
     segr_ref,
     q_ref,
@@ -255,16 +257,15 @@
     gb_ref,
     attnt_ref,
     wo_ref,
-    wq_ref,
-    wk_ref,
-    wv_ref,
-    *rest,
+    send_ref,
+    keep_ref,
+    gqkv_ref,
+    bias_ref,
+    dqt_ref,
+    dk_ref,
+    dv_ref,
+    do_ref,
 ):
-    if last:
-        gin_ref, tok_ref, gres_ref, ga_ref, send_ref, keep_ref, gtok_ref, gain_ref, gatt_ref = rest[:9]
-    else:
-        gin_ref, send_ref, keep_ref, gatt_ref = rest[:4]
-    bias_ref, dqt_ref, dk_ref, dv_ref, do_ref = rest[-5:]
     p = pl.program_id(0)
     toks, width = gb_ref.shape
     count = toks // QB
@@ -273,7 +274,6 @@
     @pl.when(p == 0)
     def _():
         fill_bias(bias_ref, segr_ref[...], count)
-        gatt_ref[...] = gin_ref[...]
 
     gb = gb_ref[...]
     do_ref[...] = mm(gb, wo_ref[...], NT).astype(BF16)
@@ -312,8 +312,9 @@
         dk_ref[...].astype(BF16),
         dv_ref[...].astype(BF16),
     ]
-    joined = jnp.concatenate(grads, axis=1)
-    gw = mm(attnt_ref[...], joined).astype(BF16)
+    for part in range(3):
+        gqkv_ref[part] = grads[part]
+    gw = mm(attnt_ref[...], jnp.concatenate(grads, axis=1)).astype(BF16)
     for turn, ref in enumerate((send_ref, keep_ref)):
 
         @pl.when(p == turn)
@@ -323,58 +324,23 @@
             for j in range(width // PAIR):
                 ref[3, j * PAIR : (j + 1) * PAIR, :] = gwo[:, j * PAIR : (j + 1) * PAIR]
 
-    weights = jnp.concatenate([wq_ref[...], wk_ref[...], wv_ref[...]], axis=1)
-    gatt_ref[...] += mm(joined, weights, NT)
-
-    if last:
-
-        @pl.when(p == pl.num_programs(0) - 1)
-        def _():
-            gain = jnp.zeros(gain_ref.shape, F32)
-            for i in range(count):
-                part = slice(i * QB, (i + 1) * QB)
-                dx, dgain = norm_back(tok_ref[part, :].astype(F32), ga_ref[...], gatt_ref[part, :])
-                gtok_ref[part, :] = gres_ref[part, :] + dx
-                gain = gain + dgain
-            gain_ref[...] = gain
-
-
-def attend_back(first, core, segr, q, k, v, lse, mixt, gb, attnt, w_o, w_qkv, gin, final):
+
+def attend_back(first, core, segr, q, k, v, lse, mixt, gb, attnt, w_o):
     toks, width = gb.shape
 
     def pair(p, core_ref):
-        return first + jnp.where(p == 0, 1 - core_ref[0], core_ref[0])
+        return jnp.where(p == 0, 1 - core_ref[0], core_ref[0])
 
     def fixed(shape):
         return pl.BlockSpec(
             shape, lambda p, c: (0,) * len(shape), pipeline_mode=pl.Buffered(buffer_count=1)
         )
 
-    pair_cols = pl.BlockSpec((toks, PAIR), lambda p, c: (0, pair(p, c)))
-    weights = [
-        pl.BlockSpec((width, PAIR), lambda p, c, part=part: (0, part * PAIRS + pair(p, c)))
-        for part in range(3)
-    ]
-    full = fixed((toks, width))
-    row = fixed((1, width))
-    f32_full = jax.ShapeDtypeStruct((toks, width), F32)
+    pair_cols = pl.BlockSpec((toks, PAIR), lambda p, c: (0, first + pair(p, c)))
     gw_spec = fixed((4, width, PAIR))
     gw_shape = jax.ShapeDtypeStruct((4, width, PAIR), BF16)
-    scratch = [
-        pltpu.VMEM((toks // QB, 3 * QB, QB), F32),
-        pltpu.VMEM((PAIR, toks), F32),
-        pltpu.VMEM((toks, PAIR), F32),
-        pltpu.VMEM((toks, PAIR), F32),
-        pltpu.VMEM((toks, PAIR), BF16),
-    ]
-    if final:
-        out_specs = [gw_spec, gw_spec, full, row]
-        out_shape = [gw_shape, gw_shape, f32_full, jax.ShapeDtypeStruct((1, width), F32)]
-        scratch = [pltpu.VMEM((toks, width), F32)] + scratch
-    else:
-        out_specs, out_shape = [gw_spec, gw_spec, full], [gw_shape, gw_shape, f32_full]
-    return pl.pallas_call(
-        functools.partial(attend_back_kernel, bool(final)),
+    return pl.pallas_call(
+        attend_back_kernel,
         grid_spec=pltpu.PrefetchScalarGridSpec(
             num_scalar_prefetch=1,
             grid=(2,),
@@ -383,23 +349,55 @@
                 pair_cols,
                 pair_cols,
                 pair_cols,
-                pl.BlockSpec((1, 2, toks), lambda p, c: (pair(p, c), 0, 0)),
-                pl.BlockSpec((PAIR, toks), lambda p, c: (pair(p, c), 0)),
-                full,
+                pl.BlockSpec((1, 2, toks), lambda p, c: (first + pair(p, c), 0, 0)),
+                pl.BlockSpec((PAIR, toks), lambda p, c: (first + pair(p, c), 0)),
+                fixed((toks, width)),
                 fixed((width, toks)),
-                pl.BlockSpec((PAIR, width), lambda p, c: (pair(p, c), 0)),
-                *weights,
-                full,
-            ]
-            + ([full, full, row] if final else []),
-            out_specs=out_specs,
-            scratch_shapes=scratch,
+                pl.BlockSpec((PAIR, width), lambda p, c: (first + pair(p, c), 0)),
+            ],
+            out_specs=[
+                gw_spec,
+                gw_spec,
+                pl.BlockSpec((3, toks, PAIR), lambda p, c: (0, 0, pair(p, c))),
+            ],
+            scratch_shapes=[
+                pltpu.VMEM((toks // QB, 3 * QB, QB), F32),
+                pltpu.VMEM((PAIR, toks), F32),
+                pltpu.VMEM((toks, PAIR), F32),
+                pltpu.VMEM((toks, PAIR), F32),
+                pltpu.VMEM((toks, PAIR), BF16),
+            ],
         ),
-        out_shape=out_shape,
-        compiler_params=params(56),
-        cost_estimate=cost(19),
+        out_shape=[gw_shape, gw_shape, jax.ShapeDtypeStruct((3, toks, 2 * PAIR), BF16)],
+        compiler_params=params(),
+        cost_estimate=cost(10 if first + 2 == PAIRS else 2),
         name="attend_back",
-    )(core, segr, q, k, v, lse, mixt, gb, attnt, w_o, w_qkv, w_qkv, w_qkv, gin, *final)
+    )(core, segr, q, k, v, lse, mixt, gb, attnt, w_o)
+
+
+def grad_tokens_kernel(tok_ref, gres_ref, ga_ref, w_ref, *rest):
+    *g_refs, out_ref = rest
+    grads = [ref[part] for part in range(3) for ref in g_refs]
+    dy = mm(jnp.concatenate(grads, axis=1), w_ref[...], NT)
+    dx, _ = norm_back(tok_ref[...].astype(F32), ga_ref[...], dy)
+    out_ref[...] = gres_ref[...] + dx
+
+
+def grad_tokens_of(tokens, gres, ga, w_qkv, grads):
+    toks, width = tokens.shape
+    rows = 2 * QB
+    tile = pl.BlockSpec((rows, width), lambda i: (i, 0))
+    return pl.pallas_call(
+        grad_tokens_kernel,
+        grid=(toks // rows,),
+        in_specs=[tile, tile, whole((1, width)), whole(w_qkv.shape)]
+        + [pl.BlockSpec((3, rows, 2 * PAIR), lambda i: (0, i, 0))] * len(grads),
+        out_specs=tile,
+        out_shape=jax.ShapeDtypeStruct((toks, width), F32),
+        compiler_params=params(),
+        cost_estimate=cost(9),
+        name="grad_tokens",
+    )(tokens, gres, ga, w_qkv, *grads)
 
 
 def unit_scale(values, axis):
@@ -431,14 +429,24 @@
     return z, inv, total, zn, en, chances, mine
 
 
-def expert_kernel(grads, me_ref, wrt_ref, emb_ref, x_ref, win_ref, ga_ref, *rest):
-    if grads:
-        acta_ref, gpa_ref, xta_ref, gta_ref, gtb_ref, gw_ref, act_ref, *rest = rest
-    else:
-        act_ref, gp_ref, xt_ref, *rest = rest
-    gout_ref, gwrt_ref, gemb_ref, gin_s, acc_s, gate_s, *rest = rest
-    if grads:
-        gp_ref, xt_ref = rest
+def expert_kernel(
+    me_ref,
+    wrt_ref,
+    emb_ref,
+    x_ref,
+    win_ref,
+    ga_ref,
+    act_ref,
+    gp_ref,
+    xt_ref,
+    gout_ref,
+    gwrt_ref,
+    gemb_ref,
+    w_s,
+    gp_s,
+    acc_s,
+    gate_s,
+):
     c = pl.program_id(0)
     rows, width = x_ref.shape
     me = me_ref[0]
@@ -448,13 +456,14 @@
         chances, mine = route(me, x_ref[...], wrt_ref[...], emb_ref[...])[-2:]
         gate = column_of(jnp.sum(chances * mine, axis=0, keepdims=True))
         gate_s[...] = jnp.broadcast_to(gate, (rows, LANES))
+        acc_s[...] = jnp.zeros_like(acc_s)
         for r in range(0, rows, QB):
             xt_ref[:, r : r + QB] = x_ref[r : r + QB, :].T
-        gin_s[...] = jnp.zeros_like(gin_s)
-        acc_s[...] = jnp.zeros_like(acc_s)
 
     w_in = win_ref[0]
     wide = w_in.shape[1]
+    chunk = pl.ds(pl.multiple_of(c * wide, LANES), wide)
+    w_s[:, chunk] = w_in
     step = min(2 * QB, rows)
     for r in range(0, rows, step):
         part = slice(r, r + step)
@@ -465,18 +474,13 @@
         act = act * gate
         act_ref[part, :] = act.astype(BF16)
         gp = (ga * (slope * gate)).astype(BF16)
+        gp_s[part, chunk] = gp
         gp_ref[part, :] = gp
         prod = act * ga
         folded = prod[:, :LANES]
         for j in range(LANES, wide, LANES):
             folded = folded + prod[:, j : j + LANES]
         acc_s[part, :] += folded
-        gin_s[part, :] += mm(gp, w_in, NT)
-    if grads:
-        gw_ref[0, 0] = (mm(xta_ref[...], gpa_ref[...]) + mm(xt_ref[...], gp_ref[...])).astype(BF16)
-        gw_ref[0, 1] = (mm(gta_ref[...], acta_ref[...]) + mm(gtb_ref[...], act_ref[...])).astype(
-            BF16
-        )
 
     @pl.when(c == pl.num_programs(0) - 1)
     def _():
@@ -492,61 +496,83 @@
         einv, etotal = unit_scale(emb, 1)
         gemb_ref[...] = unit_back(emb, einv, etotal, gen, 1)
         dz_top, dz_low = dz_top.astype(F32).T.astype(BF16), dz_low.astype(F32).T.astype(BF16)
-        for r in range(0, rows, QB):
-            part = slice(r, r + QB)
-            back = gin_s[part, :].astype(BF16).astype(F32)
+        for r in range(0, rows, step):
+            part = slice(r, r + step)
+            back = mm(gp_s[part, :], w_s[...], NT).astype(BF16).astype(F32)
             back = back + mm(dz_top[part], wrt) + mm(dz_low[part], wrt)
             gout_ref[part, :] = back.astype(BF16)
 
 
-def expert(me, wrt, emb, x, w_in, ga, wide, other=None):
+def expert(me, wrt, emb, x, w_in, ga, wide):
     rows, width = x.shape
     hidden = w_in.shape[2]
-    steps = hidden // wide
-    grads = other is not None
     cols = pl.BlockSpec((rows, wide), lambda c: (0, c))
     hid = jax.ShapeDtypeStruct((rows, hidden), BF16)
-    xt_spec = whole((width, rows))
-    operands = [me, wrt, emb, x, w_in, ga]
-    in_specs = [
-        smem(),
-        whole(wrt.shape),
-        whole(emb.shape),
-        whole((rows, width)),
-        pl.BlockSpec((1, width, wide), lambda c: (0, 0, c)),
-        cols,
-    ]
-    scratch = [
-        pltpu.VMEM((rows, width), F32),
-        pltpu.VMEM((rows, LANES), F32),
-        pltpu.VMEM((rows, LANES), F32),
-    ]
-    if grads:
-        operands += list(other)
-        in_specs += [cols, cols, xt_spec, xt_spec, xt_spec]
-        out_specs = [pl.BlockSpec((1, 2, width, wide), lambda c: (c, 0, 0, 0)), cols]
-        out_shape = [jax.ShapeDtypeStruct((steps, 2, width, wide), BF16), hid]
-        scratch += [pltpu.VMEM((rows, wide), BF16), pltpu.VMEM((width, rows), BF16)]
-    else:
-        out_specs = [cols, cols, xt_spec]
-        out_shape = [hid, hid, jax.ShapeDtypeStruct((width, rows), BF16)]
-    out_specs += [whole((rows, width)), whole(wrt.shape), whole(emb.shape)]
-    out_shape += [
-        jax.ShapeDtypeStruct((rows, width), BF16),
-        jax.ShapeDtypeStruct(wrt.shape, F32),
-        jax.ShapeDtypeStruct(emb.shape, F32),
-    ]
-    return pl.pallas_call(
-        functools.partial(expert_kernel, grads),
+    return pl.pallas_call(
+        expert_kernel,
+        grid=(hidden // wide,),
+        in_specs=[
+            smem(),
+            whole(wrt.shape),
+            whole(emb.shape),
+            whole((rows, width)),
+            pl.BlockSpec((1, width, wide), lambda c: (0, 0, c)),
+            cols,
+        ],
+        out_specs=[
+            cols,
+            cols,
+            whole((width, rows)),
+            whole((rows, width)),
+            whole(wrt.shape),
+            whole(emb.shape),
+        ],
+        out_shape=[
+            hid,
+            hid,
+            jax.ShapeDtypeStruct((width, rows), BF16),
+            jax.ShapeDtypeStruct((rows, width), BF16),
+            jax.ShapeDtypeStruct(wrt.shape, F32),
+            jax.ShapeDtypeStruct(emb.shape, F32),
+        ],
+        scratch_shapes=[
+            pltpu.VMEM((width, hidden), BF16),
+            pltpu.VMEM((rows, hidden), BF16),
+            pltpu.VMEM((rows, LANES), F32),
+            pltpu.VMEM((rows, LANES), F32),
+        ],
+        compiler_params=params(),
+        cost_estimate=cost(23),
+        name="expert",
+    )(me, wrt, emb, x, w_in, ga)
+
+
+def expert_grads_kernel(lefta_ref, leftb_ref, righta_ref, rightb_ref, out_ref, left_s):
+    rows = lefta_ref.shape[1]
+
+    @pl.when(pl.program_id(0) == 0)
+    def _():
+        left_s[:, :rows] = lefta_ref[...]
+        left_s[:, rows:] = leftb_ref[...]
+
+    right = jnp.concatenate([righta_ref[...], rightb_ref[...]], axis=0)
+    out_ref[0] = mm(left_s[...], right).astype(BF16)
+
+
+def expert_grads(lefts, rights, wide):
+    width, rows = lefts[0].shape
+    steps = rights[0].shape[1] // wide
+    return pl.pallas_call(
+        expert_grads_kernel,
         grid=(steps,),
-        in_specs=in_specs,
-        out_specs=out_specs,
-        out_shape=out_shape,
-        scratch_shapes=scratch,
-        compiler_params=params(60),
-        cost_estimate=cost(45 if grads else 24),
-        name="expert",
-    )(*operands)
+        in_specs=[whole((width, rows))] * 2 + [pl.BlockSpec((rows, wide), lambda c: (0, c))] * 2,
+        out_specs=pl.BlockSpec((1, width, wide), lambda c: (c, 0, 0)),
+        out_shape=jax.ShapeDtypeStruct((steps, width, wide), BF16),
+        scratch_shapes=[pltpu.VMEM((width, 2 * rows), BF16)],
+        compiler_params=params(),
+        cost_estimate=cost(5),
+        name="expert_grads",
+    )(*lefts, *rights)
 
 
 def grad_act_kernel(g_ref, wout_ref, out_ref, gt_ref):
@@ -575,15 +601,16 @@
             jax.ShapeDtypeStruct((rows, hidden), BF16),
             jax.ShapeDtypeStruct((width, rows), BF16),
         ],
-        compiler_params=params(40),
+        compiler_params=params(),
         cost_estimate=cost(7),
         name="grad_act",
     )(g, w_out)
 
 
-def expert_out_kernel(acta_ref, actb_ref, wout_ref, outa_ref, outb_ref, acc_ref):
+def expert_out_kernel(acta_ref, actb_ref, wout_ref, out_ref, acc_ref):
     c = pl.program_id(0)
     rows = acta_ref.shape[0]
+    peers, _, slots, width = out_ref.shape
 
     @pl.when(c == 0)
     def _():
@@ -595,52 +622,53 @@
 
     @pl.when(c == pl.num_programs(0) - 1)
     def _():
-        outa_ref[...] = acc_ref[:rows, :].astype(BF16)
-        outb_ref[...] = acc_ref[rows:, :].astype(BF16)
-
-
-def expert_out_of(acta, actb, w_out, wide):
+        for h in range(2):
+            part = acc_ref[h * rows : (h + 1) * rows, :].astype(BF16)
+            out_ref[:, h] = part.reshape(peers, slots, width)
+
+
+def expert_out_of(acta, actb, w_out, wide, peers):
     rows, hidden = acta.shape
     width = w_out.shape[2]
-    block = jax.ShapeDtypeStruct((rows, width), BF16)
+    shape = (peers, 2, rows // peers, width)
     cols = pl.BlockSpec((rows, wide), lambda c: (0, c))
     return pl.pallas_call(
         expert_out_kernel,
         grid=(hidden // wide,),
         in_specs=[cols, cols, pl.BlockSpec((1, wide, width), lambda c: (0, c, 0))],
-        out_specs=[whole((rows, width))] * 2,
-        out_shape=[block] * 2,
+        out_specs=whole(shape),
+        out_shape=jax.ShapeDtypeStruct(shape, BF16),
         scratch_shapes=[pltpu.VMEM((2 * rows, width), F32)],
-        compiler_params=params(50),
+        compiler_params=params(),
         cost_estimate=cost(14),
         name="expert_out",
     )(acta, actb, w_out)
 
 
-def expert_sums_kernel(sum_ref, win_ref, wout_ref):
-    win_ref[0] = sum_ref[0].astype(F32)
-    wout_ref[0] = sum_ref[1].astype(F32).T
-
-
-def expert_sums(total):
-    _, width, share = total.shape
-    wide = LANES
+def expert_sums_kernel(in_ref, out_ref, win_ref, wout_ref):
+    win_ref[0] = in_ref[...].astype(F32)
+    wout_ref[0] = out_ref[...].astype(F32).T
+
+
+def expert_sums(grad_in, grad_out):
+    width, share = grad_in.shape
+    block = pl.BlockSpec((width, LANES), lambda k: (0, k))
     return pl.pallas_call(
         expert_sums_kernel,
-        grid=(share // wide,),
-        in_specs=[pl.BlockSpec((2, width, wide), lambda k: (0, 0, k))],
+        grid=(share // LANES,),
+        in_specs=[block, block],
         out_specs=[
-            pl.BlockSpec((1, width, wide), lambda k: (0, 0, k)),
-            pl.BlockSpec((1, wide, width), lambda k: (0, k, 0)),
+            pl.BlockSpec((1, width, LANES), lambda k: (0, 0, k)),
+            pl.BlockSpec((1, LANES, width), lambda k: (0, k, 0)),
         ],
         out_shape=[
             jax.ShapeDtypeStruct((1, width, share), F32),
             jax.ShapeDtypeStruct((1, share, width), F32),
         ],
-        compiler_params=params(32),
+        compiler_params=params(),
         cost_estimate=cost(3),
         name="expert_sums",
-    )(total)
+    )(grad_in, grad_out)
 
 
 def gather_rows(key_row, row_refs):
@@ -689,17 +717,17 @@
             jax.ShapeDtypeStruct((toks, width), BF16),
             jax.ShapeDtypeStruct((1, width), F32),
         ],
-        compiler_params=params(40),
-        cost_estimate=cost(8),
+        compiler_params=params(),
+        cost_estimate=cost(100),
         name="combine_back",
     )(keyr, res, cot, gf, *rows)
 
 
-def combine_kernel(keyr_ref, res_ref, ra_ref, rb_ref, out_ref):
-    out_ref[...] = (res_ref[...] + gather_rows(keyr_ref[...], (ra_ref, rb_ref))).astype(BF16)
-
-
-def combine(keyr, res, rows):
+def combine_kernel(keyn_ref, res_ref, rows_ref, out_ref):
+    out_ref[...] = (res_ref[...] + gather_rows(keyn_ref[...], (rows_ref,))).astype(BF16)
+
+
+def combine(keyn, res, rows):
     toks, width = res.shape
     tile = pl.BlockSpec((QB, width), lambda i: (i, 0))
     return pl.pallas_call(
@@ -708,73 +736,112 @@
         in_specs=[
             pl.BlockSpec((1, QB), lambda i: (0, i)),
             tile,
-            *[whole(r.shape) for r in rows],
+            whole(rows.shape),
         ],
         out_specs=tile,
         out_shape=jax.ShapeDtypeStruct((toks, width), BF16),
-        compiler_params=params(40),
+        compiler_params=params(),
         cost_estimate=cost(5),
         name="combine",
-    )(keyr, res, *rows)
-
-
-def shared_sums_kernel(
-    me_ref, mine_ref, other_ref, mine_tail, other_tail, qkv_ref, o_ref, small_ref
-):
-    pair, part = pl.program_id(0), pl.program_id(1)
-    chips, extra = mine_tail.shape[:2]
-    quarter = chips // 4
-    chip = me_ref[0] >> 1
-    is_mine = (me_ref[0] & 1) == pair % 2
-
-    def piece(ref, index):
-        blocks = [ref[(index * quarter + t) ^ chip] for t in range(quarter)]
-        return jnp.concatenate(blocks, axis=0).astype(F32)
-
-    for ref, chosen in ((mine_ref, is_mine), (other_ref, jnp.logical_not(is_mine))):
-
-        @pl.when(chosen)
-        def _(ref=ref):
-            qkv_ref[...] = piece(ref, part)
-
-        @pl.when(chosen & (part == 0))
-        def _(ref=ref):
-            block = piece(ref, 3)
-            for j in range(block.shape[0] // PAIR):
-                o_ref[:, j * PAIR : (j + 1) * PAIR] = block[j * PAIR : (j + 1) * PAIR]
-
-    @pl.when((pair == 0) & (part == 0))
-    def _():
-        for t in range(chips):
-            both = mine_tail[t ^ chip].astype(F32) + other_tail[t ^ chip].astype(F32)
-            small_ref[t * extra : (t + 1) * extra, :] = both
-
-
-def shared_sums(me, mine, other, width):
-    chips = mine.shape[0]
-    rows = 4 * width // chips
-    count = PAIRS // 2 * rows
-    extra = mine.shape[1] - count
-    block = pl.BlockSpec((chips, rows, PAIR), lambda pair, part: (0, pair // 2, 0))
-    tail = pl.BlockSpec((chips, extra, PAIR), lambda pair, part: (0, count // extra, 0))
-    return pl.pallas_call(
-        shared_sums_kernel,
-        grid=(PAIRS, 3),
-        in_specs=[smem(), block, block, tail, tail],
+    )(keyn, res, rows)
+
+
+def shared_sums_kernel(count, experts, rows, extra, me_ref, w_ref, ga_ref, *rest):
+    blocks, rest = rest[: 2 * count], rest[2 * count :]
+    qkv_ref, o_ref, gain_ref, gain_ffn_ref, router_ref, embed_ref = rest[:6]
+    held, small_s, sems = rest[6:]
+    i = pl.program_id(0)
+    width = o_ref.shape[1]
+    chip, core = me_ref[0] >> 1, me_ref[0] & 1
+    grain = math.gcd(rows, PAIR)
+
+    @pl.when(i == 0)
+    def _():
+        copies = []
+        for n, ref in enumerate(blocks):
+            side = core if n < count else 1 - core
+            copies.append(
+                pltpu.make_async_copy(ref, held.at[side, (n % count) ^ chip], sems.at[n])
+            )
+        for copy in copies:
+            copy.start()
+        for copy in copies:
+            copy.wait()
+
+    def piece(side, two, row):
+        base = two * rows + (two // 2) * extra
+        pieces = []
+        for t in range(0, PAIR, grain):
+            at = pl.multiple_of(base + (row + t) % rows, math.gcd(grain, extra))
+            pieces.append(held[side, (row + t) // rows, pl.ds(at, grain), :])
+        return jnp.concatenate(pieces, axis=0).astype(F32)
+
+    for pair in range(PAIRS):
+        for part in range(3):
+            at = (part * PAIRS + pair) * PAIR
+            qkv_ref[:, at : at + PAIR] = piece(pair % 2, pair // 2, part * width + i * PAIR)
+    for two in range(PAIRS // 2):
+
+        @pl.when(i // 2 == two)
+        def _(two=two):
+            for j in range(width // PAIR):
+                o_ref[:, j * PAIR : (j + 1) * PAIR] = piece(i % 2, two, 3 * width + j * PAIR)
+
+    folded = jnp.zeros((PAIR, LANES), F32)
+    for at in range(0, qkv_ref.shape[1], LANES):
+        folded += qkv_ref[:, at : at + LANES] * w_ref[:, at : at + LANES].astype(F32)
+    gain = jnp.sum(folded.T, axis=0, keepdims=True) / ga_ref[...]
+    gain_ref[pl.ds(pl.multiple_of(i * PAIR, PAIR), PAIR)] = gain[0]
+
+    @pl.when(i == 0)
+    def _():
+        for t in range(count):
+            part = slice(2 * rows, 2 * rows + extra)
+            small_s[t * extra : (t + 1) * extra, :] = held[0, t, part, :].astype(F32)
+        rdim = router_ref.shape[0]
+        for j in range(width // LANES):
+            lanes = slice(j * LANES, (j + 1) * LANES)
+            gain_ffn_ref[lanes] = small_s[j, :]
+            at = 8 + j * rdim
+            router_ref[:, lanes] = small_s[at : at + rdim, :]
+        at = 8 + width // LANES * rdim
+        embed_ref[...] = small_s[at : at + experts, :rdim]
+
+
+def shared_sums(me, blocks, rows, extra, w_qkv, ga, experts, rdim):
+    width = w_qkv.shape[0]
+    count = len(blocks) // 2
+    lanes = pl.BlockSpec((1, PAIR), lambda i: (0, i))
+    return pl.pallas_call(
+        functools.partial(shared_sums_kernel, count, experts, rows, extra),
+        grid=(width // PAIR,),
+        in_specs=[smem(), pl.BlockSpec((PAIR, 3 * width), lambda i: (i, 0)), lanes]
+        + [pl.BlockSpec(memory_space=pl.ANY)] * (2 * count),
         out_specs=[
-            pl.BlockSpec((width, PAIR), lambda pair, part: (0, part * PAIRS + pair)),
-            pl.BlockSpec((PAIR, width), lambda pair, part: (pair, 0)),
-            whole((chips * extra, PAIR)),
+            pl.BlockSpec((PAIR, 3 * width), lambda i: (i, 0)),
+            pl.BlockSpec((PAIR, width), lambda i: (i, 0)),
+            pl.BlockSpec((width,), lambda i: (0,)),
+            pl.BlockSpec((width,), lambda i: (0,)),
+            whole((rdim, width)),
+            whole((experts, rdim)),
         ],
         out_shape=[
             jax.ShapeDtypeStruct((width, 3 * width), F32),
             jax.ShapeDtypeStruct((width, width), F32),
-            jax.ShapeDtypeStruct((chips * extra, PAIR), F32),
-        ],
-        compiler_params=params(32),
-        cost_estimate=cost(8),
+            jax.ShapeDtypeStruct((width,), F32),
+            jax.ShapeDtypeStruct((width,), F32),
+            jax.ShapeDtypeStruct((rdim, width), F32),
+            jax.ShapeDtypeStruct((experts, rdim), F32),
+        ],
+        scratch_shapes=[
+            pltpu.VMEM((2, count, *blocks[0].shape), BF16),
+            pltpu.VMEM((count * extra, LANES), F32),
+            pltpu.SemaphoreType.DMA((2 * count,)),
+        ],
+        compiler_params=params(),
+        cost_estimate=cost(2),
         name="shared_sums",
-    )(me, mine, other, mine, other)
+    )(me, w_qkv, ga, *blocks)
 
 
 def exchange(rows):
@@ -805,19 +872,8 @@
     )
 
 
-def finish_sums(shares):
-    peers = lax.axis_size("expert")
-    groups = lax.axis_size("dp")
-    joined = jnp.concatenate(shares, axis=0)
-    blocks = joined.reshape(groups, joined.shape[0] // groups, -1)
-    total = sum_blocks(lax.all_to_all(blocks, "dp", 0, 0, tiled=True))
-    total = lax.all_gather(total, "dp", axis=0, tiled=True)
-    pieces = [total] + [
-        lax.ppermute(total, "expert", [(j, j ^ (2 * d)) for j in range(peers)])
-        for d in range(1, peers // 2)
-    ]
-    mine = jnp.stack(pieces)
-    return mine, swap_cores(mine)
+def xor_permute(value, axis, d):
+    return lax.ppermute(value, axis, [(j, j ^ d) for j in range(lax.axis_size(axis))])
 
 
 def on_device(
@@ -839,7 +895,7 @@
     peers = lax.axis_size("expert")
     shards = lax.axis_size("dp")
     chips = peers // 2
-    wide = w_in.shape[2] // shards
+    share = w_in.shape[2] // shards
     me = lax.axis_index("expert").astype(I32).reshape(1)
     core = me & 1
     ga, gf = gain_attn.reshape(1, width), gain_ffn.reshape(1, width)
@@ -847,70 +903,74 @@
     wrt = w_router.T
     hold = lax.optimization_barrier
 
-    keyr, g_slots = place(routes.reshape(1, toks), cotangent, peers, 2 * toks)
+    keyr, keyn, g_slots = place(routes.reshape(1, toks), cotangent, peers, 2 * toks)
     g_rows = exchange(g_slots).reshape(peers, 2, toks // peers, width)
     q, k, v, lse, mixt, attn_in, res, xa_slots, xb_slots = attend(
         tokens, segr, keyr, w_qkv, w_attn_out, ga, gf
     )
     x_a = exchange(xa_slots)
-    gact_a, gt_a = grad_act(g_rows, 0, w_out, wide)
-    gact_b, gt_b = grad_act(g_rows, 1, w_out, wide)
-    x_a, xb_slots, gact_b, gt_b = hold((x_a, xb_slots, gact_b, gt_b))
+    gact_a, gt_a = grad_act(g_rows, 0, w_out, share)
+    gact_b, gt_b = grad_act(g_rows, 1, w_out, share)
+    x_a, xb_slots, gact_b, gt_b, attn_in = hold((x_a, xb_slots, gact_b, gt_b, attn_in))
     x_b = exchange(xb_slots)
-    act_a, gp_a, xt_a, gout_a, gwr_a, gemb_a = expert(me, wrt, embed, x_a, w_in, gact_a, wide)
+    act_a, gp_a, xt_a, gout_a, gwr_a, gemb_a = expert(me, wrt, embed, x_a, w_in, gact_a, share)
     gback_a = exchange(gout_a)
-    gw, act_b, gout_b, gwr_b, gemb_b = expert(
-        me, wrt, embed, x_b, w_in, gact_b, wide, (act_a, gp_a, xt_a, gt_a, gt_b)
-    )
-    expert_total = lax.psum_scatter(gw, "dp", scatter_dimension=0, tiled=True)[0]
+    act_b, gp_b, xt_b, gout_b, gwr_b, gemb_b = expert(me, wrt, embed, x_b, w_in, gact_b, share)
     gout_b, gback_a = hold((gout_b, gback_a))
     gback_b = exchange(gout_b)
+    gw_one = expert_grads((gt_a, gt_b), (act_a, act_b), share)
+    total_one = lax.psum_scatter(gw_one, "dp", scatter_dimension=0, tiled=True)[0]
+    gw_one, late_gp = hold((gw_one, gp_b))
+    gw_two = expert_grads((xt_a, xt_b), (gp_a, late_gp), share)
+    total_two = lax.psum_scatter(gw_two, "dp", scatter_dimension=0, tiled=True)[0]
     attnt = attn_in.T
-    fout_a, fout_b = expert_out_of(act_a, act_b, w_out, wide)
-    gback_b, fout_a, fout_b, attnt = hold((gback_b, fout_a, fout_b, attnt))
+    gback_b, gw_two, attnt = hold((gback_b, gw_two, attnt))
     gres, gb, ggf = combine_back(keyr, res, cotangent, gf, (gback_a, gback_b))
 
-    gatt = jnp.zeros((toks, width), F32)
-    fback, both, shares = [], [], []
+    small = jnp.concatenate(
+        [
+            jnp.pad(ggf.reshape(-1, LANES), ((0, 8 - width // LANES), (0, 0))),
+            *jnp.split(gwr_a + gwr_b, width // LANES, axis=1),
+            jnp.pad(gemb_a + gemb_b, ((0, 0), (0, LANES - rdim))),
+        ],
+        axis=0,
+    )
+    rows = 4 * width // chips
+    extra = -(-small.shape[0] // (16 * chips)) * 16
+    small = jnp.pad(small, ((0, chips * extra - small.shape[0]), (0, 0)))
+    small = (small + swap_cores(small)).astype(BF16).reshape(chips, extra, LANES)
+    both, grads = [], []
     for turn in range(PAIRS // 2):
-        final = (tokens, gres, ga) if turn + 1 == PAIRS // 2 else ()
-        send, keep, gatt, *gga = attend_back(
-            2 * turn, core, segr, q, k, v, lse, mixt, gb, attnt, w_attn_out, w_qkv, gatt, final
+        send, keep, grad = attend_back(
+            2 * turn, core, segr, q, k, v, lse, mixt, gb, attnt, w_attn_out
         )
+        grads.append(grad)
         got = swap_cores(send)
         both.append((keep.astype(F32) + got.astype(F32)).astype(BF16).reshape(chips, -1, PAIR))
         if turn == 0:
-            fback.append(exchange(fout_a))
-            gatt, fout_b, *fback = hold((gatt, fout_b, *fback))
-        elif not final:
-            fback.append(exchange(fout_b))
-            gatt, both, fback = hold((gatt, both, fback))
-            shares.append(sum_over_chips(jnp.concatenate(both, axis=1)))
-            both = []
-    grad_tokens = gatt
-    gemb = (gemb_a + gemb_b).reshape(-1)
-    small = jnp.concatenate(
-        [
-            gga[0].reshape(-1, LANES),
-            ggf.reshape(-1, LANES),
-            (gwr_a + gwr_b).reshape(-1, LANES),
-            jnp.pad(gemb, (0, -experts * rdim % LANES)).reshape(-1, LANES),
-        ],
-        axis=0,
+            (gb, grad) = hold((gb, grad))
+        elif turn == 1:
+            gb, both, small, grad = hold((gb, both, small, grad))
+            share_one = sum_over_chips(jnp.concatenate([*both, small], axis=1))
+    last, late_act = hold((both[-1], act_b))
+    share_two = sum_over_chips(last)
+    fout = expert_out_of(act_a, late_act, w_out, share, peers)
+    share_two, share_one, fout, total_one = hold((share_two, share_one, fout, total_one))
+    blocks = jnp.concatenate([share_one, share_two], axis=0).reshape(shards, -1, LANES)
+    blocks = lax.all_to_all(blocks, "dp", 0, 0, tiled=True)
+    blocks, fout = hold((blocks, fout))
+    fback = exchange(fout.reshape(2 * toks, width))
+    total = lax.all_gather(sum_blocks(blocks), "dp", axis=0, tiled=True)
+    pieces = [total] + [xor_permute(total, "expert", d) for d in range(2, peers, 2)]
+    grad_tokens = grad_tokens_of(tokens, gres, ga, w_qkv, grads)
+    out_tokens = combine(keyn, res, fback)
+    pieces, grad_tokens, out_tokens = hold((pieces, grad_tokens, out_tokens))
+    blocks = pieces + [swap_cores(piece) for piece in pieces]
+    grad_w_qkv, grad_w_attn_out, grad_gain_attn, grad_gain_ffn, grad_router, grad_embed = (
+        shared_sums(me, blocks, rows, extra, w_qkv, ga, experts, rdim)
     )
-    small = jnp.pad(small, ((0, -small.shape[0] % (16 * chips)), (0, 0))).astype(BF16)
-    small = small.reshape(chips, -1, LANES)
-    shares.append(sum_over_chips(jnp.concatenate([*both, small], axis=1)))
-    mine, others = finish_sums(shares)
-    grad_w_qkv, grad_w_attn_out, small = shared_sums(me, mine, others, width)
-    small = small.reshape(-1)
-    grad_gain_attn = small[:width]
-    grad_gain_ffn = small[width : 2 * width]
-    grad_router = small[2 * width : (2 + rdim) * width].reshape(rdim, width).T
-    at = (2 + rdim) * width
-    grad_embed = small[at : at + experts * rdim].reshape(experts, rdim)
-    out_tokens = combine(keyr, res, fback)
-    grad_w_in, grad_w_out = expert_sums(expert_total)
+    grad_w_qkv, total_two = hold((grad_w_qkv, total_two))
+    grad_w_in, grad_w_out = expert_sums(total_two, total_one)
     return (
         out_tokens,
         grad_tokens,
@@ -918,7 +978,7 @@
         grad_w_attn_out,
         grad_gain_attn,
         grad_gain_ffn,
-        grad_router,
+        grad_router.T,
         grad_embed,
         grad_w_in,
         grad_w_out,

time: 427 us -> 417 us (0.977)
  local copies, waits for them, and re-layouts: 31.3 us -> 7.67 us
  blocking collectives: 39.3 us -> 62.5 us
  Pallas kernels: 236 us -> 253 us
  waiting for transfers between devices: 41.5 us -> 27.7 us
  other arithmetic: 15.6 us -> 5.84 us
    unnamed x58 -> x47, local copies, waits for them, and re-layouts: 24.6 us -> 4.83 us
    all_to_all x1, blocking collectives: 22.9 us -> 37.8 us  [on_device(): blocks = lax.all_to_all(blocks, 'dp', 0, 0, tiled=True)]
    all_to_all x2, waiting for transfers between devices: 10.2 us -> 0.01 us  [sum_over_chips(): lax.all_to_all(blocks, 'expert', 0, 0, axis_index_groups=core_groups(), t...]
    all_gather x1, blocking collectives: 16.5 us -> 24.6 us  [on_device(): total = lax.all_gather(sum_blocks(blocks), 'dp', axis=0, tiled=True)]
    ppermute x4 -> x8, waiting for transfers between devices: 1.58 us -> 8.36 us  [swap_cores(): return lax.ppermute(value, 'expert', [(j, j ^ 1) for j in range(peers)])]
    ppermute x3, waiting for transfers between devices: 23 us -> 17.3 us  [xor_permute(): lax.ppermute(value, axis, [(j, j ^ d) for j in range(lax.axis_size(axis))])]
    all_to_all x7 -> x6, waiting for transfers between devices: 6.7 us -> 1.9 us  [exchange(): lax.all_to_all(rows.reshape(peers, -1, width), 'expert', split_axis=0, co...]
    pallas_call x7 -> x10, Pallas kernels: 145 us -> 149 us  [the longest x2 47.8 us: expert(): pl.pallas_call(expert_kernel, grid=(hidden // wide,), in_specs=[smem(), w...]
  transfers between devices with their start and end apart: 17 -> 21, of which waited for: 6 -> 8; matrix products, arithmetic and copies ran while one was open for 5% -> 2% of each run, Pallas kernels for 54% -> 58%
where the time goes in v3:
time: 417 us; the launch traced here: 413 us
  Pallas kernels  253 us (61%)
  blocking collectives  62.5 us (15%)
  starting transfers between devices  41.7 us (10%)
  waiting for transfers between devices  27.7 us (7%)
  between operations  14.6 us (4%)
  local copies, waits for them, and re-layouts  7.67 us (2%)
  other arithmetic  5.84 us (1%)
    pallas_call x2, Pallas kernels, expert(): pl.pallas_call(expert_kernel, grid=(hidden // wide,), in_specs=[smem(), w...  47.8 us
    pallas_call x3, Pallas kernels, attend_back(): pl.pallas_call(attend_back_kernel, grid_spec=pltpu.PrefetchScalarGridSpec...  46.5 us
    pallas_call x1, Pallas kernels, attend(): pl.pallas_call(attend_kernel, grid=(PAIRS,), in_specs=[whole((toks, width...  44.4 us
    all_to_all x1, blocking collectives, on_device(): blocks = lax.all_to_all(blocks, 'dp', 0, 0, tiled=True)  37.8 us
    pallas_call x2, Pallas kernels, expert_grads(): pl.pallas_call(expert_grads_kernel, grid=(steps,), in_specs=[whole((width...  29.6 us
    all_to_all x6, starting transfers between devices, exchange(): lax.all_to_all(rows.reshape(peers, -1, width), 'expert', split_axis=0, co...  27.2 us
    all_gather x1, blocking collectives, on_device(): total = lax.all_gather(sum_blocks(blocks), 'dp', axis=0, tiled=True)  24.6 us
    pallas_call x2, Pallas kernels, grad_act(): pl.pallas_call(grad_act_kernel, grid=(hidden // wide,), in_specs=[pl.Bloc...  20.1 us
  transfers between devices with their start and end apart: 21, of which 8 were waited for; matrix products, arithmetic and copies ran while one was open for 2% of the time, Pallas kernels for 58%

profile of v3, /device:TPU:0, one launch (start us, length us, event | category | flops | bytes accessed | tf_op | source)
XLA Modules:
  0.0 412.9 jit_solution(18342369323246581704)
XLA Ops:
  7.2 6.9 %place.1 = (s32[1,1024]{1,0:T(1,128)}, s32[1,1024]{1,0:T(1,128)}, bf16[2048,768]{1,0:T(8,128)(2,1)}) custom-call(s32[1,1024]{1,0:T(1,128)} %bitcast.39, bf16[1024,768]{1,0:T(8,128)(2,1)} %cot_ref.3), custom_call_target="tpu_custom_call" | custom-call | flops 5750000128 | tf_op jit(solution)/shard_map/place/pallas_call | solution.py:98
  14.0 5.7 %all-to-all-start.1 = ((bf16[8,256,768]{2,1,0:T(8,128)(2,1)}), bf16[8,256,768]{2,1,0:T(8,128)(2,1)}, u32[]{:S(2)}, u32[]{:S(2)}) async-start(bf16[8,256,768]{2,1,0:T(8,128)(2,1)} %bitcast.25), calls=%async_computation.1 | async-start | bytes 6291456 | tf_op jit(solution)/shard_map/all_to_all | solution.py:850
  20.9 44.4 %attend.1 = (bf16[1024,768]{1,0:T(8,128)(2,1)}, bf16[1024,768]{1,0:T(8,128)(2,1)}, bf16[1024,768]{1,0:T(8,128)(2,1)}, f32[6,2,1024]{2,1,0:T(2,128)}, bf16[768,10...) custom-call(bf16[1024,768]{1,0:T(8,128)(2,1)} %tok_ref.3, ...), custom_call_target="tpu_custom_call" | custom-call | flops 48299999232 | tf_op jit(solution)/shard_map/attend/pallas_call | solution.py:205
  65.3 4.9 %all-to-all-start = ((bf16[8,128,768]{2,1,0:T(8,128)(2,1)}), bf16[8,128,768]{2,1,0:T(8,128)(2,1)S(1)}, u32[]{:S(2)}, u32[]{:S(2)}) async-start(bf16[8,128,768]{2,1,0:T(8,128)(2,1)} %bitcast.32), calls=%async_computation | async-start | bytes 3145728 | tf_op jit(solution)/shard_map/all_to_all | solution.py:850
  70.2 10.2 %grad_act.2 = (bf16[1024,3072]{1,0:T(8,128)(2,1)}, bf16[768,1024]{1,0:T(8,128)(2,1)}) custom-call(bf16[8,2,128,768]{3,2,1,0:T(8,128)(2,1)} %bitcast.6.g_ref, bf16[1,3072,768]{2,1,0:T(8,128)(2,1)} %wout_ref.5), custom_call_target="tpu_custom_call" | custom-call | flops 8049999872 | tf_op jit(solution)/shard_map/grad_act/pallas_call | solution.py:592
  80.4 9.9 %grad_act.3 = (bf16[1024,3072]{1,0:T(8,128)(2,1)}, bf16[768,1024]{1,0:T(8,128)(2,1)}) custom-call(bf16[8,2,128,768]{3,2,1,0:T(8,128)(2,1)} %bitcast.6.g_ref, bf16[1,3072,768]{2,1,0:T(8,128)(2,1)} %wout_ref.5), custom_call_target="tpu_custom_call" | custom-call | flops 8049999872 | tf_op jit(solution)/shard_map/grad_act/pallas_call | solution.py:592
  95.9 23.9 %expert.3 = (bf16[1024,3072]{1,0:T(8,128)(2,1)}, bf16[1024,3072]{1,0:T(8,128)(2,1)}, bf16[768,1024]{1,0:T(8,128)(2,1)}, bf16[1024,768]{1,0:T(8,128)(2,1)}, f32[16,768]{1,0:T(8,128)}, /*index=5*/f32[8,16]{1,0:T(8,128)}) custom-call(s32[1]{0:T(128)} %bitcast.me_ref, bf16[16,768]{1,0:T(8,128)(2,1)} %bitcast.37, f32[8,16]{1,0:T(8,128)} %emb_ref.3, ...), custom_call_target="tpu_custom_call" | custom-call | flops 26449999872 | tf_op jit(solution)/shard_map/expert/pallas_call | solution.py:511
  125.3 24.0 %expert.2 = (bf16[1024,3072]{1,0:T(8,128)(2,1)}, bf16[1024,3072]{1,0:T(8,128)(2,1)}, bf16[768,1024]{1,0:T(8,128)(2,1)}, bf16[1024,768]{1,0:T(8,128)(2,1)}, f32[16,768]{1,0:T(8,128)}, /*index=5*/f32[8,16]{1,0:T(8,128)}) custom-call(s32[1]{0:T(128)} %bitcast.me_ref, bf16[16,768]{1,0:T(8,128)(2,1)} %bitcast.38, f32[8,16]{1,0:T(8,128)} %emb_ref.3, ...), custom_call_target="tpu_custom_call" | custom-call | flops 26449999872 | tf_op jit(solution)/shard_map/expert/pallas_call | solution.py:511
  156.4 14.6 %expert_grads.2 = bf16[4,768,768]{2,1,0:T(8,128)(2,1)} custom-call(bf16[768,1024]{1,0:T(8,128)(2,1)} %get-tuple-element.113.lefta_ref, bf16[768,1024]{1,0:T(8,128)(2,1)} %get-tuple-element.114.leftb_ref, bf16[1024,3072]{1,0:T(8,128)(2,1)} %get-tuple-element.115.righta_ref.acta_ref, bf16[1024,3072]{1,0:T(8,128)(2,1)} %get-tuple-element.142.rightb_ref.actb_ref), custom_call_target="tpu_custom_call" | custom-call | flops 5750000128 | tf_op jit(solution)/shard_map/expert_grads/pallas_call | solution.py:565
  171.9 15.1 %expert_grads.3 = bf16[4,768,768]{2,1,0:T(8,128)(2,1)} custom-call(bf16[768,1024]{1,0:T(8,128)(2,1)} %get-tuple-element.110.lefta_ref, bf16[768,1024]{1,0:T(8,128)(2,1)} %get-tuple-element.111.leftb_ref, bf16[1024,3072]{1,0:T(8,128)(2,1)} %get-tuple-element.112.righta_ref, bf16[1024,3072]{1,0:T(8,128)(2,1)} %get-tuple-element.118.rightb_ref), custom_call_target="tpu_custom_call" | custom-call | flops 5750000128 | tf_op jit(solution)/shard_map/expert_grads/pallas_call | solution.py:565
  186.9 10.0 %combine_back.1 = (f32[1024,768]{1,0:T(8,128)}, bf16[1024,768]{1,0:T(8,128)(2,1)}, f32[1,768]{1,0:T(1,128)}) custom-call(s32[1,1024]{1,0:T(1,128)} %get-tuple-element.89.keyr_ref, f32[1024,768]{1,0:T(8,128)} %get-tuple-element.95.res_ref, bf16[1024,768]{1,0:T(8,128)(2,1)} %cot_ref.3, f32[1,768]{1,0:T(1,128)} %reshape.74.gf_ref, bf16[1024,768]{1,0:T(8,128)(2,1)} %bitcast.27, ...), custom_call_target="tpu_custom_call" | custom-call | flops 115000000512 | tf_op jit(solution)/shard_map/combine_back/pallas_call | solution.py:704
  197.0 15.4 %attend_back.3 = (bf16[4,768,128]{2,1,0:T(8,128)(2,1)}, bf16[4,768,128]{2,1,0:T(8,128)(2,1)}, bf16[3,1024,256]{2,1,0:T(8,128)(2,1)}) custom-call(s32[1]{0:T(128)S(6)} %and.4.core_ref, s32[1,1024]{1,0:T(1,128)} %segr_ref.7, bf16[1024,768]{1,0:T(8,128)(2,1)} %get-tuple-element.90.q_ref, bf16[1024,768]{1,0:T(8,128)(2,1)} %get-tuple-element.91.k_ref, ...), custom_call_target="tpu_custom_call" | custom-call | flops 2300000000 | tf_op jit(solution)/shard_map/attend_back/pallas_call | solution.py:342
  212.4 15.8 %attend_back.4 = (bf16[4,768,128]{2,1,0:T(8,128)(2,1)}, bf16[4,768,128]{2,1,0:T(8,128)(2,1)}, bf16[3,1024,256]{2,1,0:T(8,128)(2,1)}) custom-call(s32[1]{0:T(128)S(6)} %and.4.core_ref, s32[1,1024]{1,0:T(1,128)} %segr_ref.7, bf16[1024,768]{1,0:T(8,128)(2,1)} %get-tuple-element.90.q_ref, bf16[1024,768]{1,0:T(8,128)(2,1)} %get-tuple-element.91.k_ref, ...), custom_call_target="tpu_custom_call" | custom-call | flops 2300000000 | tf_op jit(solution)/shard_map/attend_back/pallas_call | solution.py:342
  237.6 15.4 %attend_back.5 = (bf16[4,768,128]{2,1,0:T(8,128)(2,1)}, bf16[4,768,128]{2,1,0:T(8,128)(2,1)}, bf16[3,1024,256]{2,1,0:T(8,128)(2,1)}) custom-call(s32[1]{0:T(128)S(6)} %and.4.core_ref, s32[1,1024]{1,0:T(1,128)} %segr_ref.7, bf16[1024,768]{1,0:T(8,128)(2,1)} %get-tuple-element.90.q_ref, bf16[1024,768]{1,0:T(8,128)(2,1)} %get-tuple-element.91.k_ref, ...), custom_call_target="tpu_custom_call" | custom-call | flops 11500000256 | tf_op jit(solution)/shard_map/attend_back/pallas_call | solution.py:342
  257.8 4.4 %all-to-all-start.5 = ((bf16[4,768,128]{2,1,0:T(8,128)(2,1)}), bf16[4,768,128]{2,1,0:T(8,128)(2,1)}, u32[]{:S(2)}, u32[]{:S(2)}) async-start(bf16[4,768,128]{2,1,0:T(8,128)(2,1)} %add_convert_fusion), calls=%async_computation.5 | async-start | bytes 1572864 | tf_op jit(solution)/shard_map/all_to_all | solution.py:871
  262.2 15.2 %expert_out.1 = bf16[8,2,128,768]{3,2,1,0:T(8,128)(2,1)} custom-call(bf16[1024,3072]{1,0:T(8,128)(2,1)} %get-tuple-element.115.righta_ref.acta_ref, bf16[1024,3072]{1,0:T(8,128)(2,1)} %get-tuple-element.142.rightb_ref.actb_ref, bf16[1,3072,768]{2,1,0:T(8,128)(2,1)} %wout_ref.5), custom_call_target="tpu_custom_call" | custom-call | flops 16099999744 | tf_op jit(solution)/shard_map/expert_out/pallas_call | solution.py:635
  279.2 37.8 %all_to_all.45 = bf16[4,584,128]{2,1,0:T(8,128)(2,1)S(1)} all-to-all(bf16[4,584,128]{2,1,0:T(8,128)(2,1)S(1)} %bitcast.26), channel_id=1, replica_groups=mesh['dp'=4,'expert'=8] {'dp'}, dimensions={0} | all-to-all | bytes 1196032 | tf_op jit(solution)/shard_map/all_to_all | solution.py:960
  317.1 4.4 %all-to-all-start.8 = ((bf16[8,256,768]{2,1,0:T(8,128)(2,1)}), bf16[8,256,768]{2,1,0:T(8,128)(2,1)}, u32[]{:S(2)}, u32[]{:S(2)}) async-start(bf16[8,256,768]{2,1,0:T(8,128)(2,1)} %bitcast.17), calls=%async_computation.9 | async-start | bytes 6291456 | tf_op jit(solution)/shard_map/all_to_all | solution.py:850
  321.6 24.6 %all_gather.3.rest_0_ = bf16[2336,128]{1,0:T(8,128)(2,1)S(1)} all-gather(bf16[584,128]{1,0:T(8,128)(2,1)S(1)} %reduce_sum.38), channel_id=1, replica_groups=mesh['dp'=4,'expert'=8] {'dp'}, dimensions={0}, use_global_device_ids=true | all-gather | bytes 747520 | tf_op jit(solution)/shard_map/all_gather | solution.py:963
  349.7 9.2 %grad_tokens.1 = f32[1024,768]{1,0:T(8,128)} custom-call(bf16[1024,768]{1,0:T(8,128)(2,1)} %tok_ref.3, f32[1024,768]{1,0:T(8,128)} %get-tuple-element.147.gres_ref, f32[1,768]{1,0:T(1,128)} %reshape.73.ga_ref, bf16[768,2304]{1,0:T(8,128)(2,1)} %w_ref.3, bf16[3,1024,256]{2,1,0:T(8,128)(2,1)} %get-tuple-element.123.rest_0_, ...), custom_call_target="tpu_custom_call" | custom-call | flops 10350000128 | tf_op jit(solution)/shard_map/grad_tokens/pallas_call | solution.py:390
  359.9 7.8 %combine.1 = bf16[1024,768]{1,0:T(8,128)(2,1)} custom-call(s32[1,1024]{1,0:T(1,128)} %get-tuple-element.149.keyn_ref, f32[1024,768]{1,0:T(8,128)} %get-tuple-element.95.res_ref, bf16[2048,768]{1,0:T(8,128)(2,1)} %bitcast.18.rows_ref), custom_call_target="tpu_custom_call" | custom-call | flops 5750000128 | tf_op jit(solution)/shard_map/combine/pallas_call | solution.py:733
  371.7 13.4 %collective-permute-done.6.rest_3_ = bf16[2336,128]{1,0:T(8,128)(2,1)} collective-permute-done((bf16[2336,128]{1,0:T(8,128)(2,1)S(1)}, bf16[2336,128]{1,0:T(8,128)(2,1)}, u32[]{:S(2)}, u32[]{:S(2)}) %collective-permute-start.6) | collective-permute-done | bytes 598048 | tf_op jit(solution)/shard_map/ppermute | solution.py:876
  390.5 9.6 %shared_sums.1 = (f32[768,2304]{1,0:T(8,128)}, f32[768,768]{1,0:T(8,128)}, f32[768]{0:T(1024)}, f32[768]{0:T(1024)}, f32[16,768]{1,0:T(8,128)}, /*index=5*/f32[8,16]{1,0:T(8,128)}) custom-call(s32[1]{0:T(128)} %bitcast.me_ref, bf16[768,2304]{1,0:T(8,128)(2,1)} %w_ref.3, f32[1,768]{1,0:T(1,128)} %reshape.73.ga_ref, bf16[2336,128]{1,0:T(8,128)(2,1)} %copy-done.6, ...), custom_call_target="tpu_custom_call" | custom-call | flops 2300000000 | tf_op jit(solution)/shard_map/shared_sums/pallas_call | solution.py:815
  400.2 5.7 %expert_sums.1 = (f32[1,768,768]{2,1,0:T(8,128)}, f32[1,768,768]{2,1,0:T(8,128)}) custom-call(bf16[768,768]{1,0:T(8,128)(2,1)} %bitcast.36, bf16[768,768]{1,0:T(8,128)(2,1)} %bitcast.35), custom_call_target="tpu_custom_call" | custom-call | flops 3449999872 | tf_op jit(solution)/shard_map/expert_sums/pallas_call | solution.py:656
  (103 shorter events, 50.1 us)
Async XLA Ops:
  14.0 51.3 %all-to-all-start.1 = ((bf16[8,256,768]{2,1,0:T(8,128)(2,1)}), bf16[8,256,768]{2,1,0:T(8,128)(2,1)}, u32[]{:S(2)}, u32[]{:S(2)}) async-start(bf16[8,256,768]{2,1,0:T(8,128)(2,1)} %bitcast.25), calls=%async_computation.1 | async-start | bytes 6291456 | tf_op jit(solution)/shard_map/all_to_all | solution.py:850
  65.3 25.9 %all-to-all-start = ((bf16[8,128,768]{2,1,0:T(8,128)(2,1)}), bf16[8,128,768]{2,1,0:T(8,128)(2,1)S(1)}, u32[]{:S(2)}, u32[]{:S(2)}) async-start(bf16[8,128,768]{2,1,0:T(8,128)(2,1)} %bitcast.32), calls=%async_computation | async-start | bytes 3145728 | tf_op jit(solution)/shard_map/all_to_all | solution.py:850
  92.3 27.5 %all-to-all-start.2 = ((bf16[8,128,768]{2,1,0:T(8,128)(2,1)}), bf16[8,128,768]{2,1,0:T(8,128)(2,1)S(1)}, u32[]{:S(2)}, u32[]{:S(2)}) async-start(bf16[8,128,768]{2,1,0:T(8,128)(2,1)} %bitcast.7), calls=%async_computation.2 | async-start | bytes 3145728 | tf_op jit(solution)/shard_map/all_to_all | solution.py:850
  121.0 28.3 %all-to-all-start.3 = ((bf16[8,128,768]{2,1,0:T(8,128)(2,1)}), bf16[8,128,768]{2,1,0:T(8,128)(2,1)S(1)}, u32[]{:S(2)}, u32[]{:S(2)}) async-start(bf16[8,128,768]{2,1,0:T(8,128)(2,1)} %bitcast.31), calls=%async_computation.3 | async-start | bytes 3145728 | tf_op jit(solution)/shard_map/all_to_all | solution.py:850
  150.4 36.5 %all-to-all-start.4 = ((bf16[8,128,768]{2,1,0:T(8,128)(2,1)}), bf16[8,128,768]{2,1,0:T(8,128)(2,1)}, u32[]{:S(2)}, u32[]{:S(2)}) async-start(bf16[8,128,768]{2,1,0:T(8,128)(2,1)} %bitcast.28), calls=%async_computation.4 | async-start | bytes 3145728 | tf_op jit(solution)/shard_map/all_to_all | solution.py:850
  154.7 124.4 %reduce-scatter.3.cloned.1.call-start = ((), (), s32[]{:S(2)}) async-start(), calls=%async_computation.11 | async-start | bytes 5898240 | tf_op jit(solution)/shard_map/reduce_scatter | solution.py:922
  171.1 229.1 %reduce-scatter.5.cloned.1.call-start = ((), (), s32[]{:S(2)}) async-start(), calls=%async_computation.12 | async-start | bytes 5898240 | tf_op jit(solution)/shard_map/reduce_scatter | solution.py:925
  228.1 3.8 collective-permute-start.1
  228.8 3.4 collective-permute-start
  229.0 2.9 collective-permute-start.2
  233.7 24.1 %all-to-all-start.6 = ((bf16[4,1568,128]{2,1,0:T(8,128)(2,1)}), bf16[4,1568,128]{2,1,0:T(8,128)(2,1)S(1)}, u32[]{:S(2)}, u32[]{:S(2)}) async-start(bf16[4,1568,128]{2,1,0:T(8,128)(2,1)} %pad_maximum_fusion), calls=%async_computation.6 | async-start | bytes 3211264 | tf_op jit(solution)/shard_map/all_to_all | solution.py:871
  253.0 2.5 collective-permute-start.3
  257.8 20.1 %all-to-all-start.5 = ((bf16[4,768,128]{2,1,0:T(8,128)(2,1)}), bf16[4,768,128]{2,1,0:T(8,128)(2,1)}, u32[]{:S(2)}, u32[]{:S(2)}) async-start(bf16[4,768,128]{2,1,0:T(8,128)(2,1)} %add_convert_fusion), calls=%async_computation.5 | async-start | bytes 1572864 | tf_op jit(solution)/shard_map/all_to_all | solution.py:871
  317.1 42.9 %all-to-all-start.8 = ((bf16[8,256,768]{2,1,0:T(8,128)(2,1)}), bf16[8,256,768]{2,1,0:T(8,128)(2,1)}, u32[]{:S(2)}, u32[]{:S(2)}) async-start(bf16[8,256,768]{2,1,0:T(8,128)(2,1)} %bitcast.17), calls=%async_computation.9 | async-start | bytes 6291456 | tf_op jit(solution)/shard_map/all_to_all | solution.py:850
  346.3 38.8 %copy-start.6 = (bf16[2336,128]{1,0:T(8,128)(2,1)}, bf16[2336,128]{1,0:T(8,128)(2,1)S(1)}, u32[]{:S(2)}) copy-start(bf16[2336,128]{1,0:T(8,128)(2,1)S(1)} %all_gather.3.rest_0_) | copy-start | bytes 1794052
  346.3 25.5 %collective-permute-start.4 = (bf16[2336,128]{1,0:T(8,128)(2,1)S(1)}, bf16[2336,128]{1,0:T(8,128)(2,1)S(1)}, u32[]{:S(2)}, u32[]{:S(2)}) collective-permute-start(bf16[2336,128]{1,0:T(8,128)(2,1)S(1)} %all_gather.3.rest_0_), channel_id=1, source_target_pairs={{0,2},{1,3},{2,0},{3,1},{4,6},{5,7},{6,4},{7,5},{8,10},{9,11},{10,... | collective-permute-start | bytes 1794056 | tf_op jit(solution)/shard_map/ppermute | solution.py:876
  348.1 23.6 %collective-permute-start.5 = (bf16[2336,128]{1,0:T(8,128)(2,1)S(1)}, bf16[2336,128]{1,0:T(8,128)(2,1)S(1)}, u32[]{:S(2)}, u32[]{:S(2)}) collective-permute-start(bf16[2336,128]{1,0:T(8,128)(2,1)S(1)} %all_gather.3.rest_0_), channel_id=1, source_target_pairs={{0,4},{1,5},{2,6},{3,7},{4,0},{5,1},{6,2},{7,3},{8,12},{9,13},{10,... | collective-permute-start | bytes 1794056 | tf_op jit(solution)/shard_map/ppermute | solution.py:876
  349.6 35.5 %collective-permute-start.6 = (bf16[2336,128]{1,0:T(8,128)(2,1)S(1)}, bf16[2336,128]{1,0:T(8,128)(2,1)}, u32[]{:S(2)}, u32[]{:S(2)}) collective-permute-start(bf16[2336,128]{1,0:T(8,128)(2,1)S(1)} %all_gather.3.rest_0_), channel_id=1, source_target_pairs={{0,6},{1,7},{2,4},{3,5},{4,2},{5,3},{6,0},{7,1},{8,14},{9,15},{10,... | collective-permute-start | bytes 1794056 | tf_op jit(solution)/shard_map/ppermute | solution.py:876
  371.7 18.8 %copy-start.15 = (bf16[2336,128]{1,0:T(8,128)(2,1)}, bf16[2336,128]{1,0:T(8,128)(2,1)S(1)}, u32[]{:S(2)}) copy-start(bf16[2336,128]{1,0:T(8,128)(2,1)S(1)} %collective-permute-done.4.rest_1_) | copy-start | bytes 1794052
  371.7 18.8 %copy-start.16 = (bf16[2336,128]{1,0:T(8,128)(2,1)}, bf16[2336,128]{1,0:T(8,128)(2,1)S(1)}, u32[]{:S(2)}) copy-start(bf16[2336,128]{1,0:T(8,128)(2,1)S(1)} %collective-permute-done.5.rest_2_) | copy-start | bytes 1794052
  385.1 3.0 collective-permute-start.10
  385.1 3.0 collective-permute-start.7
  385.6 4.1 collective-permute-start.8
  385.6 4.9 %collective-permute-start.9 = (bf16[2336,128]{1,0:T(8,128)(2,1)S(1)}, bf16[2336,128]{1,0:T(8,128)(2,1)}, u32[]{:S(2)}, u32[]{:S(2)}) collective-permute-start(bf16[2336,128]{1,0:T(8,128)(2,1)S(1)} %collective-permute-done.5.rest_2_), channel_id=1, source_target_pairs={{0,1},{1,0},{2,3},{3,2},{4,5},{5,4},{6,7},{7,6},{8,9},{9,8},{10,11... | collective-permute-start | bytes 1794056 | tf_op jit(solution)/shard_map/ppermute | solution.py:862
  (17 other events, 66.7 us)
Sparse Core Ops, SparseCore 0:
  171.2 87.4 reduce-scatter.2
  261.0 105.0 reduce-scatter.4

commit v4 on v3

--- a/solution.py
+++ b/solution.py
@@ -153,42 +153,52 @@
     p = pl.program_id(0)
     toks, width = tok_ref.shape
     count = toks // QB
+    both = q_ref.shape[1]
 
     @pl.when(p == 0)
     def _():
-        fill_bias(bias_ref, segr_ref[...], count)
+        segr = segr_ref[...]
+        segc = column_of(segr)
+        for i in range(count):
+            low, high = band(i)
+            keys = lax.broadcasted_iota(I32, (QB, high - low), 1) + low
+            queries = lax.broadcasted_iota(I32, (QB, high - low), 0) + i * QB
+            same = segr[:, low:high] == segc[i * QB : (i + 1) * QB]
+            bias_ref[i, :, : high - low] = jnp.where((keys <= queries) & same, 0.0, MASK_VALUE)
         x = tok_ref[...].astype(F32)
         inv = lax.rsqrt(jnp.mean(x * x, axis=1, keepdims=True) + EPSILON)
         attn_ref[...] = (x * inv * ga_ref[...]).astype(BF16)
 
     attn_in = attn_ref[...]
-    weights = jnp.concatenate([wq_ref[...], wk_ref[...], wv_ref[...]], axis=1)
-    qkv = mm(attn_in, weights)
-    q_ref[...] = qkv[:, :PAIR].astype(BF16)
-    k_ref[...] = qkv[:, PAIR : 2 * PAIR].astype(BF16)
-    v = qkv[:, 2 * PAIR :]
-    v_ref[...] = v.astype(BF16)
-    vt = v.T.astype(BF16)
+    q_ref[...] = mm(attn_in, wq_ref[...]).astype(BF16)
+    k_ref[...] = mm(attn_in, wk_ref[...]).astype(BF16)
+    v_ref[...] = mm(attn_in, wv_ref[...]).astype(BF16)
+    lane = lax.broadcasted_iota(I32, (QB, PAIR), 1)
     for i in range(count):
         low, high = band(i)
         cols = slice(i * QB, (i + 1) * QB)
-        q = q_ref[cols, :] * HEAD**-0.5
-        keys = k_ref[low:high, :]
-        parts = []
-        for h in range(2):
-            s = mm(keys, head_mask(q, h), NT) + bias_ref[i, : high - low, :]
-            top = jnp.max(s, axis=0, keepdims=True)
-            w = jnp.exp(s - top)
-            total = jnp.sum(w, axis=0, keepdims=True)
-            lse_ref[0, h : h + 1, cols] = top + jnp.log(total)
-            chances = (w * (1.0 / total)).astype(BF16)
-            parts.append(mm(vt[h * HEAD : (h + 1) * HEAD, low:high], chances))
-        mixt_ref[:, cols] = jnp.concatenate(parts, axis=0).astype(BF16)
-    mix_ref[pl.ds(pl.multiple_of(p * PAIR, PAIR), PAIR), :] = mixt_ref[...]
+        for pair in range(both // PAIR):
+            lanes = slice(pair * PAIR, (pair + 1) * PAIR)
+            q = q_ref[cols, lanes] * HEAD**-0.5
+            keys = k_ref[low:high, lanes]
+            values = v_ref[low:high, lanes]
+            parts, sums = [], []
+            for h in range(2):
+                s = mm(head_mask(q, h), keys, NT) + bias_ref[i, :, : high - low]
+                top = jnp.max(s, axis=1, keepdims=True)
+                w = jnp.exp(s - top)
+                total = jnp.sum(w, axis=1, keepdims=True)
+                sums.append(top + jnp.log(total))
+                parts.append(mm((w * (1.0 / total)).astype(BF16), values))
+            mixed = jnp.where(lane < HEAD, parts[0], parts[1])
+            lse_ref[pair, :, cols] = jnp.where(lane == 0, sums[0], sums[1]).T[:2]
+            mixt_ref[lanes, cols] = mixed.T.astype(BF16)
+            at = pl.ds(pl.multiple_of(p * both + pair * PAIR, PAIR), PAIR)
+            mix_ref[cols, at] = mixed.astype(BF16)
 
     @pl.when(p == pl.num_programs(0) - 1)
     def _():
-        res = tok_ref[...].astype(F32) + mm(mix_ref[...], wo_ref[...], TN)
+        res = tok_ref[...].astype(F32) + mm(mix_ref[...], wo_ref[...])
         res_ref[...] = res
         inv = lax.rsqrt(jnp.mean(res * res, axis=1, keepdims=True) + EPSILON)
         ffn_in = (res * inv * gf_ref[...]).astype(BF16)
@@ -197,14 +207,16 @@
 
 def attend(tokens, segr, keyr, w_qkv, w_o, ga, gf):
     toks, width = tokens.shape
-    pair_cols = pl.BlockSpec((toks, PAIR), lambda p: (0, p))
+    both = 2 * PAIR
+    pair_cols = pl.BlockSpec((toks, both), lambda p: (0, p))
     heads = jax.ShapeDtypeStruct((toks, width), BF16)
     weights = [
-        pl.BlockSpec((width, PAIR), lambda p, part=part: (0, part * PAIRS + p)) for part in range(3)
+        pl.BlockSpec((width, both), lambda p, part=part: (0, part * PAIRS // 2 + p))
+        for part in range(3)
     ]
     return pl.pallas_call(
         attend_kernel,
-        grid=(PAIRS,),
+        grid=(PAIRS // 2,),
         in_specs=[
             whole((toks, width)),
             whole((1, toks)),
@@ -218,8 +230,8 @@
             pair_cols,
             pair_cols,
             pair_cols,
-            pl.BlockSpec((1, 2, toks), lambda p: (p, 0, 0)),
-            pl.BlockSpec((PAIR, toks), lambda p: (p, 0)),
+            pl.BlockSpec((2, 2, toks), lambda p: (p, 0, 0)),
+            pl.BlockSpec((both, toks), lambda p: (p, 0)),
             whole((toks, width)),
             whole((toks, width)),
             whole((toks, width)),
@@ -237,8 +249,8 @@
             heads,
         ],
         scratch_shapes=[
-            pltpu.VMEM((toks // QB, 3 * QB, QB), F32),
-            pltpu.VMEM((width, toks), BF16),
+            pltpu.VMEM((toks // QB, QB, 3 * QB), F32),
+            pltpu.VMEM((toks, width), BF16),
         ],
         compiler_params=params(),
         cost_estimate=cost(42),
@@ -266,23 +278,20 @@
     dv_ref,
     do_ref,
 ):
-    p = pl.program_id(0)
     toks, width = gb_ref.shape
+    both = q_ref.shape[1]
     count = toks // QB
     scale = HEAD**-0.5
-
-    @pl.when(p == 0)
-    def _():
-        fill_bias(bias_ref, segr_ref[...], count)
-
+    fill_bias(bias_ref, segr_ref[...], count)
     gb = gb_ref[...]
-    do_ref[...] = mm(gb, wo_ref[...], NT).astype(BF16)
-    dot_ = mm(wo_ref[...], gb, NT).astype(BF16).astype(F32)
+    grad_out = mm(gb, wo_ref[...], NT)
+    do_ref[...] = grad_out.astype(BF16)
     mixt = mixt_ref[...]
     gwo = mm(mixt, gb).astype(BF16)
-    weighted = dot_ * mixt.astype(F32)
+    weighted = grad_out.astype(BF16).astype(F32).T * mixt.astype(F32)
     delta = [
-        jnp.sum(weighted[h * HEAD : (h + 1) * HEAD], axis=0, keepdims=True) for h in range(2)
+        jnp.sum(weighted[h * HEAD : (h + 1) * HEAD], axis=0, keepdims=True)
+        for h in range(both // HEAD)
     ]
     kt = k_ref[...].astype(F32).T.astype(BF16)
     dk_ref[...] = jnp.zeros_like(dk_ref)
@@ -290,23 +299,25 @@
     for i in range(count):
         low, high = band(i)
         cols = slice(i * QB, (i + 1) * QB)
-        q = q_ref[cols, :] * scale
-        do = do_ref[cols, :]
-        keys = k_ref[low:high, :]
-        values = v_ref[low:high, :]
-        dk_add, dv_add, dqs = [], [], []
-        for h in range(2):
-            qm, dom = head_mask(q, h), head_mask(do, h)
-            s = mm(keys, qm, NT) + bias_ref[i, : high - low, :]
-            pr = jnp.exp(s - lse_ref[0, h : h + 1, cols])
-            dpr = mm(values, dom, NT)
-            ds = (pr * (dpr - delta[h][:, cols])).astype(BF16)
-            dv_add.append(mm(pr.astype(BF16), dom))
-            dk_add.append(mm(ds, qm))
-            dqs.append(mm(kt[h * HEAD : (h + 1) * HEAD, low:high], ds))
-        dk_ref[low:high, :] += dk_add[0] + dk_add[1]
-        dv_ref[low:high, :] += dv_add[0] + dv_add[1]
-        dqt_ref[:, cols] = jnp.concatenate(dqs, axis=0) * scale
+        for pair in range(both // PAIR):
+            lanes = slice(pair * PAIR, (pair + 1) * PAIR)
+            q = q_ref[cols, lanes] * scale
+            do = do_ref[cols, lanes]
+            keys = k_ref[low:high, lanes]
+            values = v_ref[low:high, lanes]
+            dk_add, dv_add = [], []
+            for h in range(2):
+                head = slice((2 * pair + h) * HEAD, (2 * pair + h + 1) * HEAD)
+                qm, dom = head_mask(q, h), head_mask(do, h)
+                s = mm(keys, qm, NT) + bias_ref[i, : high - low, :]
+                pr = jnp.exp(s - lse_ref[pair, h : h + 1, cols])
+                dpr = mm(values, dom, NT)
+                ds = (pr * (dpr - delta[2 * pair + h][:, cols])).astype(BF16)
+                dv_add.append(mm(pr.astype(BF16), dom))
+                dk_add.append(mm(ds, qm))
+                dqt_ref[head, cols] = mm(kt[head, low:high], ds) * scale
+            dk_ref[low:high, lanes] += dk_add[0] + dk_add[1]
+            dv_ref[low:high, lanes] += dv_add[0] + dv_add[1]
     grads = [
         dqt_ref[...].T.astype(BF16),
         dk_ref[...].astype(BF16),
@@ -315,62 +326,51 @@
     for part in range(3):
         gqkv_ref[part] = grads[part]
     gw = mm(attnt_ref[...], jnp.concatenate(grads, axis=1)).astype(BF16)
-    for turn, ref in enumerate((send_ref, keep_ref)):
-
-        @pl.when(p == turn)
-        def _(ref=ref):
-            for part in range(3):
-                ref[part] = gw[:, part * PAIR : (part + 1) * PAIR]
-            for j in range(width // PAIR):
-                ref[3, j * PAIR : (j + 1) * PAIR, :] = gwo[:, j * PAIR : (j + 1) * PAIR]
-
-
-def attend_back(first, core, segr, q, k, v, lse, mixt, gb, attnt, w_o):
+    for core in range(2):
+
+        @pl.when(core_ref[0] == core)
+        def _(core=core):
+            for pair, ref in ((1 - core, send_ref), (core, keep_ref)):
+                for part in range(3):
+                    at = part * both + pair * PAIR
+                    ref[part] = gw[:, at : at + PAIR]
+                for j in range(width // PAIR):
+                    ref[3, j * PAIR : (j + 1) * PAIR, :] = gwo[
+                        pair * PAIR : (pair + 1) * PAIR, j * PAIR : (j + 1) * PAIR
+                    ]
+
+
+def attend_back(turn, core, segr, q, k, v, lse, mixt, gb, attnt, w_o):
     toks, width = gb.shape
-
-    def pair(p, core_ref):
-        return jnp.where(p == 0, 1 - core_ref[0], core_ref[0])
-
-    def fixed(shape):
-        return pl.BlockSpec(
-            shape, lambda p, c: (0,) * len(shape), pipeline_mode=pl.Buffered(buffer_count=1)
-        )
-
-    pair_cols = pl.BlockSpec((toks, PAIR), lambda p, c: (0, first + pair(p, c)))
-    gw_spec = fixed((4, width, PAIR))
+    both = 2 * PAIR
+    pair_cols = pl.BlockSpec((toks, both), lambda p: (0, turn))
     gw_shape = jax.ShapeDtypeStruct((4, width, PAIR), BF16)
     return pl.pallas_call(
         attend_back_kernel,
-        grid_spec=pltpu.PrefetchScalarGridSpec(
-            num_scalar_prefetch=1,
-            grid=(2,),
-            in_specs=[
-                fixed((1, toks)),
-                pair_cols,
-                pair_cols,
-                pair_cols,
-                pl.BlockSpec((1, 2, toks), lambda p, c: (first + pair(p, c), 0, 0)),
-                pl.BlockSpec((PAIR, toks), lambda p, c: (first + pair(p, c), 0)),
-                fixed((toks, width)),
-                fixed((width, toks)),
-                pl.BlockSpec((PAIR, width), lambda p, c: (first + pair(p, c), 0)),
-            ],
-            out_specs=[
-                gw_spec,
-                gw_spec,
-                pl.BlockSpec((3, toks, PAIR), lambda p, c: (0, 0, pair(p, c))),
-            ],
-            scratch_shapes=[
-                pltpu.VMEM((toks // QB, 3 * QB, QB), F32),
-                pltpu.VMEM((PAIR, toks), F32),
-                pltpu.VMEM((toks, PAIR), F32),
-                pltpu.VMEM((toks, PAIR), F32),
-                pltpu.VMEM((toks, PAIR), BF16),
-            ],
-        ),
-        out_shape=[gw_shape, gw_shape, jax.ShapeDtypeStruct((3, toks, 2 * PAIR), BF16)],
-        compiler_params=params(),
-        cost_estimate=cost(10 if first + 2 == PAIRS else 2),
+        grid=(1,),
+        in_specs=[
+            smem(),
+            whole((1, toks)),
+            pair_cols,
+            pair_cols,
+            pair_cols,
+            pl.BlockSpec((2, 2, toks), lambda p: (turn, 0, 0)),
+            pl.BlockSpec((both, toks), lambda p: (turn, 0)),
+            whole((toks, width)),
+            whole((width, toks)),
+            pl.BlockSpec((both, width), lambda p: (turn, 0)),
+        ],
+        out_specs=[whole((4, width, PAIR)), whole((4, width, PAIR)), whole((3, toks, both))],
+        out_shape=[gw_shape, gw_shape, jax.ShapeDtypeStruct((3, toks, both), BF16)],
+        scratch_shapes=[
+            pltpu.VMEM((toks // QB, 3 * QB, QB), F32),
+            pltpu.VMEM((both, toks), F32),
+            pltpu.VMEM((toks, both), F32),
+            pltpu.VMEM((toks, both), F32),
+            pltpu.VMEM((toks, both), BF16),
+        ],
+        compiler_params=params(),
+        cost_estimate=cost(10 if turn + 1 == PAIRS // 2 else 2),
         name="attend_back",
     )(core, segr, q, k, v, lse, mixt, gb, attnt, w_o)
 
@@ -547,32 +547,75 @@
     )(me, wrt, emb, x, w_in, ga)
 
 
-def expert_grads_kernel(lefta_ref, leftb_ref, righta_ref, rightb_ref, out_ref, left_s):
-    rows = lefta_ref.shape[1]
+def early_grads_kernel(
+    gta_ref, gtb_ref, xta_ref, xtb_ref, acta_ref, actb_ref, gpa_ref, gpb_ref, out_ref, gt_s, xt_s
+):
+    rows = gta_ref.shape[1]
+    width = gta_ref.shape[0]
 
     @pl.when(pl.program_id(0) == 0)
     def _():
-        left_s[:, :rows] = lefta_ref[...]
-        left_s[:, rows:] = leftb_ref[...]
-
-    right = jnp.concatenate([righta_ref[...], rightb_ref[...]], axis=0)
-    out_ref[0] = mm(left_s[...], right).astype(BF16)
-
-
-def expert_grads(lefts, rights, wide):
-    width, rows = lefts[0].shape
-    steps = rights[0].shape[1] // wide
-    return pl.pallas_call(
-        expert_grads_kernel,
+        gt_s[:, :rows] = gta_ref[...]
+        gt_s[:, rows:] = gtb_ref[...]
+        xt_s[:, :rows] = xta_ref[...]
+        xt_s[:, rows:] = xtb_ref[...]
+
+    act = jnp.concatenate([acta_ref[...], actb_ref[...]], axis=0)
+    out_ref[0, :width] = mm(gt_s[...], act).astype(BF16)
+    gp = jnp.concatenate([gpa_ref[...], gpb_ref[...]], axis=0)
+    out_ref[0, width:] = mm(xt_s[...], gp).astype(BF16)
+
+
+def early_grads(gts, xts, acts, gps, wide):
+    width, rows = gts[0].shape
+    third = width // 3
+    steps = acts[0].shape[1] // wide
+    return pl.pallas_call(
+        early_grads_kernel,
+        grid=(steps,),
+        in_specs=[whole((width, rows))] * 2
+        + [whole((third, rows))] * 2
+        + [pl.BlockSpec((rows, wide), lambda c: (0, c))] * 4,
+        out_specs=pl.BlockSpec((1, width + third, wide), lambda c: (c, 0, 0)),
+        out_shape=jax.ShapeDtypeStruct((steps, width + third, wide), BF16),
+        scratch_shapes=[
+            pltpu.VMEM((width, 2 * rows), BF16),
+            pltpu.VMEM((third, 2 * rows), BF16),
+        ],
+        compiler_params=params(),
+        cost_estimate=cost(10),
+        name="early_grads",
+    )(*gts, *xts, *acts, *gps)
+
+
+def late_grads_kernel(xta_ref, xtb_ref, gpa_ref, gpb_ref, out_ref, xt_s):
+    width, rows = xta_ref.shape
+    third = width // 3
+
+    @pl.when(pl.program_id(0) == 0)
+    def _():
+        xt_s[:, :rows] = xta_ref[third:, :]
+        xt_s[:, rows:] = xtb_ref[third:, :]
+
+    gp = jnp.concatenate([gpa_ref[...], gpb_ref[...]], axis=0)
+    out_ref[0] = mm(xt_s[...], gp).astype(BF16)
+
+
+def late_grads(xts, gps, wide):
+    width, rows = xts[0].shape
+    left = width - width // 3
+    steps = gps[0].shape[1] // wide
+    return pl.pallas_call(
+        late_grads_kernel,
         grid=(steps,),
         in_specs=[whole((width, rows))] * 2 + [pl.BlockSpec((rows, wide), lambda c: (0, c))] * 2,
-        out_specs=pl.BlockSpec((1, width, wide), lambda c: (c, 0, 0)),
-        out_shape=jax.ShapeDtypeStruct((steps, width, wide), BF16),
-        scratch_shapes=[pltpu.VMEM((width, 2 * rows), BF16)],
-        compiler_params=params(),
-        cost_estimate=cost(5),
-        name="expert_grads",
-    )(*lefts, *rights)
+        out_specs=pl.BlockSpec((1, left, wide), lambda c: (c, 0, 0)),
+        out_shape=jax.ShapeDtypeStruct((steps, left, wide), BF16),
+        scratch_shapes=[pltpu.VMEM((left, 2 * rows), BF16)],
+        compiler_params=params(),
+        cost_estimate=cost(10),
+        name="late_grads",
+    )(*xts, *gps)
 
 
 def grad_act_kernel(g_ref, wout_ref, out_ref, gt_ref):
@@ -645,18 +688,24 @@
     )(acta, actb, w_out)
 
 
-def expert_sums_kernel(in_ref, out_ref, win_ref, wout_ref):
-    win_ref[0] = in_ref[...].astype(F32)
-    wout_ref[0] = out_ref[...].astype(F32).T
-
-
-def expert_sums(grad_in, grad_out):
-    width, share = grad_in.shape
-    block = pl.BlockSpec((width, LANES), lambda k: (0, k))
+def expert_sums_kernel(early_ref, late_ref, win_ref, wout_ref):
+    width = wout_ref.shape[2]
+    third = width // 3
+    win_ref[0, :third] = early_ref[width:].astype(F32)
+    win_ref[0, third:] = late_ref[...].astype(F32)
+    wout_ref[0] = early_ref[:width].astype(F32).T
+
+
+def expert_sums(early, late):
+    share = early.shape[1]
+    width = early.shape[0] * 3 // 4
     return pl.pallas_call(
         expert_sums_kernel,
         grid=(share // LANES,),
-        in_specs=[block, block],
+        in_specs=[
+            pl.BlockSpec((early.shape[0], LANES), lambda k: (0, k)),
+            pl.BlockSpec((late.shape[0], LANES), lambda k: (0, k)),
+        ],
         out_specs=[
             pl.BlockSpec((1, width, LANES), lambda k: (0, 0, k)),
             pl.BlockSpec((1, LANES, width), lambda k: (0, k, 0)),
@@ -668,7 +717,7 @@
         compiler_params=params(),
         cost_estimate=cost(3),
         name="expert_sums",
-    )(grad_in, grad_out)
+    )(early, late)
 
 
 def gather_rows(key_row, row_refs):
@@ -874,6 +923,18 @@
 
 def xor_permute(value, axis, d):
     return lax.ppermute(value, axis, [(j, j ^ d) for j in range(lax.axis_size(axis))])
+
+
+def gather_over_dp(part, beside):
+    groups = lax.axis_size("dp")
+    me = lax.axis_index("dp")
+    parts = [part] + [xor_permute(part, "dp", d) for d in range(1, groups)]
+    parts, beside = lax.optimization_barrier((parts, beside))
+    parts = jnp.stack(parts)
+    for bit in range((groups - 1).bit_length()):
+        split = parts.reshape(-1, 2, 1 << bit, *part.shape)
+        parts = jnp.where((me >> bit) & 1 == 1, split[:, ::-1], split)
+    return parts.reshape(-1, part.shape[1]), beside
 
 
 def on_device(
@@ -918,13 +979,10 @@
     act_b, gp_b, xt_b, gout_b, gwr_b, gemb_b = expert(me, wrt, embed, x_b, w_in, gact_b, share)
     gout_b, gback_a = hold((gout_b, gback_a))
     gback_b = exchange(gout_b)
-    gw_one = expert_grads((gt_a, gt_b), (act_a, act_b), share)
-    total_one = lax.psum_scatter(gw_one, "dp", scatter_dimension=0, tiled=True)[0]
-    gw_one, late_gp = hold((gw_one, gp_b))
-    gw_two = expert_grads((xt_a, xt_b), (gp_a, late_gp), share)
-    total_two = lax.psum_scatter(gw_two, "dp", scatter_dimension=0, tiled=True)[0]
+    early = early_grads((gt_a, gt_b), (xt_a, xt_b), (act_a, act_b), (gp_a, gp_b), share)
+    early_sum = lax.psum_scatter(early, "dp", scatter_dimension=0, tiled=True)[0]
     attnt = attn_in.T
-    gback_b, gw_two, attnt = hold((gback_b, gw_two, attnt))
+    gback_b, early, attnt = hold((gback_b, early, attnt))
     gres, gb, ggf = combine_back(keyr, res, cotangent, gf, (gback_a, gback_b))
 
     small = jnp.concatenate(
@@ -942,7 +1000,7 @@
     both, grads = [], []
     for turn in range(PAIRS // 2):
         send, keep, grad = attend_back(
-            2 * turn, core, segr, q, k, v, lse, mixt, gb, attnt, w_attn_out
+            turn, core, segr, q, k, v, lse, mixt, gb, attnt, w_attn_out
         )
         grads.append(grad)
         got = swap_cores(send)
@@ -952,25 +1010,29 @@
         elif turn == 1:
             gb, both, small, grad = hold((gb, both, small, grad))
             share_one = sum_over_chips(jnp.concatenate([*both, small], axis=1))
-    last, late_act = hold((both[-1], act_b))
+    last, late_act, share_one = hold((both[-1], act_b, share_one))
     share_two = sum_over_chips(last)
     fout = expert_out_of(act_a, late_act, w_out, share, peers)
-    share_two, share_one, fout, total_one = hold((share_two, share_one, fout, total_one))
+    share_two, fout, late_gp, late_res = hold((share_two, fout, gp_b, gres))
     blocks = jnp.concatenate([share_one, share_two], axis=0).reshape(shards, -1, LANES)
     blocks = lax.all_to_all(blocks, "dp", 0, 0, tiled=True)
-    blocks, fout = hold((blocks, fout))
+    late = late_grads((xt_a, xt_b), (gp_a, late_gp), share)
+    grad_tokens = grad_tokens_of(tokens, late_res, ga, w_qkv, grads)
+    blocks, fout, late, grad_tokens, early_sum = hold(
+        (blocks, fout, late, grad_tokens, early_sum)
+    )
     fback = exchange(fout.reshape(2 * toks, width))
-    total = lax.all_gather(sum_blocks(blocks), "dp", axis=0, tiled=True)
+    total, fback = gather_over_dp(sum_blocks(blocks), fback)
+    late_sum = lax.psum_scatter(late, "dp", scatter_dimension=0, tiled=True)[0]
     pieces = [total] + [xor_permute(total, "expert", d) for d in range(2, peers, 2)]
-    grad_tokens = grad_tokens_of(tokens, gres, ga, w_qkv, grads)
     out_tokens = combine(keyn, res, fback)
-    pieces, grad_tokens, out_tokens = hold((pieces, grad_tokens, out_tokens))
+    pieces, out_tokens = hold((pieces, out_tokens))
     blocks = pieces + [swap_cores(piece) for piece in pieces]
     grad_w_qkv, grad_w_attn_out, grad_gain_attn, grad_gain_ffn, grad_router, grad_embed = (
         shared_sums(me, blocks, rows, extra, w_qkv, ga, experts, rdim)
     )
-    grad_w_qkv, total_two = hold((grad_w_qkv, total_two))
-    grad_w_in, grad_w_out = expert_sums(total_two, total_one)
+    grad_w_qkv, late_sum = hold((grad_w_qkv, late_sum))
+    grad_w_in, grad_w_out = expert_sums(early_sum, late_sum)
     return (
         out_tokens,
         grad_tokens,

time: 417 us -> 402 us (0.964)
  blocking collectives: 62.5 us -> 0 us
  waiting for transfers between devices: 27.7 us -> 66.6 us
  starting transfers between devices: 41.7 us -> 49.4 us
  Pallas kernels: 253 us -> 247 us
  other arithmetic: 5.84 us -> 10.2 us
    all_to_all x1 -> x0, blocking collectives: 37.8 us -> none  [on_device(): blocks = lax.all_to_all(blocks, 'dp', 0, 0, tiled=True)]
    ppermute x3 -> x6, waiting for transfers between devices: 17.3 us -> 45.7 us  [xor_permute(): lax.ppermute(value, axis, [(j, j ^ d) for j in range(lax.axis_size(axis))])]
    all_gather x1 -> x0, blocking collectives: 24.6 us -> none  [on_device(): total = lax.all_gather(sum_blocks(blocks), 'dp', axis=0, tiled=True)]
    all_to_all x0 -> x1, waiting for transfers between devices: none -> 8.44 us  [on_device(): blocks = lax.all_to_all(blocks, 'dp', 0, 0, tiled=True)]
    pallas_call x7, Pallas kernels: 126 us -> 121 us  [the longest x3 42.7 us: attend_back(): pl.pallas_call(attend_back_kernel, grid=(1,), in_specs=[smem(), whole((1,...]
    all_to_all x0 -> x1, starting transfers between devices: none -> 5.44 us  [on_device(): blocks = lax.all_to_all(blocks, 'dp', 0, 0, tiled=True)]
    ppermute x3 -> x6, starting transfers between devices: 3.49 us -> 7.94 us  [xor_permute(): lax.ppermute(value, axis, [(j, j ^ d) for j in range(lax.axis_size(axis))])]
  transfers between devices with their start and end apart: 21 -> 25, of which waited for: 8 -> 13; matrix products, arithmetic and copies ran while one was open for 2% -> 3% of each run, Pallas kernels for 58% -> 59%
where the time goes in v4:
time: 402 us; the launch traced here: 397 us
  Pallas kernels  247 us (61%)
  waiting for transfers between devices  66.6 us (17%)
  starting transfers between devices  49.4 us (12%)
  between operations  14.6 us (4%)
  other arithmetic  10.2 us (3%)
  local copies, waits for them, and re-layouts  8.86 us (2%)
    pallas_call x2, Pallas kernels, expert(): pl.pallas_call(expert_kernel, grid=(hidden // wide,), in_specs=[smem(), w...  47.9 us
    ppermute x6, waiting for transfers between devices, xor_permute(): lax.ppermute(value, axis, [(j, j ^ d) for j in range(lax.axis_size(axis))])  45.7 us
    pallas_call x3, Pallas kernels, attend_back(): pl.pallas_call(attend_back_kernel, grid=(1,), in_specs=[smem(), whole((1,...  42.7 us
    pallas_call x1, Pallas kernels, attend(): pl.pallas_call(attend_kernel, grid=(PAIRS // 2,), in_specs=[whole((toks,...  41.1 us
    all_to_all x6, starting transfers between devices, exchange(): lax.all_to_all(rows.reshape(peers, -1, width), 'expert', split_axis=0, co...  25.9 us
    pallas_call x2, Pallas kernels, grad_act(): pl.pallas_call(grad_act_kernel, grid=(hidden // wide,), in_specs=[pl.Bloc...  20.1 us
    pallas_call x1, Pallas kernels, early_grads(): pl.pallas_call(early_grads_kernel, grid=(steps,), in_specs=[whole((width,...  19.7 us
    pallas_call x1, Pallas kernels, expert_out_of(): pl.pallas_call(expert_out_kernel, grid=(hidden // wide,), in_specs=[cols,...  15.1 us
  transfers between devices with their start and end apart: 25, of which 13 were waited for; matrix products, arithmetic and copies ran while one was open for 3% of the time, Pallas kernels for 59%

profile of v4, /device:TPU:0, one launch (start us, length us, event | category | flops | bytes accessed | tf_op | source)
XLA Modules:
  0.0 397.1 jit_solution(17544402797948401494)
XLA Ops:
  7.2 6.9 %place.1 = (s32[1,1024]{1,0:T(1,128)}, s32[1,1024]{1,0:T(1,128)}, bf16[2048,768]{1,0:T(8,128)(2,1)}) custom-call(s32[1,1024]{1,0:T(1,128)} %bitcast.50, bf16[1024,768]{1,0:T(8,128)(2,1)} %cot_ref.3), custom_call_target="tpu_custom_call" | custom-call | flops 5750000128 | tf_op jit(solution)/shard_map/place/pallas_call | solution.py:98
  14.0 5.3 %all-to-all-start.1 = ((bf16[8,256,768]{2,1,0:T(8,128)(2,1)}), bf16[8,256,768]{2,1,0:T(8,128)(2,1)}, u32[]{:S(2)}, u32[]{:S(2)}) async-start(bf16[8,256,768]{2,1,0:T(8,128)(2,1)} %bitcast.34), calls=%async_computation.1 | async-start | bytes 6291456 | tf_op jit(solution)/shard_map/all_to_all | solution.py:899
  20.5 41.1 %attend.1 = (bf16[1024,768]{1,0:T(8,128)(2,1)}, bf16[1024,768]{1,0:T(8,128)(2,1)}, bf16[1024,768]{1,0:T(8,128)(2,1)}, f32[6,2,1024]{2,1,0:T(2,128)}, bf16[768,10...) custom-call(bf16[1024,768]{1,0:T(8,128)(2,1)} %tok_ref.3, ...), custom_call_target="tpu_custom_call" | custom-call | flops 48299999232 | tf_op jit(solution)/shard_map/attend/pallas_call | solution.py:217
  66.1 10.0 %grad_act.3 = (bf16[1024,3072]{1,0:T(8,128)(2,1)}, bf16[768,1024]{1,0:T(8,128)(2,1)}) custom-call(bf16[8,2,128,768]{3,2,1,0:T(8,128)(2,1)} %bitcast.6.g_ref, bf16[1,3072,768]{2,1,0:T(8,128)(2,1)} %wout_ref.5), custom_call_target="tpu_custom_call" | custom-call | flops 8049999872 | tf_op jit(solution)/shard_map/grad_act/pallas_call | solution.py:635
  76.0 10.1 %grad_act.2 = (bf16[1024,3072]{1,0:T(8,128)(2,1)}, bf16[768,1024]{1,0:T(8,128)(2,1)}) custom-call(bf16[8,2,128,768]{3,2,1,0:T(8,128)(2,1)} %bitcast.6.g_ref, bf16[1,3072,768]{2,1,0:T(8,128)(2,1)} %wout_ref.5), custom_call_target="tpu_custom_call" | custom-call | flops 8049999872 | tf_op jit(solution)/shard_map/grad_act/pallas_call | solution.py:635
  91.8 24.0 %expert.3 = (bf16[1024,3072]{1,0:T(8,128)(2,1)}, bf16[1024,3072]{1,0:T(8,128)(2,1)}, bf16[768,1024]{1,0:T(8,128)(2,1)}, bf16[1024,768]{1,0:T(8,128)(2,1)}, f32[16,768]{1,0:T(8,128)}, /*index=5*/f32[8,16]{1,0:T(8,128)}) custom-call(s32[1]{0:T(128)} %bitcast.me_ref, bf16[16,768]{1,0:T(8,128)(2,1)} %bitcast.48, f32[8,16]{1,0:T(8,128)} %emb_ref.3, ...), custom_call_target="tpu_custom_call" | custom-call | flops 26449999872 | tf_op jit(solution)/shard_map/expert/pallas_call | solution.py:511
  121.6 23.9 %expert.2 = (bf16[1024,3072]{1,0:T(8,128)(2,1)}, bf16[1024,3072]{1,0:T(8,128)(2,1)}, bf16[768,1024]{1,0:T(8,128)(2,1)}, bf16[1024,768]{1,0:T(8,128)(2,1)}, f32[16,768]{1,0:T(8,128)}, /*index=5*/f32[8,16]{1,0:T(8,128)}) custom-call(s32[1]{0:T(128)} %bitcast.me_ref, bf16[16,768]{1,0:T(8,128)(2,1)} %bitcast.49, f32[8,16]{1,0:T(8,128)} %emb_ref.3, ...), custom_call_target="tpu_custom_call" | custom-call | flops 26449999872 | tf_op jit(solution)/shard_map/expert/pallas_call | solution.py:511
  152.8 19.7 %early_grads.1 = bf16[4,1024,768]{2,1,0:T(8,128)(2,1)} custom-call(bf16[768,1024]{1,0:T(8,128)(2,1)} %get-tuple-element.117.gta_ref, bf16[768,1024]{1,0:T(8,128)(2,1)} %get-tuple-element.118.gtb_ref, bf16[768,1024]{1,0:T(8,128)(2,1)} %get-tuple-element.119.xta_ref, bf16[768,1024]{1,0:T(8,128)(2,1)} %get-tuple-element.120.xtb_ref, ...), custom_call_target="tpu_custom_call" | custom-call | flops 11500000256 | tf_op jit(solution)/shard_map/early_grads/pallas_call | solution.py:573
  173.4 10.1 %combine_back.1 = (f32[1024,768]{1,0:T(8,128)}, bf16[1024,768]{1,0:T(8,128)(2,1)}, f32[1,768]{1,0:T(1,128)}) custom-call(s32[1,1024]{1,0:T(1,128)} %get-tuple-element.96.keyr_ref, f32[1024,768]{1,0:T(8,128)} %get-tuple-element.102.res_ref, bf16[1024,768]{1,0:T(8,128)(2,1)} %cot_ref.3, f32[1,768]{1,0:T(1,128)} %reshape.83.gf_ref, bf16[1024,768]{1,0:T(8,128)(2,1)} %bitcast.36, ...), custom_call_target="tpu_custom_call" | custom-call | flops 115000000512 | tf_op jit(solution)/shard_map/combine_back/pallas_call | solution.py:753
  183.5 14.3 %attend_back.3 = (bf16[4,768,128]{2,1,0:T(8,128)(2,1)}, bf16[4,768,128]{2,1,0:T(8,128)(2,1)}, bf16[3,1024,256]{2,1,0:T(8,128)(2,1)}) custom-call(s32[1]{0:T(128)S(6)} %and.13.core_ref, s32[1,1024]{1,0:T(1,128)} %segr_ref.7, bf16[1024,768]{1,0:T(8,128)(2,1)} %get-tuple-element.97.q_ref, bf16[1024,768]{1,0:T(8,128)(2,1)} %get-tuple-element.98.k_ref, ...), custom_call_target="tpu_custom_call" | custom-call | flops 2300000000 | tf_op jit(solution)/shard_map/attend_back/pallas_call | solution.py:348
  198.3 14.1 %attend_back.4 = (bf16[4,768,128]{2,1,0:T(8,128)(2,1)}, bf16[4,768,128]{2,1,0:T(8,128)(2,1)}, bf16[3,1024,256]{2,1,0:T(8,128)(2,1)}) custom-call(s32[1]{0:T(128)S(6)} %and.13.core_ref, s32[1,1024]{1,0:T(1,128)} %segr_ref.7, bf16[1024,768]{1,0:T(8,128)(2,1)} %get-tuple-element.97.q_ref, bf16[1024,768]{1,0:T(8,128)(2,1)} %get-tuple-element.98.k_ref, ...), custom_call_target="tpu_custom_call" | custom-call | flops 2300000000 | tf_op jit(solution)/shard_map/attend_back/pallas_call | solution.py:348
  222.0 14.2 %attend_back.5 = (bf16[4,768,128]{2,1,0:T(8,128)(2,1)}, bf16[4,768,128]{2,1,0:T(8,128)(2,1)}, bf16[3,1024,256]{2,1,0:T(8,128)(2,1)}) custom-call(s32[1]{0:T(128)S(6)} %and.13.core_ref, s32[1,1024]{1,0:T(1,128)} %segr_ref.7, bf16[1024,768]{1,0:T(8,128)(2,1)} %get-tuple-element.97.q_ref, bf16[1024,768]{1,0:T(8,128)(2,1)} %get-tuple-element.98.k_ref, ...), custom_call_target="tpu_custom_call" | custom-call | flops 11500000256 | tf_op jit(solution)/shard_map/attend_back/pallas_call | solution.py:348
  246.3 15.1 %expert_out.1 = bf16[8,2,128,768]{3,2,1,0:T(8,128)(2,1)} custom-call(bf16[1024,3072]{1,0:T(8,128)(2,1)} %get-tuple-element.121.acta_ref, bf16[1024,3072]{1,0:T(8,128)(2,1)} %get-tuple-element.149.actb_ref, bf16[1,3072,768]{2,1,0:T(8,128)(2,1)} %wout_ref.5), custom_call_target="tpu_custom_call" | custom-call | flops 16099999744 | tf_op jit(solution)/shard_map/expert_out/pallas_call | solution.py:678
  262.4 5.4 %all-to-all-start.7 = ((bf16[4,584,128]{2,1,0:T(8,128)(2,1)}), bf16[4,584,128]{2,1,0:T(8,128)(2,1)S(1)}, u32[]{:S(2)}, u32[]{:S(2)}) async-start(bf16[4,584,128]{2,1,0:T(8,128)(2,1)} %bitcast.15), calls=%async_computation.7 | async-start | bytes 1196032 | tf_op jit(solution)/shard_map/all_to_all | solution.py:1018
  267.8 11.7 %late_grads.1 = bf16[4,512,768]{2,1,0:T(8,128)(2,1)} custom-call(bf16[768,1024]{1,0:T(8,128)(2,1)} %get-tuple-element.119.xta_ref, bf16[768,1024]{1,0:T(8,128)(2,1)} %get-tuple-element.120.xtb_ref, bf16[1024,3072]{1,0:T(8,128)(2,1)} %get-tuple-element.123.gpa_ref, bf16[1024,3072]{1,0:T(8,128)(2,1)} %get-tuple-element.153.gpb_ref), custom_call_target="tpu_custom_call" | custom-call | flops 11500000256 | tf_op jit(solution)/shard_map/late_grads/pallas_call | solution.py:608
  279.5 9.3 %grad_tokens.1 = f32[1024,768]{1,0:T(8,128)} custom-call(bf16[1024,768]{1,0:T(8,128)(2,1)} %tok_ref.3, f32[1024,768]{1,0:T(8,128)} %get-tuple-element.154.gres_ref, f32[1,768]{1,0:T(1,128)} %reshape.82.ga_ref, bf16[768,2304]{1,0:T(8,128)(2,1)} %w_ref.3, bf16[3,1024,256]{2,1,0:T(8,128)(2,1)} %get-tuple-element.129.rest_0_, ...), custom_call_target="tpu_custom_call" | custom-call | flops 10350000128 | tf_op jit(solution)/shard_map/grad_tokens/pallas_call | solution.py:390
  288.8 8.4 %all-to-all-done.7 = bf16[4,584,128]{2,1,0:T(8,128)(2,1)S(1)} async-done(((bf16[4,584,128]{2,1,0:T(8,128)(2,1)}), bf16[4,584,128]{2,1,0:T(8,128)(2,1)S(1)}, u32[]{:S(2)}, u32[]{:S(2)}) %all-to-all-start.7) | async-done | bytes 598048 | tf_op jit(solution)/shard_map/all_to_all | solution.py:1018
  307.4 6.0 %collective-permute-done.6 = bf16[584,128]{1,0:T(8,128)(2,1)S(1)} collective-permute-done((bf16[584,128]{1,0:T(8,128)(2,1)S(1)}, bf16[584,128]{1,0:T(8,128)(2,1)S(1)}, u32[]{:S(2)}, u32[]{:S(2)}) %collective-permute-start.6) | collective-permute-done | bytes 149536 | tf_op jit(solution)/shard_map/ppermute | solution.py:925
  313.4 23.6 %collective-permute-done.5 = bf16[584,128]{1,0:T(8,128)(2,1)} collective-permute-done((bf16[584,128]{1,0:T(8,128)(2,1)S(1)}, bf16[584,128]{1,0:T(8,128)(2,1)}, u32[]{:S(2)}, u32[]{:S(2)}) %collective-permute-start.5) | collective-permute-done | bytes 149536 | tf_op jit(solution)/shard_map/ppermute | solution.py:925
  345.6 7.8 %combine.1 = bf16[1024,768]{1,0:T(8,128)(2,1)} custom-call(s32[1,1024]{1,0:T(1,128)} %get-tuple-element.162.keyn_ref, f32[1024,768]{1,0:T(8,128)} %get-tuple-element.102.res_ref, bf16[2048,768]{1,0:T(8,128)(2,1)} %bitcast.33), custom_call_target="tpu_custom_call" | custom-call | flops 5750000128 | tf_op jit(solution)/shard_map/combine/pallas_call | solution.py:782
  353.4 6.3 %collective-permute-done.9.rest_3_ = bf16[2336,128]{1,0:T(8,128)(2,1)S(1)} collective-permute-done((bf16[2336,128]{1,0:T(8,128)(2,1)}, bf16[2336,128]{1,0:T(8,128)(2,1)S(1)}, u32[]{:S(2)}, u32[]{:S(2)}) %collective-permute-start.9) | collective-permute-done | bytes 598048 | tf_op jit(solution)/shard_map/ppermute | solution.py:925
  359.7 9.6 %collective-permute-done.8.rest_2_ = bf16[2336,128]{1,0:T(8,128)(2,1)S(1)} collective-permute-done((bf16[2336,128]{1,0:T(8,128)(2,1)}, bf16[2336,128]{1,0:T(8,128)(2,1)S(1)}, u32[]{:S(2)}, u32[]{:S(2)}) %collective-permute-start.8) | collective-permute-done | bytes 598048 | tf_op jit(solution)/shard_map/ppermute | solution.py:925
  374.9 9.6 %shared_sums.1 = (f32[768,2304]{1,0:T(8,128)}, f32[768,768]{1,0:T(8,128)}, f32[768]{0:T(1024)}, f32[768]{0:T(1024)}, f32[16,768]{1,0:T(8,128)}, /*index=5*/f32[8,16]{1,0:T(8,128)}) custom-call(s32[1]{0:T(128)} %bitcast.me_ref, bf16[768,2304]{1,0:T(8,128)(2,1)} %w_ref.3, f32[1,768]{1,0:T(1,128)} %reshape.82.ga_ref, bf16[2336,128]{1,0:T(8,128)(2,1)} %bitcast.25.rest_0_, ...), custom_call_target="tpu_custom_call" | custom-call | flops 2300000000 | tf_op jit(solution)/shard_map/shared_sums/pallas_call | solution.py:864
  384.6 5.5 %expert_sums.1 = (f32[1,768,768]{2,1,0:T(8,128)}, f32[1,768,768]{2,1,0:T(8,128)}) custom-call(bf16[1024,768]{1,0:T(8,128)(2,1)} %bitcast.46, bf16[512,768]{1,0:T(8,128)(2,1)} %bitcast.47), custom_call_target="tpu_custom_call" | custom-call | flops 3449999872 | tf_op jit(solution)/shard_map/expert_sums/pallas_call | solution.py:702
  (114 shorter events, 70.4 us)
Async XLA Ops:
  14.0 47.6 %all-to-all-start.1 = ((bf16[8,256,768]{2,1,0:T(8,128)(2,1)}), bf16[8,256,768]{2,1,0:T(8,128)(2,1)}, u32[]{:S(2)}, u32[]{:S(2)}) async-start(bf16[8,256,768]{2,1,0:T(8,128)(2,1)} %bitcast.34), calls=%async_computation.1 | async-start | bytes 6291456 | tf_op jit(solution)/shard_map/all_to_all | solution.py:899
  61.6 25.5 %all-to-all-start = ((bf16[8,128,768]{2,1,0:T(8,128)(2,1)}), bf16[8,128,768]{2,1,0:T(8,128)(2,1)S(1)}, u32[]{:S(2)}, u32[]{:S(2)}) async-start(bf16[8,128,768]{2,1,0:T(8,128)(2,1)} %bitcast.41), calls=%async_computation | async-start | bytes 3145728 | tf_op jit(solution)/shard_map/all_to_all | solution.py:899
  88.3 27.6 %all-to-all-start.2 = ((bf16[8,128,768]{2,1,0:T(8,128)(2,1)}), bf16[8,128,768]{2,1,0:T(8,128)(2,1)S(1)}, u32[]{:S(2)}, u32[]{:S(2)}) async-start(bf16[8,128,768]{2,1,0:T(8,128)(2,1)} %bitcast.7), calls=%async_computation.2 | async-start | bytes 3145728 | tf_op jit(solution)/shard_map/all_to_all | solution.py:899
  117.0 28.5 %all-to-all-start.3 = ((bf16[8,128,768]{2,1,0:T(8,128)(2,1)}), bf16[8,128,768]{2,1,0:T(8,128)(2,1)S(1)}, u32[]{:S(2)}, u32[]{:S(2)}) async-start(bf16[8,128,768]{2,1,0:T(8,128)(2,1)} %bitcast.40), calls=%async_computation.3 | async-start | bytes 3145728 | tf_op jit(solution)/shard_map/all_to_all | solution.py:899
  146.6 26.8 %all-to-all-start.4 = ((bf16[8,128,768]{2,1,0:T(8,128)(2,1)}), bf16[8,128,768]{2,1,0:T(8,128)(2,1)}, u32[]{:S(2)}, u32[]{:S(2)}) async-start(bf16[8,128,768]{2,1,0:T(8,128)(2,1)} %bitcast.37), calls=%async_computation.4 | async-start | bytes 3145728 | tf_op jit(solution)/shard_map/all_to_all | solution.py:899
  151.0 146.3 %reduce-scatter.3.cloned.1.call-start = ((), (), s32[]{:S(2)}) async-start(), calls=%async_computation.11 | async-start | bytes 7864320 | tf_op jit(solution)/shard_map/reduce_scatter | solution.py:983
  197.8 17.0 %collective-permute-start = (bf16[4,768,128]{2,1,0:T(8,128)(2,1)}, bf16[4,768,128]{2,1,0:T(8,128)(2,1)S(1)}, u32[]{:S(2)}, u32[]{:S(2)}) collective-permute-start(bf16[4,768,128]{2,1,0:T(8,128)(2,1)} %get-tuple-element.132), channel_id=1, source_target_pairs={{0,1},{1,0},{2,3},{3,2},{4,5},{5,4},{6,7},{7,6},{8,9},{9,8},{10,11... | collective-permute-start | bytes 2359304 | tf_op jit(solution)/shard_map/ppermute | solution.py:911
  212.4 2.6 collective-permute-start.1
  217.7 24.4 %all-to-all-start.5 = ((bf16[4,1568,128]{2,1,0:T(8,128)(2,1)}), bf16[4,1568,128]{2,1,0:T(8,128)(2,1)S(1)}, u32[]{:S(2)}, u32[]{:S(2)}) async-start(bf16[4,1568,128]{2,1,0:T(8,128)(2,1)} %pad_maximum_fusion), calls=%async_computation.5 | async-start | bytes 3211264 | tf_op jit(solution)/shard_map/all_to_all | solution.py:920
  236.2 2.5 collective-permute-start.3
  242.6 18.7 %all-to-all-start.6 = ((bf16[4,768,128]{2,1,0:T(8,128)(2,1)}), bf16[4,768,128]{2,1,0:T(8,128)(2,1)S(1)}, u32[]{:S(2)}, u32[]{:S(2)}) async-start(bf16[4,768,128]{2,1,0:T(8,128)(2,1)} %add_convert_fusion), calls=%async_computation.6 | async-start | bytes 1572864 | tf_op jit(solution)/shard_map/all_to_all | solution.py:920
  262.4 34.9 %all-to-all-start.7 = ((bf16[4,584,128]{2,1,0:T(8,128)(2,1)}), bf16[4,584,128]{2,1,0:T(8,128)(2,1)S(1)}, u32[]{:S(2)}, u32[]{:S(2)}) async-start(bf16[4,584,128]{2,1,0:T(8,128)(2,1)} %bitcast.15), calls=%async_computation.7 | async-start | bytes 1196032 | tf_op jit(solution)/shard_map/all_to_all | solution.py:1018
  267.8 116.8 %reduce-scatter.5.cloned.1.call-start = ((), (), s32[]{:S(2)}) async-start(), calls=%async_computation.12 | async-start | bytes 3932160 | tf_op jit(solution)/shard_map/reduce_scatter | solution.py:1026
  298.1 41.5 %all-to-all-start.8 = ((bf16[8,256,768]{2,1,0:T(8,128)(2,1)}), bf16[8,256,768]{2,1,0:T(8,128)(2,1)S(1)}, u32[]{:S(2)}, u32[]{:S(2)}) async-start(bf16[8,256,768]{2,1,0:T(8,128)(2,1)} %bitcast.17), calls=%async_computation.9 | async-start | bytes 6291456 | tf_op jit(solution)/shard_map/all_to_all | solution.py:899
  302.9 10.5 %collective-permute-start.6 = (bf16[584,128]{1,0:T(8,128)(2,1)S(1)}, bf16[584,128]{1,0:T(8,128)(2,1)S(1)}, u32[]{:S(2)}, u32[]{:S(2)}) collective-permute-start(bf16[584,128]{1,0:T(8,128)(2,1)S(1)} %reduce_sum.38), channel_id=1, source_target_pairs={{0,24},{8,16},{16,8},{24,0},{1,25},{9,17},{17,9},{25,1},{2,26},{10... | collective-permute-start | bytes 448520 | tf_op jit(solution)/shard_map/ppermute | solution.py:925
  304.8 32.2 %collective-permute-start.5 = (bf16[584,128]{1,0:T(8,128)(2,1)S(1)}, bf16[584,128]{1,0:T(8,128)(2,1)}, u32[]{:S(2)}, u32[]{:S(2)}) collective-permute-start(bf16[584,128]{1,0:T(8,128)(2,1)S(1)} %reduce_sum.38), channel_id=1, source_target_pairs={{0,16},{8,24},{16,0},{24,8},{1,17},{9,25},{17,1},{25,9},{2,18},{10... | collective-permute-start | bytes 448520 | tf_op jit(solution)/shard_map/ppermute | solution.py:925
  306.3 30.7 %collective-permute-start.4 = (bf16[584,128]{1,0:T(8,128)(2,1)S(1)}, bf16[584,128]{1,0:T(8,128)(2,1)}, u32[]{:S(2)}, u32[]{:S(2)}) collective-permute-start(bf16[584,128]{1,0:T(8,128)(2,1)S(1)} %reduce_sum.38), channel_id=1, source_target_pairs={{0,8},{8,0},{16,24},{24,16},{1,9},{9,1},{17,25},{25,17},{2,10},{10... | collective-permute-start | bytes 448520 | tf_op jit(solution)/shard_map/ppermute | solution.py:925
  342.1 17.6 %collective-permute-start.9 = (bf16[2336,128]{1,0:T(8,128)(2,1)}, bf16[2336,128]{1,0:T(8,128)(2,1)S(1)}, u32[]{:S(2)}, u32[]{:S(2)}) collective-permute-start(bf16[2336,128]{1,0:T(8,128)(2,1)} %bitcast.25.rest_0_), channel_id=1, source_target_pairs={{0,6},{1,7},{2,4},{3,5},{4,2},{5,3},{6,0},{7,1},{8,14},{9,15},{10,... | collective-permute-start | bytes 1794056 | tf_op jit(solution)/shard_map/ppermute | solution.py:925
  342.7 26.6 %collective-permute-start.8 = (bf16[2336,128]{1,0:T(8,128)(2,1)}, bf16[2336,128]{1,0:T(8,128)(2,1)S(1)}, u32[]{:S(2)}, u32[]{:S(2)}) collective-permute-start(bf16[2336,128]{1,0:T(8,128)(2,1)} %bitcast.25.rest_0_), channel_id=1, source_target_pairs={{0,4},{1,5},{2,6},{3,7},{4,0},{5,1},{6,2},{7,3},{8,12},{9,13},{10,... | collective-permute-start | bytes 1794056 | tf_op jit(solution)/shard_map/ppermute | solution.py:925
  344.1 25.4 %collective-permute-start.7 = (bf16[2336,128]{1,0:T(8,128)(2,1)}, bf16[2336,128]{1,0:T(8,128)(2,1)S(1)}, u32[]{:S(2)}, u32[]{:S(2)}) collective-permute-start(bf16[2336,128]{1,0:T(8,128)(2,1)} %bitcast.25.rest_0_), channel_id=1, source_target_pairs={{0,2},{1,3},{2,0},{3,1},{4,6},{5,7},{6,4},{7,5},{8,10},{9,11},{10,... | collective-permute-start | bytes 1794056 | tf_op jit(solution)/shard_map/ppermute | solution.py:925
  369.5 3.0 collective-permute-start.10
  369.5 3.0 collective-permute-start.11
  370.0 4.1 %collective-permute-start.12 = (bf16[2336,128]{1,0:T(8,128)(2,1)S(1)}, bf16[2336,128]{1,0:T(8,128)(2,1)S(1)}, u32[]{:S(2)}, u32[]{:S(2)}) collective-permute-start(bf16[2336,128]{1,0:T(8,128)(2,1)S(1)} %collective-permute-done.8.rest_2_), channel_id=1, source_target_pairs={{0,1},{1,0},{2,3},{3,2},{4,5},{5,4},{6,7},{7,6},{8,9},{9,8},{10,11... | collective-permute-start | bytes 1794056 | tf_op jit(solution)/shard_map/ppermute | solution.py:911
  370.0 4.9 %collective-permute-start.13 = (bf16[2336,128]{1,0:T(8,128)(2,1)S(1)}, bf16[2336,128]{1,0:T(8,128)(2,1)}, u32[]{:S(2)}, u32[]{:S(2)}) collective-permute-start(bf16[2336,128]{1,0:T(8,128)(2,1)S(1)} %collective-permute-done.9.rest_3_), channel_id=1, source_target_pairs={{0,1},{1,0},{2,3},{3,2},{4,5},{5,4},{6,7},{7,6},{8,9},{9,8},{10,11... | collective-permute-start | bytes 1794056 | tf_op jit(solution)/shard_map/ppermute | solution.py:911
  (22 other events, 93.3 us)
Sparse Core Ops, SparseCore 0:
  172.7 120.7 reduce-scatter.2
  297.4 71.7 reduce-scatter.4

commit v5 on v4

--- a/solution.py
+++ b/solution.py
@@ -925,16 +925,26 @@
     return lax.ppermute(value, axis, [(j, j ^ d) for j in range(lax.axis_size(axis))])
 
 
-def gather_over_dp(part, beside):
+def sum_over_dp(share):
+    groups = lax.axis_size("dp")
+    me = lax.axis_index("dp")
+    blocks = share.reshape(groups, share.shape[0] // groups, -1)
+    total = lax.dynamic_index_in_dim(blocks, me, 0, keepdims=False).astype(F32)
+    for d in range(1, groups):
+        send = lax.dynamic_index_in_dim(blocks, me ^ d, 0, keepdims=False)
+        total = total + xor_permute(send, "dp", d).astype(F32)
+    return total.astype(BF16)
+
+
+def gather_over_dp(part):
     groups = lax.axis_size("dp")
     me = lax.axis_index("dp")
     parts = [part] + [xor_permute(part, "dp", d) for d in range(1, groups)]
-    parts, beside = lax.optimization_barrier((parts, beside))
     parts = jnp.stack(parts)
     for bit in range((groups - 1).bit_length()):
         split = parts.reshape(-1, 2, 1 << bit, *part.shape)
         parts = jnp.where((me >> bit) & 1 == 1, split[:, ::-1], split)
-    return parts.reshape(-1, part.shape[1]), beside
+    return parts.reshape(-1, part.shape[1])
 
 
 def on_device(
@@ -1014,15 +1024,14 @@
     share_two = sum_over_chips(last)
     fout = expert_out_of(act_a, late_act, w_out, share, peers)
     share_two, fout, late_gp, late_res = hold((share_two, fout, gp_b, gres))
-    blocks = jnp.concatenate([share_one, share_two], axis=0).reshape(shards, -1, LANES)
-    blocks = lax.all_to_all(blocks, "dp", 0, 0, tiled=True)
+    fback = exchange(fout.reshape(2 * toks, width))
+    part = sum_over_dp(jnp.concatenate([share_one, share_two], axis=0))
     late = late_grads((xt_a, xt_b), (gp_a, late_gp), share)
     grad_tokens = grad_tokens_of(tokens, late_res, ga, w_qkv, grads)
-    blocks, fout, late, grad_tokens, early_sum = hold(
-        (blocks, fout, late, grad_tokens, early_sum)
+    part, fback, late, grad_tokens, early_sum = hold(
+        (part, fback, late, grad_tokens, early_sum)
     )
-    fback = exchange(fout.reshape(2 * toks, width))
-    total, fback = gather_over_dp(sum_blocks(blocks), fback)
+    total = gather_over_dp(part)
     late_sum = lax.psum_scatter(late, "dp", scatter_dimension=0, tiled=True)[0]
     pieces = [total] + [xor_permute(total, "expert", d) for d in range(2, peers, 2)]
     out_tokens = combine(keyn, res, fback)

time: 402 us -> 391 us (0.973)
  waiting for transfers between devices: 66.6 us -> 52.3 us
  starting transfers between devices: 49.4 us -> 58.1 us
  other arithmetic: 10.2 us -> 6.14 us
    ppermute x6 -> x9, starting transfers between devices: 7.94 us -> 21.1 us  [xor_permute(): lax.ppermute(value, axis, [(j, j ^ d) for j in range(lax.axis_size(axis))])]
    ppermute x6 -> x9, waiting for transfers between devices: 45.7 us -> 35.9 us  [xor_permute(): lax.ppermute(value, axis, [(j, j ^ d) for j in range(lax.axis_size(axis))])]
    all_to_all x1 -> x0, waiting for transfers between devices: 8.44 us -> none  [on_device(): blocks = lax.all_to_all(blocks, 'dp', 0, 0, tiled=True)]
    all_to_all x1 -> x0, starting transfers between devices: 5.44 us -> none  [on_device(): blocks = lax.all_to_all(blocks, 'dp', 0, 0, tiled=True)]
  transfers between devices with their start and end apart: 25 -> 27, of which waited for: 13 -> 14; matrix products, arithmetic and copies ran while one was open for 3% -> 2% of each run, Pallas kernels for 59% -> 61%
where the time goes in v5:
time: 391 us; the launch traced here: 386 us
  Pallas kernels  247 us (63%)
  starting transfers between devices  58.1 us (15%)
  waiting for transfers between devices  52.3 us (13%)
  between operations  14.6 us (4%)
  local copies, waits for them, and re-layouts  8.14 us (2%)
  other arithmetic  6.14 us (2%)
    pallas_call x2, Pallas kernels, expert(): pl.pallas_call(expert_kernel, grid=(hidden // wide,), in_specs=[smem(), w...  47.9 us
    pallas_call x3, Pallas kernels, attend_back(): pl.pallas_call(attend_back_kernel, grid=(1,), in_specs=[smem(), whole((1,...  42.7 us
    pallas_call x1, Pallas kernels, attend(): pl.pallas_call(attend_kernel, grid=(PAIRS // 2,), in_specs=[whole((toks,...  41.1 us
    ppermute x9, waiting for transfers between devices, xor_permute(): lax.ppermute(value, axis, [(j, j ^ d) for j in range(lax.axis_size(axis))])  35.9 us
    all_to_all x6, starting transfers between devices, exchange(): lax.all_to_all(rows.reshape(peers, -1, width), 'expert', split_axis=0, co...  26.7 us
    ppermute x9, starting transfers between devices, xor_permute(): lax.ppermute(value, axis, [(j, j ^ d) for j in range(lax.axis_size(axis))])  21.1 us
    pallas_call x2, Pallas kernels, grad_act(): pl.pallas_call(grad_act_kernel, grid=(hidden // wide,), in_specs=[pl.Bloc...  20 us
    pallas_call x1, Pallas kernels, early_grads(): pl.pallas_call(early_grads_kernel, grid=(steps,), in_specs=[whole((width,...  19.6 us
  transfers between devices with their start and end apart: 27, of which 14 were waited for; matrix products, arithmetic and copies ran while one was open for 2% of the time, Pallas kernels for 61%

profile of v5, /device:TPU:0, one launch (start us, length us, event | category | flops | bytes accessed | tf_op | source)
XLA Modules:
  0.0 386.4 jit_solution(17599533266221986868)
XLA Ops:
  7.2 6.9 %place.1 = (s32[1,1024]{1,0:T(1,128)}, s32[1,1024]{1,0:T(1,128)}, bf16[2048,768]{1,0:T(8,128)(2,1)}) custom-call(s32[1,1024]{1,0:T(1,128)} %bitcast.68, bf16[1024,768]{1,0:T(8,128)(2,1)} %cot_ref.3), custom_call_target="tpu_custom_call" | custom-call | flops 5750000128 | tf_op jit(solution)/shard_map/place/pallas_call | solution.py:98
  14.0 5.3 %all-to-all-start.1 = ((bf16[8,256,768]{2,1,0:T(8,128)(2,1)}), bf16[8,256,768]{2,1,0:T(8,128)(2,1)}, u32[]{:S(2)}, u32[]{:S(2)}) async-start(bf16[8,256,768]{2,1,0:T(8,128)(2,1)} %bitcast.43), calls=%async_computation.1 | async-start | bytes 6291456 | tf_op jit(solution)/shard_map/all_to_all | solution.py:899
  20.5 41.1 %attend.1 = (bf16[1024,768]{1,0:T(8,128)(2,1)}, bf16[1024,768]{1,0:T(8,128)(2,1)}, bf16[1024,768]{1,0:T(8,128)(2,1)}, f32[6,2,1024]{2,1,0:T(2,128)}, bf16[768,10...) custom-call(bf16[1024,768]{1,0:T(8,128)(2,1)} %tok_ref.3, ...), custom_call_target="tpu_custom_call" | custom-call | flops 48299999232 | tf_op jit(solution)/shard_map/attend/pallas_call | solution.py:217
  66.1 10.0 %grad_act.3 = (bf16[1024,3072]{1,0:T(8,128)(2,1)}, bf16[768,1024]{1,0:T(8,128)(2,1)}) custom-call(bf16[8,2,128,768]{3,2,1,0:T(8,128)(2,1)} %bitcast.6.g_ref, bf16[1,3072,768]{2,1,0:T(8,128)(2,1)} %wout_ref.5), custom_call_target="tpu_custom_call" | custom-call | flops 8049999872 | tf_op jit(solution)/shard_map/grad_act/pallas_call | solution.py:635
  76.0 10.1 %grad_act.2 = (bf16[1024,3072]{1,0:T(8,128)(2,1)}, bf16[768,1024]{1,0:T(8,128)(2,1)}) custom-call(bf16[8,2,128,768]{3,2,1,0:T(8,128)(2,1)} %bitcast.6.g_ref, bf16[1,3072,768]{2,1,0:T(8,128)(2,1)} %wout_ref.5), custom_call_target="tpu_custom_call" | custom-call | flops 8049999872 | tf_op jit(solution)/shard_map/grad_act/pallas_call | solution.py:635
  91.8 24.0 %expert.3 = (bf16[1024,3072]{1,0:T(8,128)(2,1)}, bf16[1024,3072]{1,0:T(8,128)(2,1)}, bf16[768,1024]{1,0:T(8,128)(2,1)}, bf16[1024,768]{1,0:T(8,128)(2,1)}, f32[16,768]{1,0:T(8,128)}, /*index=5*/f32[8,16]{1,0:T(8,128)}) custom-call(s32[1]{0:T(128)} %bitcast.me_ref, bf16[16,768]{1,0:T(8,128)(2,1)} %bitcast.66, f32[8,16]{1,0:T(8,128)} %emb_ref.3, ...), custom_call_target="tpu_custom_call" | custom-call | flops 26449999872 | tf_op jit(solution)/shard_map/expert/pallas_call | solution.py:511
  121.5 23.9 %expert.2 = (bf16[1024,3072]{1,0:T(8,128)(2,1)}, bf16[1024,3072]{1,0:T(8,128)(2,1)}, bf16[768,1024]{1,0:T(8,128)(2,1)}, bf16[1024,768]{1,0:T(8,128)(2,1)}, f32[16,768]{1,0:T(8,128)}, /*index=5*/f32[8,16]{1,0:T(8,128)}) custom-call(s32[1]{0:T(128)} %bitcast.me_ref, bf16[16,768]{1,0:T(8,128)(2,1)} %bitcast.67, f32[8,16]{1,0:T(8,128)} %emb_ref.3, ...), custom_call_target="tpu_custom_call" | custom-call | flops 26449999872 | tf_op jit(solution)/shard_map/expert/pallas_call | solution.py:511
  152.7 19.6 %early_grads.1 = bf16[4,1024,768]{2,1,0:T(8,128)(2,1)} custom-call(bf16[768,1024]{1,0:T(8,128)(2,1)} %get-tuple-element.112.gta_ref, bf16[768,1024]{1,0:T(8,128)(2,1)} %get-tuple-element.113.gtb_ref, bf16[768,1024]{1,0:T(8,128)(2,1)} %get-tuple-element.114.xta_ref, bf16[768,1024]{1,0:T(8,128)(2,1)} %get-tuple-element.115.xtb_ref, ...), custom_call_target="tpu_custom_call" | custom-call | flops 11500000256 | tf_op jit(solution)/shard_map/early_grads/pallas_call | solution.py:573
  173.2 10.1 %combine_back.1 = (f32[1024,768]{1,0:T(8,128)}, bf16[1024,768]{1,0:T(8,128)(2,1)}, f32[1,768]{1,0:T(1,128)}) custom-call(s32[1,1024]{1,0:T(1,128)} %get-tuple-element.91.keyr_ref, f32[1024,768]{1,0:T(8,128)} %get-tuple-element.97.res_ref, bf16[1024,768]{1,0:T(8,128)(2,1)} %cot_ref.3, f32[1,768]{1,0:T(1,128)} %reshape.85.gf_ref, bf16[1024,768]{1,0:T(8,128)(2,1)} %bitcast.47, ...), custom_call_target="tpu_custom_call" | custom-call | flops 115000000512 | tf_op jit(solution)/shard_map/combine_back/pallas_call | solution.py:753
  183.3 14.3 %attend_back.3 = (bf16[4,768,128]{2,1,0:T(8,128)(2,1)}, bf16[4,768,128]{2,1,0:T(8,128)(2,1)}, bf16[3,1024,256]{2,1,0:T(8,128)(2,1)}) custom-call(s32[1]{0:T(128)S(6)} %and.13.core_ref, s32[1,1024]{1,0:T(1,128)} %segr_ref.7, bf16[1024,768]{1,0:T(8,128)(2,1)} %get-tuple-element.92.q_ref, bf16[1024,768]{1,0:T(8,128)(2,1)} %get-tuple-element.93.k_ref, ...), custom_call_target="tpu_custom_call" | custom-call | flops 2300000000 | tf_op jit(solution)/shard_map/attend_back/pallas_call | solution.py:348
  198.1 14.1 %attend_back.4 = (bf16[4,768,128]{2,1,0:T(8,128)(2,1)}, bf16[4,768,128]{2,1,0:T(8,128)(2,1)}, bf16[3,1024,256]{2,1,0:T(8,128)(2,1)}) custom-call(s32[1]{0:T(128)S(6)} %and.13.core_ref, s32[1,1024]{1,0:T(1,128)} %segr_ref.7, bf16[1024,768]{1,0:T(8,128)(2,1)} %get-tuple-element.92.q_ref, bf16[1024,768]{1,0:T(8,128)(2,1)} %get-tuple-element.93.k_ref, ...), custom_call_target="tpu_custom_call" | custom-call | flops 2300000000 | tf_op jit(solution)/shard_map/attend_back/pallas_call | solution.py:348
  221.8 14.2 %attend_back.5 = (bf16[4,768,128]{2,1,0:T(8,128)(2,1)}, bf16[4,768,128]{2,1,0:T(8,128)(2,1)}, bf16[3,1024,256]{2,1,0:T(8,128)(2,1)}) custom-call(s32[1]{0:T(128)S(6)} %and.13.core_ref, s32[1,1024]{1,0:T(1,128)} %segr_ref.7, bf16[1024,768]{1,0:T(8,128)(2,1)} %get-tuple-element.92.q_ref, bf16[1024,768]{1,0:T(8,128)(2,1)} %get-tuple-element.93.k_ref, ...), custom_call_target="tpu_custom_call" | custom-call | flops 11500000256 | tf_op jit(solution)/shard_map/attend_back/pallas_call | solution.py:348
  246.1 15.1 %expert_out.1 = bf16[8,2,128,768]{3,2,1,0:T(8,128)(2,1)} custom-call(bf16[1024,3072]{1,0:T(8,128)(2,1)} %get-tuple-element.116.acta_ref, bf16[1024,3072]{1,0:T(8,128)(2,1)} %get-tuple-element.144.actb_ref, bf16[1,3072,768]{2,1,0:T(8,128)(2,1)} %wout_ref.5), custom_call_target="tpu_custom_call" | custom-call | flops 16099999744 | tf_op jit(solution)/shard_map/expert_out/pallas_call | solution.py:678
  270.8 11.6 %late_grads.1 = bf16[4,512,768]{2,1,0:T(8,128)(2,1)} custom-call(bf16[768,1024]{1,0:T(8,128)(2,1)} %get-tuple-element.114.xta_ref, bf16[768,1024]{1,0:T(8,128)(2,1)} %get-tuple-element.115.xtb_ref, bf16[1024,3072]{1,0:T(8,128)(2,1)} %get-tuple-element.118.gpa_ref, bf16[1024,3072]{1,0:T(8,128)(2,1)} %get-tuple-element.148.gpb_ref), custom_call_target="tpu_custom_call" | custom-call | flops 11500000256 | tf_op jit(solution)/shard_map/late_grads/pallas_call | solution.py:608
  282.4 9.2 %grad_tokens.1 = f32[1024,768]{1,0:T(8,128)} custom-call(bf16[1024,768]{1,0:T(8,128)(2,1)} %tok_ref.3, f32[1024,768]{1,0:T(8,128)} %get-tuple-element.149.gres_ref, f32[1,768]{1,0:T(1,128)} %reshape.84.ga_ref, bf16[768,2304]{1,0:T(8,128)(2,1)} %w_ref.3, bf16[3,1024,256]{2,1,0:T(8,128)(2,1)} %get-tuple-element.124.rest_0_, ...), custom_call_target="tpu_custom_call" | custom-call | flops 10350000128 | tf_op jit(solution)/shard_map/grad_tokens/pallas_call | solution.py:390
  291.6 5.6 %collective-permute-done.5 = bf16[584,128]{1,0:T(8,128)(2,1)S(1)} collective-permute-done((bf16[584,128]{1,0:T(8,128)(2,1)S(1)}, bf16[584,128]{1,0:T(8,128)(2,1)S(1)}, u32[]{:S(2)}, u32[]{:S(2)}) %collective-permute-start.5) | collective-permute-done | bytes 149536 | tf_op jit(solution)/shard_map/ppermute | solution.py:925
  297.2 6.5 %all-to-all-done.7 = bf16[8,256,768]{2,1,0:T(8,128)(2,1)} async-done(((bf16[8,256,768]{2,1,0:T(8,128)(2,1)}), bf16[8,256,768]{2,1,0:T(8,128)(2,1)}, u32[]{:S(2)}, u32[]{:S(2)}) %all-to-all-start.7) | async-done | bytes 3145760 | tf_op jit(solution)/shard_map/all_to_all | solution.py:899
  308.6 5.5 %collective-permute-done.9 = bf16[584,128]{1,0:T(8,128)(2,1)S(1)} collective-permute-done((bf16[584,128]{1,0:T(8,128)(2,1)S(1)}, bf16[584,128]{1,0:T(8,128)(2,1)S(1)}, u32[]{:S(2)}, u32[]{:S(2)}) %collective-permute-start.9) | collective-permute-done | bytes 149536 | tf_op jit(solution)/shard_map/ppermute | solution.py:925
  314.1 14.3 %collective-permute-done.8 = bf16[584,128]{1,0:T(8,128)(2,1)S(1)} collective-permute-done((bf16[584,128]{1,0:T(8,128)(2,1)S(1)}, bf16[584,128]{1,0:T(8,128)(2,1)S(1)}, u32[]{:S(2)}, u32[]{:S(2)}) %collective-permute-start.8) | collective-permute-done | bytes 149536 | tf_op jit(solution)/shard_map/ppermute | solution.py:925
  328.8 7.5 %collective-permute-start.12 = (bf16[2336,128]{1,0:T(8,128)(2,1)S(1)}, bf16[2336,128]{1,0:T(8,128)(2,1)S(1)}, u32[]{:S(2)}, u32[]{:S(2)}) collective-permute-start(bf16[2336,128]{1,0:T(8,128)(2,1)S(1)} %bitcast.54), channel_id=1, source_target_pairs={{0,6},{1,7},{2,4},{3,5},{4,2},{5,3},{6,0},{7,1},{8,14},{9,15},{10,... | collective-permute-start | bytes 1794056 | tf_op jit(solution)/shard_map/ppermute | solution.py:925
  340.2 7.9 %combine.1 = bf16[1024,768]{1,0:T(8,128)(2,1)} custom-call(s32[1,1024]{1,0:T(1,128)} %get-tuple-element.152.keyn_ref, f32[1024,768]{1,0:T(8,128)} %get-tuple-element.97.res_ref, bf16[2048,768]{1,0:T(8,128)(2,1)} %bitcast.21.rows_ref), custom_call_target="tpu_custom_call" | custom-call | flops 5750000128 | tf_op jit(solution)/shard_map/combine/pallas_call | solution.py:782
  350.7 7.2 %collective-permute-done.11.rest_2_ = bf16[2336,128]{1,0:T(8,128)(2,1)S(1)} collective-permute-done((bf16[2336,128]{1,0:T(8,128)(2,1)S(1)}, bf16[2336,128]{1,0:T(8,128)(2,1)S(1)}, u32[]{:S(2)}, u32[]{:S(2)}) %collective-permute-start.11) | collective-permute-done | bytes 598048 | tf_op jit(solution)/shard_map/ppermute | solution.py:925
  364.1 9.7 %shared_sums.1 = (f32[768,2304]{1,0:T(8,128)}, f32[768,768]{1,0:T(8,128)}, f32[768]{0:T(1024)}, f32[768]{0:T(1024)}, f32[16,768]{1,0:T(8,128)}, /*index=5*/f32[8,16]{1,0:T(8,128)}) custom-call(s32[1]{0:T(128)} %bitcast.me_ref, bf16[768,2304]{1,0:T(8,128)(2,1)} %w_ref.3, f32[1,768]{1,0:T(1,128)} %reshape.84.ga_ref, bf16[2336,128]{1,0:T(8,128)(2,1)} %bitcast.58, ...), custom_call_target="tpu_custom_call" | custom-call | flops 2300000000 | tf_op jit(solution)/shard_map/shared_sums/pallas_call | solution.py:864
  373.9 5.5 %expert_sums.1 = (f32[1,768,768]{2,1,0:T(8,128)}, f32[1,768,768]{2,1,0:T(8,128)}) custom-call(bf16[1024,768]{1,0:T(8,128)(2,1)} %bitcast.64, bf16[512,768]{1,0:T(8,128)(2,1)} %bitcast.65), custom_call_target="tpu_custom_call" | custom-call | flops 3449999872 | tf_op jit(solution)/shard_map/expert_sums/pallas_call | solution.py:702
  (115 shorter events, 72.7 us)
Async XLA Ops:
  14.0 47.6 %all-to-all-start.1 = ((bf16[8,256,768]{2,1,0:T(8,128)(2,1)}), bf16[8,256,768]{2,1,0:T(8,128)(2,1)}, u32[]{:S(2)}, u32[]{:S(2)}) async-start(bf16[8,256,768]{2,1,0:T(8,128)(2,1)} %bitcast.43), calls=%async_computation.1 | async-start | bytes 6291456 | tf_op jit(solution)/shard_map/all_to_all | solution.py:899
  61.6 25.5 %all-to-all-start = ((bf16[8,128,768]{2,1,0:T(8,128)(2,1)}), bf16[8,128,768]{2,1,0:T(8,128)(2,1)S(1)}, u32[]{:S(2)}, u32[]{:S(2)}) async-start(bf16[8,128,768]{2,1,0:T(8,128)(2,1)} %bitcast.52), calls=%async_computation | async-start | bytes 3145728 | tf_op jit(solution)/shard_map/all_to_all | solution.py:899
  88.2 27.6 %all-to-all-start.2 = ((bf16[8,128,768]{2,1,0:T(8,128)(2,1)}), bf16[8,128,768]{2,1,0:T(8,128)(2,1)S(1)}, u32[]{:S(2)}, u32[]{:S(2)}) async-start(bf16[8,128,768]{2,1,0:T(8,128)(2,1)} %bitcast.7), calls=%async_computation.2 | async-start | bytes 3145728 | tf_op jit(solution)/shard_map/all_to_all | solution.py:899
  117.0 28.5 %all-to-all-start.3 = ((bf16[8,128,768]{2,1,0:T(8,128)(2,1)}), bf16[8,128,768]{2,1,0:T(8,128)(2,1)S(1)}, u32[]{:S(2)}, u32[]{:S(2)}) async-start(bf16[8,128,768]{2,1,0:T(8,128)(2,1)} %bitcast.51), calls=%async_computation.3 | async-start | bytes 3145728 | tf_op jit(solution)/shard_map/all_to_all | solution.py:899
  146.6 26.7 %all-to-all-start.4 = ((bf16[8,128,768]{2,1,0:T(8,128)(2,1)}), bf16[8,128,768]{2,1,0:T(8,128)(2,1)}, u32[]{:S(2)}, u32[]{:S(2)}) async-start(bf16[8,128,768]{2,1,0:T(8,128)(2,1)} %bitcast.48), calls=%async_computation.4 | async-start | bytes 3145728 | tf_op jit(solution)/shard_map/all_to_all | solution.py:899
  150.9 152.9 %reduce-scatter.3.cloned.1.call-start = ((), (), s32[]{:S(2)}) async-start(), calls=%async_computation.10 | async-start | bytes 7864320 | tf_op jit(solution)/shard_map/reduce_scatter | solution.py:993
  197.6 17.0 %collective-permute-start = (bf16[4,768,128]{2,1,0:T(8,128)(2,1)}, bf16[4,768,128]{2,1,0:T(8,128)(2,1)S(1)}, u32[]{:S(2)}, u32[]{:S(2)}) collective-permute-start(bf16[4,768,128]{2,1,0:T(8,128)(2,1)} %get-tuple-element.127), channel_id=1, source_target_pairs={{0,1},{1,0},{2,3},{3,2},{4,5},{5,4},{6,7},{7,6},{8,9},{9,8},{10,11... | collective-permute-start | bytes 2359304 | tf_op jit(solution)/shard_map/ppermute | solution.py:911
  217.5 24.4 %all-to-all-start.5 = ((bf16[4,1568,128]{2,1,0:T(8,128)(2,1)}), bf16[4,1568,128]{2,1,0:T(8,128)(2,1)S(1)}, u32[]{:S(2)}, u32[]{:S(2)}) async-start(bf16[4,1568,128]{2,1,0:T(8,128)(2,1)} %pad_maximum_fusion), calls=%async_computation.5 | async-start | bytes 3211264 | tf_op jit(solution)/shard_map/all_to_all | solution.py:920
  242.4 18.8 %all-to-all-start.6 = ((bf16[4,768,128]{2,1,0:T(8,128)(2,1)}), bf16[4,768,128]{2,1,0:T(8,128)(2,1)S(1)}, u32[]{:S(2)}, u32[]{:S(2)}) async-start(bf16[4,768,128]{2,1,0:T(8,128)(2,1)} %add_convert_fusion), calls=%async_computation.6 | async-start | bytes 1572864 | tf_op jit(solution)/shard_map/all_to_all | solution.py:920
  261.3 42.4 %all-to-all-start.7 = ((bf16[8,256,768]{2,1,0:T(8,128)(2,1)}), bf16[8,256,768]{2,1,0:T(8,128)(2,1)}, u32[]{:S(2)}, u32[]{:S(2)}) async-start(bf16[8,256,768]{2,1,0:T(8,128)(2,1)} %bitcast.42), calls=%async_computation.7 | async-start | bytes 6291456 | tf_op jit(solution)/shard_map/all_to_all | solution.py:899
  265.8 108.0 %reduce-scatter.5.cloned.1.call-start = ((), (), s32[]{:S(2)}) async-start(), calls=%async_computation.11 | async-start | bytes 3932160 | tf_op jit(solution)/shard_map/reduce_scatter | solution.py:1035
  266.0 25.6 %collective-permute-start.4 = (bf16[584,128]{1,0:T(8,128)(2,1)S(1)}, bf16[584,128]{1,0:T(8,128)(2,1)S(1)}, u32[]{:S(2)}, u32[]{:S(2)}) collective-permute-start(bf16[584,128]{1,0:T(8,128)(2,1)S(1)} %get-tuple-element.172), channel_id=1, source_target_pairs={{0,8},{8,0},{16,24},{24,16},{1,9},{9,1},{17,25},{25,17},{2,10},{10... | collective-permute-start | bytes 448520 | tf_op jit(solution)/shard_map/ppermute | solution.py:925
  268.3 23.3 %collective-permute-start.6 = (bf16[584,128]{1,0:T(8,128)(2,1)S(1)}, bf16[584,128]{1,0:T(8,128)(2,1)S(1)}, u32[]{:S(2)}, u32[]{:S(2)}) collective-permute-start(bf16[584,128]{1,0:T(8,128)(2,1)S(1)} %get-tuple-element.173), channel_id=1, source_target_pairs={{0,24},{8,16},{16,8},{24,0},{1,25},{9,17},{17,9},{25,1},{2,26},{10... | collective-permute-start | bytes 448520 | tf_op jit(solution)/shard_map/ppermute | solution.py:925
  270.8 26.3 %collective-permute-start.5 = (bf16[584,128]{1,0:T(8,128)(2,1)S(1)}, bf16[584,128]{1,0:T(8,128)(2,1)S(1)}, u32[]{:S(2)}, u32[]{:S(2)}) collective-permute-start(bf16[584,128]{1,0:T(8,128)(2,1)S(1)} %get-tuple-element.174), channel_id=1, source_target_pairs={{0,16},{8,24},{16,0},{24,8},{1,17},{9,25},{17,1},{25,9},{2,18},{10... | collective-permute-start | bytes 448520 | tf_op jit(solution)/shard_map/ppermute | solution.py:925
  303.8 10.4 %collective-permute-start.9 = (bf16[584,128]{1,0:T(8,128)(2,1)S(1)}, bf16[584,128]{1,0:T(8,128)(2,1)S(1)}, u32[]{:S(2)}, u32[]{:S(2)}) collective-permute-start(bf16[584,128]{1,0:T(8,128)(2,1)S(1)} %fusion.3), channel_id=1, source_target_pairs={{0,24},{8,16},{16,8},{24,0},{1,25},{9,17},{17,9},{25,1},{2,26},{10... | collective-permute-start | bytes 448520 | tf_op jit(solution)/shard_map/ppermute | solution.py:925
  308.0 20.4 %collective-permute-start.8 = (bf16[584,128]{1,0:T(8,128)(2,1)S(1)}, bf16[584,128]{1,0:T(8,128)(2,1)S(1)}, u32[]{:S(2)}, u32[]{:S(2)}) collective-permute-start(bf16[584,128]{1,0:T(8,128)(2,1)S(1)} %fusion.3), channel_id=1, source_target_pairs={{0,16},{8,24},{16,0},{24,8},{1,17},{9,25},{17,1},{25,9},{2,18},{10... | collective-permute-start | bytes 448520 | tf_op jit(solution)/shard_map/ppermute | solution.py:925
  308.0 20.4 %collective-permute-start.7 = (bf16[584,128]{1,0:T(8,128)(2,1)S(1)}, bf16[584,128]{1,0:T(8,128)(2,1)S(1)}, u32[]{:S(2)}, u32[]{:S(2)}) collective-permute-start(bf16[584,128]{1,0:T(8,128)(2,1)S(1)} %fusion.3), channel_id=1, source_target_pairs={{0,8},{8,0},{16,24},{24,16},{1,9},{9,1},{17,25},{25,17},{2,10},{10... | collective-permute-start | bytes 448520 | tf_op jit(solution)/shard_map/ppermute | solution.py:925
  328.8 21.9 %collective-permute-start.12 = (bf16[2336,128]{1,0:T(8,128)(2,1)S(1)}, bf16[2336,128]{1,0:T(8,128)(2,1)S(1)}, u32[]{:S(2)}, u32[]{:S(2)}) collective-permute-start(bf16[2336,128]{1,0:T(8,128)(2,1)S(1)} %bitcast.54), channel_id=1, source_target_pairs={{0,6},{1,7},{2,4},{3,5},{4,2},{5,3},{6,0},{7,1},{8,14},{9,15},{10,... | collective-permute-start | bytes 1794056 | tf_op jit(solution)/shard_map/ppermute | solution.py:925
  336.3 21.7 %collective-permute-start.11 = (bf16[2336,128]{1,0:T(8,128)(2,1)S(1)}, bf16[2336,128]{1,0:T(8,128)(2,1)S(1)}, u32[]{:S(2)}, u32[]{:S(2)}) collective-permute-start(bf16[2336,128]{1,0:T(8,128)(2,1)S(1)} %bitcast.55), channel_id=1, source_target_pairs={{0,4},{1,5},{2,6},{3,7},{4,0},{5,1},{6,2},{7,3},{8,12},{9,13},{10,... | collective-permute-start | bytes 1794056 | tf_op jit(solution)/shard_map/ppermute | solution.py:925
  340.2 18.5 %collective-permute-start.10 = (bf16[2336,128]{1,0:T(8,128)(2,1)S(1)}, bf16[2336,128]{1,0:T(8,128)(2,1)}, u32[]{:S(2)}, u32[]{:S(2)}) collective-permute-start(bf16[2336,128]{1,0:T(8,128)(2,1)S(1)} %bitcast.56), channel_id=1, source_target_pairs={{0,2},{1,3},{2,0},{3,1},{4,6},{5,7},{6,4},{7,5},{8,10},{9,11},{10,... | collective-permute-start | bytes 1794056 | tf_op jit(solution)/shard_map/ppermute | solution.py:925
  358.7 2.8 collective-permute-start.13
  358.7 3.6 collective-permute-start.14
  359.2 4.1 %collective-permute-start.15 = (bf16[2336,128]{1,0:T(8,128)(2,1)S(1)}, bf16[2336,128]{1,0:T(8,128)(2,1)S(1)}, u32[]{:S(2)}, u32[]{:S(2)}) collective-permute-start(bf16[2336,128]{1,0:T(8,128)(2,1)S(1)} %collective-permute-done.11.rest_2_), channel_id=1, source_target_pairs={{0,1},{1,0},{2,3},{3,2},{4,5},{5,4},{6,7},{7,6},{8,9},{9,8},{10,11... | collective-permute-start | bytes 1794056 | tf_op jit(solution)/shard_map/ppermute | solution.py:911
  359.2 4.9 %collective-permute-start.16 = (bf16[2336,128]{1,0:T(8,128)(2,1)S(1)}, bf16[2336,128]{1,0:T(8,128)(2,1)}, u32[]{:S(2)}, u32[]{:S(2)}) collective-permute-start(bf16[2336,128]{1,0:T(8,128)(2,1)S(1)} %collective-permute-done.12.rest_3_), channel_id=1, source_target_pairs={{0,1},{1,0},{2,3},{3,2},{4,5},{5,4},{6,7},{7,6},{8,9},{9,8},{10,11... | collective-permute-start | bytes 1794056 | tf_op jit(solution)/shard_map/ppermute | solution.py:911
  (22 other events, 117.8 us)
Sparse Core Ops, SparseCore 0:
  172.5 120.8 reduce-scatter.2
  303.9 64.7 reduce-scatter.4

commit v6 on v5

--- a/solution.py
+++ b/solution.py
@@ -167,7 +167,7 @@
             bias_ref[i, :, : high - low] = jnp.where((keys <= queries) & same, 0.0, MASK_VALUE)
         x = tok_ref[...].astype(F32)
         inv = lax.rsqrt(jnp.mean(x * x, axis=1, keepdims=True) + EPSILON)
-        attn_ref[...] = (x * inv * ga_ref[...]).astype(BF16)
+        attn_ref[...] = (x * inv * ga_ref[...].reshape(1, width)).astype(BF16)
 
     attn_in = attn_ref[...]
     q_ref[...] = mm(attn_in, wq_ref[...]).astype(BF16)
@@ -201,7 +201,7 @@
         res = tok_ref[...].astype(F32) + mm(mix_ref[...], wo_ref[...])
         res_ref[...] = res
         inv = lax.rsqrt(jnp.mean(res * res, axis=1, keepdims=True) + EPSILON)
-        ffn_in = (res * inv * gf_ref[...]).astype(BF16)
+        ffn_in = (res * inv * gf_ref[...].reshape(1, width)).astype(BF16)
         dispatch(keyr_ref[...], ffn_in, (xa_ref, xb_ref))
 
 
@@ -223,8 +223,8 @@
             whole((1, toks)),
             *weights,
             whole((width, width)),
-            whole((1, width)),
-            whole((1, width)),
+            whole((width,)),
+            whole((width,)),
         ],
         out_specs=[
             pair_cols,
@@ -379,7 +379,7 @@
     *g_refs, out_ref = rest
     grads = [ref[part] for part in range(3) for ref in g_refs]
     dy = mm(jnp.concatenate(grads, axis=1), w_ref[...], NT)
-    dx, _ = norm_back(tok_ref[...].astype(F32), ga_ref[...], dy)
+    dx, _ = norm_back(tok_ref[...].astype(F32), ga_ref[...].reshape(1, dy.shape[1]), dy)
     out_ref[...] = gres_ref[...] + dx
 
 
@@ -390,7 +390,7 @@
     return pl.pallas_call(
         grad_tokens_kernel,
         grid=(toks // rows,),
-        in_specs=[tile, tile, whole((1, width)), whole(w_qkv.shape)]
+        in_specs=[tile, tile, whole((width,)), whole(w_qkv.shape)]
         + [pl.BlockSpec((3, rows, 2 * PAIR), lambda i: (0, i, 0))] * len(grads),
         out_specs=tile,
         out_shape=jax.ShapeDtypeStruct((toks, width), F32),
@@ -688,35 +688,48 @@
     )(acta, actb, w_out)
 
 
-def expert_sums_kernel(early_ref, late_ref, win_ref, wout_ref):
-    width = wout_ref.shape[2]
-    third = width // 3
-    win_ref[0, :third] = early_ref[width:].astype(F32)
-    win_ref[0, third:] = late_ref[...].astype(F32)
-    wout_ref[0] = early_ref[:width].astype(F32).T
-
-
-def expert_sums(early, late):
+def early_sums_kernel(early_ref, wout_ref):
+    wout_ref[0] = early_ref[...].astype(F32).T
+
+
+def early_sums(early):
     share = early.shape[1]
     width = early.shape[0] * 3 // 4
-    return pl.pallas_call(
-        expert_sums_kernel,
-        grid=(share // LANES,),
+    wide = 2 * LANES if share % (2 * LANES) == 0 else LANES
+    return pl.pallas_call(
+        early_sums_kernel,
+        grid=(share // wide,),
+        in_specs=[pl.BlockSpec((width, wide), lambda k: (0, k))],
+        out_specs=pl.BlockSpec((1, wide, width), lambda k: (0, k, 0)),
+        out_shape=jax.ShapeDtypeStruct((1, share, width), F32),
+        compiler_params=params(),
+        cost_estimate=cost(2),
+        name="early_sums",
+    )(early)
+
+
+def late_sums_kernel(early_ref, late_ref, win_ref):
+    third = early_ref.shape[0]
+    win_ref[0, :third] = early_ref[...].astype(F32)
+    win_ref[0, third:] = late_ref[...].astype(F32)
+
+
+def late_sums(early, late):
+    left, share = late.shape
+    third = left // 2
+    wide = 2 * LANES if share % (2 * LANES) == 0 else LANES
+    return pl.pallas_call(
+        late_sums_kernel,
+        grid=(share // wide,),
         in_specs=[
-            pl.BlockSpec((early.shape[0], LANES), lambda k: (0, k)),
-            pl.BlockSpec((late.shape[0], LANES), lambda k: (0, k)),
-        ],
-        out_specs=[
-            pl.BlockSpec((1, width, LANES), lambda k: (0, 0, k)),
-            pl.BlockSpec((1, LANES, width), lambda k: (0, k, 0)),
-        ],
-        out_shape=[
-            jax.ShapeDtypeStruct((1, width, share), F32),
-            jax.ShapeDtypeStruct((1, share, width), F32),
-        ],
-        compiler_params=params(),
-        cost_estimate=cost(3),
-        name="expert_sums",
+            pl.BlockSpec((third, wide), lambda k: (3, k)),
+            pl.BlockSpec((left, wide), lambda k: (0, k)),
+        ],
+        out_specs=pl.BlockSpec((1, third + left, wide), lambda k: (0, 0, k)),
+        out_shape=jax.ShapeDtypeStruct((1, third + left, share), F32),
+        compiler_params=params(),
+        cost_estimate=cost(2),
+        name="late_sums",
     )(early, late)
 
 
@@ -740,7 +753,7 @@
     def _():
         gain_ref[...] = jnp.zeros_like(gain_ref)
 
-    dx, dgain = norm_back(res_ref[...], gf_ref[...], dy)
+    dx, dgain = norm_back(res_ref[...], gf_ref[...].reshape(1, dy.shape[1]), dy)
     gain_ref[...] += dgain
     grad = cot_ref[...].astype(F32) + dx
     gres_ref[...] = grad
@@ -757,7 +770,7 @@
             pl.BlockSpec((1, QB), lambda i: (0, i)),
             tile,
             tile,
-            whole((1, width)),
+            whole((width,)),
             *[whole(r.shape) for r in rows],
         ],
         out_specs=[tile, tile, whole((1, width))],
@@ -839,7 +852,9 @@
     folded = jnp.zeros((PAIR, LANES), F32)
     for at in range(0, qkv_ref.shape[1], LANES):
         folded += qkv_ref[:, at : at + LANES] * w_ref[:, at : at + LANES].astype(F32)
-    gain = jnp.sum(folded.T, axis=0, keepdims=True) / ga_ref[...]
+    gain = jnp.sum(folded.T, axis=0, keepdims=True) / ga_ref[pl.ds(pl.multiple_of(i * PAIR, PAIR), PAIR)].reshape(
+        1, PAIR
+    )
     gain_ref[pl.ds(pl.multiple_of(i * PAIR, PAIR), PAIR)] = gain[0]
 
     @pl.when(i == 0)
@@ -860,11 +875,10 @@
 def shared_sums(me, blocks, rows, extra, w_qkv, ga, experts, rdim):
     width = w_qkv.shape[0]
     count = len(blocks) // 2
-    lanes = pl.BlockSpec((1, PAIR), lambda i: (0, i))
     return pl.pallas_call(
         functools.partial(shared_sums_kernel, count, experts, rows, extra),
         grid=(width // PAIR,),
-        in_specs=[smem(), pl.BlockSpec((PAIR, 3 * width), lambda i: (i, 0)), lanes]
+        in_specs=[smem(), pl.BlockSpec((PAIR, 3 * width), lambda i: (i, 0)), whole((width,))]
         + [pl.BlockSpec(memory_space=pl.ANY)] * (2 * count),
         out_specs=[
             pl.BlockSpec((PAIR, 3 * width), lambda i: (i, 0)),
@@ -969,7 +983,7 @@
     share = w_in.shape[2] // shards
     me = lax.axis_index("expert").astype(I32).reshape(1)
     core = me & 1
-    ga, gf = gain_attn.reshape(1, width), gain_ffn.reshape(1, width)
+    ga, gf = gain_attn, gain_ffn
     segr = segments.reshape(1, toks)
     wrt = w_router.T
     hold = lax.optimization_barrier
@@ -1035,13 +1049,14 @@
     late_sum = lax.psum_scatter(late, "dp", scatter_dimension=0, tiled=True)[0]
     pieces = [total] + [xor_permute(total, "expert", d) for d in range(2, peers, 2)]
     out_tokens = combine(keyn, res, fback)
-    pieces, out_tokens = hold((pieces, out_tokens))
+    grad_w_out = early_sums(early_sum)
+    pieces, out_tokens, grad_w_out = hold((pieces, out_tokens, grad_w_out))
     blocks = pieces + [swap_cores(piece) for piece in pieces]
     grad_w_qkv, grad_w_attn_out, grad_gain_attn, grad_gain_ffn, grad_router, grad_embed = (
         shared_sums(me, blocks, rows, extra, w_qkv, ga, experts, rdim)
     )
     grad_w_qkv, late_sum = hold((grad_w_qkv, late_sum))
-    grad_w_in, grad_w_out = expert_sums(early_sum, late_sum)
+    grad_w_in = late_sums(early_sum, late_sum)
     return (
         out_tokens,
         grad_tokens,

time: 391 us -> 388 us (level)
  transfers between devices with their start and end apart: 27 -> 27, of which waited for: 14 -> 13; matrix products, arithmetic and copies ran while one was open for 2% -> 2% of each run, Pallas kernels for 61% -> 62%
where the time goes in v6:
time: 388 us; the launch traced here: 383 us
  Pallas kernels  249 us (64%)
  starting transfers between devices  57.7 us (15%)
  waiting for transfers between devices  48.9 us (13%)
  between operations  14.6 us (4%)
  local copies, waits for them, and re-layouts  6.97 us (2%)
  other arithmetic  6.14 us (2%)
    pallas_call x2, Pallas kernels, expert(): pl.pallas_call(expert_kernel, grid=(hidden // wide,), in_specs=[smem(), w...  47.9 us
    pallas_call x3, Pallas kernels, attend_back(): pl.pallas_call(attend_back_kernel, grid=(1,), in_specs=[smem(), whole((1,...  42.7 us
    pallas_call x1, Pallas kernels, attend(): pl.pallas_call(attend_kernel, grid=(PAIRS // 2,), in_specs=[whole((toks,...  41.2 us
    ppermute x9, waiting for transfers between devices, xor_permute(): lax.ppermute(value, axis, [(j, j ^ d) for j in range(lax.axis_size(axis))])  32.4 us
    all_to_all x6, starting transfers between devices, exchange(): lax.all_to_all(rows.reshape(peers, -1, width), 'expert', split_axis=0, co...  26.5 us
    ppermute x9, starting transfers between devices, xor_permute(): lax.ppermute(value, axis, [(j, j ^ d) for j in range(lax.axis_size(axis))])  21 us
    pallas_call x2, Pallas kernels, grad_act(): pl.pallas_call(grad_act_kernel, grid=(hidden // wide,), in_specs=[pl.Bloc...  20 us
    pallas_call x1, Pallas kernels, early_grads(): pl.pallas_call(early_grads_kernel, grid=(steps,), in_specs=[whole((width,...  19.6 us
  transfers between devices with their start and end apart: 27, of which 13 were waited for; matrix products, arithmetic and copies ran while one was open for 2% of the time, Pallas kernels for 62%

profile of v6, /device:TPU:0, one launch (start us, length us, event | category | flops | bytes accessed | tf_op | source)
XLA Modules:
  0.0 383.1 jit_solution(8058990319240543807)
XLA Ops:
  7.2 6.9 %place.1 = (s32[1,1024]{1,0:T(1,128)}, s32[1,1024]{1,0:T(1,128)}, bf16[2048,768]{1,0:T(8,128)(2,1)}) custom-call(s32[1,1024]{1,0:T(1,128)} %bitcast.69, bf16[1024,768]{1,0:T(8,128)(2,1)} %cot_ref.3), custom_call_target="tpu_custom_call" | custom-call | flops 5750000128 | tf_op jit(solution)/shard_map/place/pallas_call | solution.py:98
  14.0 5.2 %all-to-all-start.1 = ((bf16[8,256,768]{2,1,0:T(8,128)(2,1)}), bf16[8,256,768]{2,1,0:T(8,128)(2,1)}, u32[]{:S(2)}, u32[]{:S(2)}) async-start(bf16[8,256,768]{2,1,0:T(8,128)(2,1)} %bitcast.43), calls=%async_computation.1 | async-start | bytes 6291456 | tf_op jit(solution)/shard_map/all_to_all | solution.py:913
  19.2 41.2 %attend.1 = (bf16[1024,768]{1,0:T(8,128)(2,1)}, bf16[1024,768]{1,0:T(8,128)(2,1)}, bf16[1024,768]{1,0:T(8,128)(2,1)}, f32[6,2,1024]{2,1,0:T(2,128)}, bf16[768,10...) custom-call(bf16[1024,768]{1,0:T(8,128)(2,1)} %tok_ref.3, ...), custom_call_target="tpu_custom_call" | custom-call | flops 48299999232 | tf_op jit(solution)/shard_map/attend/pallas_call | solution.py:217
  64.8 10.0 %grad_act.3 = (bf16[1024,3072]{1,0:T(8,128)(2,1)}, bf16[768,1024]{1,0:T(8,128)(2,1)}) custom-call(bf16[8,2,128,768]{3,2,1,0:T(8,128)(2,1)} %bitcast.6.g_ref, bf16[1,3072,768]{2,1,0:T(8,128)(2,1)} %wout_ref.5), custom_call_target="tpu_custom_call" | custom-call | flops 8049999872 | tf_op jit(solution)/shard_map/grad_act/pallas_call | solution.py:635
  74.7 10.0 %grad_act.2 = (bf16[1024,3072]{1,0:T(8,128)(2,1)}, bf16[768,1024]{1,0:T(8,128)(2,1)}) custom-call(bf16[8,2,128,768]{3,2,1,0:T(8,128)(2,1)} %bitcast.6.g_ref, bf16[1,3072,768]{2,1,0:T(8,128)(2,1)} %wout_ref.5), custom_call_target="tpu_custom_call" | custom-call | flops 8049999872 | tf_op jit(solution)/shard_map/grad_act/pallas_call | solution.py:635
  90.5 24.0 %expert.3 = (bf16[1024,3072]{1,0:T(8,128)(2,1)}, bf16[1024,3072]{1,0:T(8,128)(2,1)}, bf16[768,1024]{1,0:T(8,128)(2,1)}, bf16[1024,768]{1,0:T(8,128)(2,1)}, f32[16,768]{1,0:T(8,128)}, /*index=5*/f32[8,16]{1,0:T(8,128)}) custom-call(s32[1]{0:T(128)} %bitcast.me_ref, bf16[16,768]{1,0:T(8,128)(2,1)} %bitcast.67, f32[8,16]{1,0:T(8,128)} %emb_ref.3, ...), custom_call_target="tpu_custom_call" | custom-call | flops 26449999872 | tf_op jit(solution)/shard_map/expert/pallas_call | solution.py:511
  115.7 4.5 %all-to-all-start.3 = ((bf16[8,128,768]{2,1,0:T(8,128)(2,1)}), bf16[8,128,768]{2,1,0:T(8,128)(2,1)S(1)}, u32[]{:S(2)}, u32[]{:S(2)}) async-start(bf16[8,128,768]{2,1,0:T(8,128)(2,1)} %bitcast.51), calls=%async_computation.3 | async-start | bytes 3145728 | tf_op jit(solution)/shard_map/all_to_all | solution.py:913
  120.3 23.9 %expert.2 = (bf16[1024,3072]{1,0:T(8,128)(2,1)}, bf16[1024,3072]{1,0:T(8,128)(2,1)}, bf16[768,1024]{1,0:T(8,128)(2,1)}, bf16[1024,768]{1,0:T(8,128)(2,1)}, f32[16,768]{1,0:T(8,128)}, /*index=5*/f32[8,16]{1,0:T(8,128)}) custom-call(s32[1]{0:T(128)} %bitcast.me_ref, bf16[16,768]{1,0:T(8,128)(2,1)} %bitcast.68, f32[8,16]{1,0:T(8,128)} %emb_ref.3, ...), custom_call_target="tpu_custom_call" | custom-call | flops 26449999872 | tf_op jit(solution)/shard_map/expert/pallas_call | solution.py:511
  151.5 19.6 %early_grads.1 = bf16[4,1024,768]{2,1,0:T(8,128)(2,1)} custom-call(bf16[768,1024]{1,0:T(8,128)(2,1)} %get-tuple-element.111.gta_ref, bf16[768,1024]{1,0:T(8,128)(2,1)} %get-tuple-element.112.gtb_ref, bf16[768,1024]{1,0:T(8,128)(2,1)} %get-tuple-element.113.xta_ref, bf16[768,1024]{1,0:T(8,128)(2,1)} %get-tuple-element.114.xtb_ref, ...), custom_call_target="tpu_custom_call" | custom-call | flops 11500000256 | tf_op jit(solution)/shard_map/early_grads/pallas_call | solution.py:573
  172.0 10.1 %combine_back.1 = (f32[1024,768]{1,0:T(8,128)}, bf16[1024,768]{1,0:T(8,128)(2,1)}, f32[1,768]{1,0:T(1,128)}) custom-call(s32[1,1024]{1,0:T(1,128)} %get-tuple-element.90.keyr_ref, f32[1024,768]{1,0:T(8,128)} %get-tuple-element.96.res_ref, bf16[1024,768]{1,0:T(8,128)(2,1)} %cot_ref.3, f32[768]{0:T(1024)} %gf_ref.3, bf16[1024,768]{1,0:T(8,128)(2,1)} %bitcast.47, ...), custom_call_target="tpu_custom_call" | custom-call | flops 115000000512 | tf_op jit(solution)/shard_map/combine_back/pallas_call | solution.py:766
  182.1 14.3 %attend_back.3 = (bf16[4,768,128]{2,1,0:T(8,128)(2,1)}, bf16[4,768,128]{2,1,0:T(8,128)(2,1)}, bf16[3,1024,256]{2,1,0:T(8,128)(2,1)}) custom-call(s32[1]{0:T(128)S(6)} %and.13.core_ref, s32[1,1024]{1,0:T(1,128)} %segr_ref.7, bf16[1024,768]{1,0:T(8,128)(2,1)} %get-tuple-element.91.q_ref, bf16[1024,768]{1,0:T(8,128)(2,1)} %get-tuple-element.92.k_ref, ...), custom_call_target="tpu_custom_call" | custom-call | flops 2300000000 | tf_op jit(solution)/shard_map/attend_back/pallas_call | solution.py:348
  196.9 14.1 %attend_back.4 = (bf16[4,768,128]{2,1,0:T(8,128)(2,1)}, bf16[4,768,128]{2,1,0:T(8,128)(2,1)}, bf16[3,1024,256]{2,1,0:T(8,128)(2,1)}) custom-call(s32[1]{0:T(128)S(6)} %and.13.core_ref, s32[1,1024]{1,0:T(1,128)} %segr_ref.7, bf16[1024,768]{1,0:T(8,128)(2,1)} %get-tuple-element.91.q_ref, bf16[1024,768]{1,0:T(8,128)(2,1)} %get-tuple-element.92.k_ref, ...), custom_call_target="tpu_custom_call" | custom-call | flops 2300000000 | tf_op jit(solution)/shard_map/attend_back/pallas_call | solution.py:348
  220.7 14.2 %attend_back.5 = (bf16[4,768,128]{2,1,0:T(8,128)(2,1)}, bf16[4,768,128]{2,1,0:T(8,128)(2,1)}, bf16[3,1024,256]{2,1,0:T(8,128)(2,1)}) custom-call(s32[1]{0:T(128)S(6)} %and.13.core_ref, s32[1,1024]{1,0:T(1,128)} %segr_ref.7, bf16[1024,768]{1,0:T(8,128)(2,1)} %get-tuple-element.91.q_ref, bf16[1024,768]{1,0:T(8,128)(2,1)} %get-tuple-element.92.k_ref, ...), custom_call_target="tpu_custom_call" | custom-call | flops 11500000256 | tf_op jit(solution)/shard_map/attend_back/pallas_call | solution.py:348
  244.9 15.1 %expert_out.1 = bf16[8,2,128,768]{3,2,1,0:T(8,128)(2,1)} custom-call(bf16[1024,3072]{1,0:T(8,128)(2,1)} %get-tuple-element.115.acta_ref, bf16[1024,3072]{1,0:T(8,128)(2,1)} %get-tuple-element.143.actb_ref, bf16[1,3072,768]{2,1,0:T(8,128)(2,1)} %wout_ref.5), custom_call_target="tpu_custom_call" | custom-call | flops 16099999744 | tf_op jit(solution)/shard_map/expert_out/pallas_call | solution.py:678
  269.6 11.6 %late_grads.1 = bf16[4,512,768]{2,1,0:T(8,128)(2,1)} custom-call(bf16[768,1024]{1,0:T(8,128)(2,1)} %get-tuple-element.113.xta_ref, bf16[768,1024]{1,0:T(8,128)(2,1)} %get-tuple-element.114.xtb_ref, bf16[1024,3072]{1,0:T(8,128)(2,1)} %get-tuple-element.117.gpa_ref, bf16[1024,3072]{1,0:T(8,128)(2,1)} %get-tuple-element.147.gpb_ref), custom_call_target="tpu_custom_call" | custom-call | flops 11500000256 | tf_op jit(solution)/shard_map/late_grads/pallas_call | solution.py:608
  281.1 9.2 %grad_tokens.1 = f32[1024,768]{1,0:T(8,128)} custom-call(bf16[1024,768]{1,0:T(8,128)(2,1)} %tok_ref.3, f32[1024,768]{1,0:T(8,128)} %get-tuple-element.148.gres_ref, f32[768]{0:T(1024)} %ga_ref.5, bf16[768,2304]{1,0:T(8,128)(2,1)} %w_ref.3, bf16[3,1024,256]{2,1,0:T(8,128)(2,1)} %get-tuple-element.123.rest_0_, ...), custom_call_target="tpu_custom_call" | custom-call | flops 10350000128 | tf_op jit(solution)/shard_map/grad_tokens/pallas_call | solution.py:390
  290.4 5.5 %collective-permute-done.5 = bf16[584,128]{1,0:T(8,128)(2,1)S(1)} collective-permute-done((bf16[584,128]{1,0:T(8,128)(2,1)S(1)}, bf16[584,128]{1,0:T(8,128)(2,1)S(1)}, u32[]{:S(2)}, u32[]{:S(2)}) %collective-permute-start.5) | collective-permute-done | bytes 149536 | tf_op jit(solution)/shard_map/ppermute | solution.py:939
  295.9 6.6 %all-to-all-done.7 = bf16[8,256,768]{2,1,0:T(8,128)(2,1)} async-done(((bf16[8,256,768]{2,1,0:T(8,128)(2,1)}), bf16[8,256,768]{2,1,0:T(8,128)(2,1)}, u32[]{:S(2)}, u32[]{:S(2)}) %all-to-all-start.7) | async-done | bytes 3145760 | tf_op jit(solution)/shard_map/all_to_all | solution.py:913
  307.4 5.5 %collective-permute-done.9 = bf16[584,128]{1,0:T(8,128)(2,1)S(1)} collective-permute-done((bf16[584,128]{1,0:T(8,128)(2,1)S(1)}, bf16[584,128]{1,0:T(8,128)(2,1)S(1)}, u32[]{:S(2)}, u32[]{:S(2)}) %collective-permute-start.9) | collective-permute-done | bytes 149536 | tf_op jit(solution)/shard_map/ppermute | solution.py:939
  312.9 14.4 %collective-permute-done.8 = bf16[584,128]{1,0:T(8,128)(2,1)S(1)} collective-permute-done((bf16[584,128]{1,0:T(8,128)(2,1)S(1)}, bf16[584,128]{1,0:T(8,128)(2,1)S(1)}, u32[]{:S(2)}, u32[]{:S(2)}) %collective-permute-start.8) | collective-permute-done | bytes 149536 | tf_op jit(solution)/shard_map/ppermute | solution.py:939
  327.6 7.5 %collective-permute-start.12 = (bf16[2336,128]{1,0:T(8,128)(2,1)S(1)}, bf16[2336,128]{1,0:T(8,128)(2,1)S(1)}, u32[]{:S(2)}, u32[]{:S(2)}) collective-permute-start(bf16[2336,128]{1,0:T(8,128)(2,1)S(1)} %bitcast.54), channel_id=1, source_target_pairs={{0,6},{1,7},{2,4},{3,5},{4,2},{5,3},{6,0},{7,1},{8,14},{9,15},{10,... | collective-permute-start | bytes 1794056 | tf_op jit(solution)/shard_map/ppermute | solution.py:939
  342.5 7.9 %combine.1 = bf16[1024,768]{1,0:T(8,128)(2,1)} custom-call(s32[1,1024]{1,0:T(1,128)} %get-tuple-element.151.keyn_ref, f32[1024,768]{1,0:T(8,128)} %get-tuple-element.96.res_ref, bf16[2048,768]{1,0:T(8,128)(2,1)} %bitcast.21.rows_ref), custom_call_target="tpu_custom_call" | custom-call | flops 5750000128 | tf_op jit(solution)/shard_map/combine/pallas_call | solution.py:795
  350.4 6.4 %collective-permute-done.11.rest_2_ = bf16[2336,128]{1,0:T(8,128)(2,1)S(1)} collective-permute-done((bf16[2336,128]{1,0:T(8,128)(2,1)S(1)}, bf16[2336,128]{1,0:T(8,128)(2,1)S(1)}, u32[]{:S(2)}, u32[]{:S(2)}) %collective-permute-start.11) | collective-permute-done | bytes 598048 | tf_op jit(solution)/shard_map/ppermute | solution.py:939
  362.9 9.7 %shared_sums.1 = (f32[768,2304]{1,0:T(8,128)}, f32[768,768]{1,0:T(8,128)}, f32[768]{0:T(1024)}, f32[768]{0:T(1024)}, f32[16,768]{1,0:T(8,128)}, /*index=5*/f32[8,16]{1,0:T(8,128)}) custom-call(s32[1]{0:T(128)} %bitcast.me_ref, bf16[768,2304]{1,0:T(8,128)(2,1)} %w_ref.3, f32[768]{0:T(1024)} %ga_ref.5, bf16[2336,128]{1,0:T(8,128)(2,1)} %bitcast.58, ...), custom_call_target="tpu_custom_call" | custom-call | flops 2300000000 | tf_op jit(solution)/shard_map/shared_sums/pallas_call | solution.py:878
  (110 shorter events, 71.2 us)
Async XLA Ops:
  14.0 46.3 %all-to-all-start.1 = ((bf16[8,256,768]{2,1,0:T(8,128)(2,1)}), bf16[8,256,768]{2,1,0:T(8,128)(2,1)}, u32[]{:S(2)}, u32[]{:S(2)}) async-start(bf16[8,256,768]{2,1,0:T(8,128)(2,1)} %bitcast.43), calls=%async_computation.1 | async-start | bytes 6291456 | tf_op jit(solution)/shard_map/all_to_all | solution.py:913
  60.4 25.4 %all-to-all-start = ((bf16[8,128,768]{2,1,0:T(8,128)(2,1)}), bf16[8,128,768]{2,1,0:T(8,128)(2,1)S(1)}, u32[]{:S(2)}, u32[]{:S(2)}) async-start(bf16[8,128,768]{2,1,0:T(8,128)(2,1)} %bitcast.52), calls=%async_computation | async-start | bytes 3145728 | tf_op jit(solution)/shard_map/all_to_all | solution.py:913
  86.9 27.6 %all-to-all-start.2 = ((bf16[8,128,768]{2,1,0:T(8,128)(2,1)}), bf16[8,128,768]{2,1,0:T(8,128)(2,1)S(1)}, u32[]{:S(2)}, u32[]{:S(2)}) async-start(bf16[8,128,768]{2,1,0:T(8,128)(2,1)} %bitcast.7), calls=%async_computation.2 | async-start | bytes 3145728 | tf_op jit(solution)/shard_map/all_to_all | solution.py:913
  115.7 28.4 %all-to-all-start.3 = ((bf16[8,128,768]{2,1,0:T(8,128)(2,1)}), bf16[8,128,768]{2,1,0:T(8,128)(2,1)S(1)}, u32[]{:S(2)}, u32[]{:S(2)}) async-start(bf16[8,128,768]{2,1,0:T(8,128)(2,1)} %bitcast.51), calls=%async_computation.3 | async-start | bytes 3145728 | tf_op jit(solution)/shard_map/all_to_all | solution.py:913
  145.3 26.7 %all-to-all-start.4 = ((bf16[8,128,768]{2,1,0:T(8,128)(2,1)}), bf16[8,128,768]{2,1,0:T(8,128)(2,1)}, u32[]{:S(2)}, u32[]{:S(2)}) async-start(bf16[8,128,768]{2,1,0:T(8,128)(2,1)} %bitcast.48), calls=%async_computation.4 | async-start | bytes 3145728 | tf_op jit(solution)/shard_map/all_to_all | solution.py:913
  149.6 152.9 %reduce-scatter.3.cloned.1.call-start = ((), (), s32[]{:S(2)}) async-start(), calls=%async_computation.10 | async-start | bytes 7864320 | tf_op jit(solution)/shard_map/reduce_scatter | solution.py:1007
  196.5 17.0 %collective-permute-start = (bf16[4,768,128]{2,1,0:T(8,128)(2,1)}, bf16[4,768,128]{2,1,0:T(8,128)(2,1)S(1)}, u32[]{:S(2)}, u32[]{:S(2)}) collective-permute-start(bf16[4,768,128]{2,1,0:T(8,128)(2,1)} %get-tuple-element.126), channel_id=1, source_target_pairs={{0,1},{1,0},{2,3},{3,2},{4,5},{5,4},{6,7},{7,6},{8,9},{9,8},{10,11... | collective-permute-start | bytes 2359304 | tf_op jit(solution)/shard_map/ppermute | solution.py:925
  216.3 24.4 %all-to-all-start.5 = ((bf16[4,1568,128]{2,1,0:T(8,128)(2,1)}), bf16[4,1568,128]{2,1,0:T(8,128)(2,1)S(1)}, u32[]{:S(2)}, u32[]{:S(2)}) async-start(bf16[4,1568,128]{2,1,0:T(8,128)(2,1)} %pad_maximum_fusion), calls=%async_computation.5 | async-start | bytes 3211264 | tf_op jit(solution)/shard_map/all_to_all | solution.py:934
  241.2 18.8 %all-to-all-start.6 = ((bf16[4,768,128]{2,1,0:T(8,128)(2,1)}), bf16[4,768,128]{2,1,0:T(8,128)(2,1)S(1)}, u32[]{:S(2)}, u32[]{:S(2)}) async-start(bf16[4,768,128]{2,1,0:T(8,128)(2,1)} %add_convert_fusion), calls=%async_computation.6 | async-start | bytes 1572864 | tf_op jit(solution)/shard_map/all_to_all | solution.py:934
  260.2 42.4 %all-to-all-start.7 = ((bf16[8,256,768]{2,1,0:T(8,128)(2,1)}), bf16[8,256,768]{2,1,0:T(8,128)(2,1)}, u32[]{:S(2)}, u32[]{:S(2)}) async-start(bf16[8,256,768]{2,1,0:T(8,128)(2,1)} %bitcast.42), calls=%async_computation.7 | async-start | bytes 6291456 | tf_op jit(solution)/shard_map/all_to_all | solution.py:913
  264.6 108.0 %reduce-scatter.5.cloned.1.call-start = ((), (), s32[]{:S(2)}) async-start(), calls=%async_computation.11 | async-start | bytes 3932160 | tf_op jit(solution)/shard_map/reduce_scatter | solution.py:1049
  264.8 25.6 %collective-permute-start.4 = (bf16[584,128]{1,0:T(8,128)(2,1)S(1)}, bf16[584,128]{1,0:T(8,128)(2,1)S(1)}, u32[]{:S(2)}, u32[]{:S(2)}) collective-permute-start(bf16[584,128]{1,0:T(8,128)(2,1)S(1)} %get-tuple-element.170), channel_id=1, source_target_pairs={{0,8},{8,0},{16,24},{24,16},{1,9},{9,1},{17,25},{25,17},{2,10},{10... | collective-permute-start | bytes 448520 | tf_op jit(solution)/shard_map/ppermute | solution.py:939
  267.0 23.3 %collective-permute-start.6 = (bf16[584,128]{1,0:T(8,128)(2,1)S(1)}, bf16[584,128]{1,0:T(8,128)(2,1)S(1)}, u32[]{:S(2)}, u32[]{:S(2)}) collective-permute-start(bf16[584,128]{1,0:T(8,128)(2,1)S(1)} %get-tuple-element.171), channel_id=1, source_target_pairs={{0,24},{8,16},{16,8},{24,0},{1,25},{9,17},{17,9},{25,1},{2,26},{10... | collective-permute-start | bytes 448520 | tf_op jit(solution)/shard_map/ppermute | solution.py:939
  269.6 26.3 %collective-permute-start.5 = (bf16[584,128]{1,0:T(8,128)(2,1)S(1)}, bf16[584,128]{1,0:T(8,128)(2,1)S(1)}, u32[]{:S(2)}, u32[]{:S(2)}) collective-permute-start(bf16[584,128]{1,0:T(8,128)(2,1)S(1)} %get-tuple-element.172), channel_id=1, source_target_pairs={{0,16},{8,24},{16,0},{24,8},{1,17},{9,25},{17,1},{25,9},{2,18},{10... | collective-permute-start | bytes 448520 | tf_op jit(solution)/shard_map/ppermute | solution.py:939
  302.6 10.3 %collective-permute-start.9 = (bf16[584,128]{1,0:T(8,128)(2,1)S(1)}, bf16[584,128]{1,0:T(8,128)(2,1)S(1)}, u32[]{:S(2)}, u32[]{:S(2)}) collective-permute-start(bf16[584,128]{1,0:T(8,128)(2,1)S(1)} %fusion.3), channel_id=1, source_target_pairs={{0,24},{8,16},{16,8},{24,0},{1,25},{9,17},{17,9},{25,1},{2,26},{10... | collective-permute-start | bytes 448520 | tf_op jit(solution)/shard_map/ppermute | solution.py:939
  306.8 20.5 %collective-permute-start.8 = (bf16[584,128]{1,0:T(8,128)(2,1)S(1)}, bf16[584,128]{1,0:T(8,128)(2,1)S(1)}, u32[]{:S(2)}, u32[]{:S(2)}) collective-permute-start(bf16[584,128]{1,0:T(8,128)(2,1)S(1)} %fusion.3), channel_id=1, source_target_pairs={{0,16},{8,24},{16,0},{24,8},{1,17},{9,25},{17,1},{25,9},{2,18},{10... | collective-permute-start | bytes 448520 | tf_op jit(solution)/shard_map/ppermute | solution.py:939
  306.8 20.5 %collective-permute-start.7 = (bf16[584,128]{1,0:T(8,128)(2,1)S(1)}, bf16[584,128]{1,0:T(8,128)(2,1)S(1)}, u32[]{:S(2)}, u32[]{:S(2)}) collective-permute-start(bf16[584,128]{1,0:T(8,128)(2,1)S(1)} %fusion.3), channel_id=1, source_target_pairs={{0,8},{8,0},{16,24},{24,16},{1,9},{9,1},{17,25},{25,17},{2,10},{10... | collective-permute-start | bytes 448520 | tf_op jit(solution)/shard_map/ppermute | solution.py:939
  327.6 22.8 %collective-permute-start.12 = (bf16[2336,128]{1,0:T(8,128)(2,1)S(1)}, bf16[2336,128]{1,0:T(8,128)(2,1)S(1)}, u32[]{:S(2)}, u32[]{:S(2)}) collective-permute-start(bf16[2336,128]{1,0:T(8,128)(2,1)S(1)} %bitcast.54), channel_id=1, source_target_pairs={{0,6},{1,7},{2,4},{3,5},{4,2},{5,3},{6,0},{7,1},{8,14},{9,15},{10,... | collective-permute-start | bytes 1794056 | tf_op jit(solution)/shard_map/ppermute | solution.py:939
  335.1 21.7 %collective-permute-start.11 = (bf16[2336,128]{1,0:T(8,128)(2,1)S(1)}, bf16[2336,128]{1,0:T(8,128)(2,1)S(1)}, u32[]{:S(2)}, u32[]{:S(2)}) collective-permute-start(bf16[2336,128]{1,0:T(8,128)(2,1)S(1)} %bitcast.55), channel_id=1, source_target_pairs={{0,4},{1,5},{2,6},{3,7},{4,0},{5,1},{6,2},{7,3},{8,12},{9,13},{10,... | collective-permute-start | bytes 1794056 | tf_op jit(solution)/shard_map/ppermute | solution.py:939
  339.0 18.5 %collective-permute-start.10 = (bf16[2336,128]{1,0:T(8,128)(2,1)S(1)}, bf16[2336,128]{1,0:T(8,128)(2,1)}, u32[]{:S(2)}, u32[]{:S(2)}) collective-permute-start(bf16[2336,128]{1,0:T(8,128)(2,1)S(1)} %bitcast.56), channel_id=1, source_target_pairs={{0,2},{1,3},{2,0},{3,1},{4,6},{5,7},{6,4},{7,5},{8,10},{9,11},{10,... | collective-permute-start | bytes 1794056 | tf_op jit(solution)/shard_map/ppermute | solution.py:939
  357.5 2.8 collective-permute-start.13
  357.5 3.6 collective-permute-start.14
  358.0 4.1 %collective-permute-start.15 = (bf16[2336,128]{1,0:T(8,128)(2,1)S(1)}, bf16[2336,128]{1,0:T(8,128)(2,1)S(1)}, u32[]{:S(2)}, u32[]{:S(2)}) collective-permute-start(bf16[2336,128]{1,0:T(8,128)(2,1)S(1)} %collective-permute-done.11.rest_2_), channel_id=1, source_target_pairs={{0,1},{1,0},{2,3},{3,2},{4,5},{5,4},{6,7},{7,6},{8,9},{9,8},{10,11... | collective-permute-start | bytes 1794056 | tf_op jit(solution)/shard_map/ppermute | solution.py:925
  358.0 4.9 %collective-permute-start.16 = (bf16[2336,128]{1,0:T(8,128)(2,1)S(1)}, bf16[2336,128]{1,0:T(8,128)(2,1)}, u32[]{:S(2)}, u32[]{:S(2)}) collective-permute-start(bf16[2336,128]{1,0:T(8,128)(2,1)S(1)} %collective-permute-done.12.rest_3_), channel_id=1, source_target_pairs={{0,1},{1,0},{2,3},{3,2},{4,5},{5,4},{6,7},{7,6},{8,9},{9,8},{10,11... | collective-permute-start | bytes 1794056 | tf_op jit(solution)/shard_map/ppermute | solution.py:925
  (20 other events, 105.8 us)
Sparse Core Ops, SparseCore 0:
  171.3 120.7 reduce-scatter.2
  302.7 64.6 reduce-scatter.4

commit v7 on v6

--- a/solution.py
+++ b/solution.py
@@ -170,9 +170,10 @@
         attn_ref[...] = (x * inv * ga_ref[...].reshape(1, width)).astype(BF16)
 
     attn_in = attn_ref[...]
-    q_ref[...] = mm(attn_in, wq_ref[...]).astype(BF16)
-    k_ref[...] = mm(attn_in, wk_ref[...]).astype(BF16)
-    v_ref[...] = mm(attn_in, wv_ref[...]).astype(BF16)
+    weights = jnp.concatenate([wq_ref[...], wk_ref[...], wv_ref[...]], axis=1)
+    qkv = mm(attn_in, weights)
+    for part, ref in enumerate((q_ref, k_ref, v_ref)):
+        ref[...] = qkv[:, part * both : (part + 1) * both].astype(BF16)
     lane = lax.broadcasted_iota(I32, (QB, PAIR), 1)
     for i in range(count):
         low, high = band(i)
@@ -207,16 +208,16 @@
 
 def attend(tokens, segr, keyr, w_qkv, w_o, ga, gf):
     toks, width = tokens.shape
-    both = 2 * PAIR
+    both = PAIR
     pair_cols = pl.BlockSpec((toks, both), lambda p: (0, p))
     heads = jax.ShapeDtypeStruct((toks, width), BF16)
     weights = [
-        pl.BlockSpec((width, both), lambda p, part=part: (0, part * PAIRS // 2 + p))
+        pl.BlockSpec((width, both), lambda p, part=part: (0, part * PAIRS + p))
         for part in range(3)
     ]
     return pl.pallas_call(
         attend_kernel,
-        grid=(PAIRS // 2,),
+        grid=(PAIRS,),
         in_specs=[
             whole((toks, width)),
             whole((1, toks)),
@@ -230,7 +231,7 @@
             pair_cols,
             pair_cols,
             pair_cols,
-            pl.BlockSpec((2, 2, toks), lambda p: (p, 0, 0)),
+            pl.BlockSpec((1, 2, toks), lambda p: (p, 0, 0)),
             pl.BlockSpec((both, toks), lambda p: (p, 0)),
             whole((toks, width)),
             whole((toks, width)),

time: 388 us -> 388 us (level)
  no operation moved by 1% of the time
where the time goes in v7:
time: 388 us; the launch traced here: 383 us
  Pallas kernels  248 us (64%)
  starting transfers between devices  58.8 us (15%)
  waiting for transfers between devices  48.7 us (13%)
  between operations  14.7 us (4%)
  local copies, waits for them, and re-layouts  6.8 us (2%)
  other arithmetic  6.14 us (2%)
    pallas_call x2, Pallas kernels, expert(): pl.pallas_call(expert_kernel, grid=(hidden // wide,), in_specs=[smem(), w...  47.9 us
    pallas_call x3, Pallas kernels, attend_back(): pl.pallas_call(attend_back_kernel, grid=(1,), in_specs=[smem(), whole((1,...  42.6 us
    pallas_call x1, Pallas kernels, attend(): pl.pallas_call(attend_kernel, grid=(PAIRS,), in_specs=[whole((toks, width...  40.7 us
    ppermute x9, waiting for transfers between devices, xor_permute(): lax.ppermute(value, axis, [(j, j ^ d) for j in range(lax.axis_size(axis))])  32.5 us
    all_to_all x6, starting transfers between devices, exchange(): lax.all_to_all(rows.reshape(peers, -1, width), 'expert', split_axis=0, co...  27 us
    ppermute x9, starting transfers between devices, xor_permute(): lax.ppermute(value, axis, [(j, j ^ d) for j in range(lax.axis_size(axis))])  21.3 us
    pallas_call x2, Pallas kernels, grad_act(): pl.pallas_call(grad_act_kernel, grid=(hidden // wide,), in_specs=[pl.Bloc...  20 us
    pallas_call x1, Pallas kernels, early_grads(): pl.pallas_call(early_grads_kernel, grid=(steps,), in_specs=[whole((width,...  19.6 us
  transfers between devices with their start and end apart: 27, of which 13 were waited for; matrix products, arithmetic and copies ran while one was open for 2% of the time, Pallas kernels for 62%

profile of v7, /device:TPU:0, one launch (start us, length us, event | category | flops | bytes accessed | tf_op | source)
XLA Modules:
  0.0 383.4 jit_solution(10687794397342604181)
XLA Ops:
  7.2 6.9 %place.1 = (s32[1,1024]{1,0:T(1,128)}, s32[1,1024]{1,0:T(1,128)}, bf16[2048,768]{1,0:T(8,128)(2,1)}) custom-call(s32[1,1024]{1,0:T(1,128)} %bitcast.69, bf16[1024,768]{1,0:T(8,128)(2,1)} %cot_ref.3), custom_call_target="tpu_custom_call" | custom-call | flops 5750000128 | tf_op jit(solution)/shard_map/place/pallas_call | solution.py:98
  14.0 5.8 %all-to-all-start.1 = ((bf16[8,256,768]{2,1,0:T(8,128)(2,1)}), bf16[8,256,768]{2,1,0:T(8,128)(2,1)}, u32[]{:S(2)}, u32[]{:S(2)}) async-start(bf16[8,256,768]{2,1,0:T(8,128)(2,1)} %bitcast.43), calls=%async_computation.1 | async-start | bytes 6291456 | tf_op jit(solution)/shard_map/all_to_all | solution.py:914
  19.8 40.7 %attend.1 = (bf16[1024,768]{1,0:T(8,128)(2,1)}, bf16[1024,768]{1,0:T(8,128)(2,1)}, bf16[1024,768]{1,0:T(8,128)(2,1)}, f32[6,2,1024]{2,1,0:T(2,128)}, bf16[768,10...) custom-call(bf16[1024,768]{1,0:T(8,128)(2,1)} %tok_ref.3, ...), custom_call_target="tpu_custom_call" | custom-call | flops 48299999232 | tf_op jit(solution)/shard_map/attend/pallas_call | solution.py:218
  60.5 4.6 %all-to-all-start = ((bf16[8,128,768]{2,1,0:T(8,128)(2,1)}), bf16[8,128,768]{2,1,0:T(8,128)(2,1)S(1)}, u32[]{:S(2)}, u32[]{:S(2)}) async-start(bf16[8,128,768]{2,1,0:T(8,128)(2,1)} %bitcast.52), calls=%async_computation | async-start | bytes 3145728 | tf_op jit(solution)/shard_map/all_to_all | solution.py:914
  65.1 10.0 %grad_act.3 = (bf16[1024,3072]{1,0:T(8,128)(2,1)}, bf16[768,1024]{1,0:T(8,128)(2,1)}) custom-call(bf16[8,2,128,768]{3,2,1,0:T(8,128)(2,1)} %bitcast.6.g_ref, bf16[1,3072,768]{2,1,0:T(8,128)(2,1)} %wout_ref.5), custom_call_target="tpu_custom_call" | custom-call | flops 8049999872 | tf_op jit(solution)/shard_map/grad_act/pallas_call | solution.py:636
  75.1 10.0 %grad_act.2 = (bf16[1024,3072]{1,0:T(8,128)(2,1)}, bf16[768,1024]{1,0:T(8,128)(2,1)}) custom-call(bf16[8,2,128,768]{3,2,1,0:T(8,128)(2,1)} %bitcast.6.g_ref, bf16[1,3072,768]{2,1,0:T(8,128)(2,1)} %wout_ref.5), custom_call_target="tpu_custom_call" | custom-call | flops 8049999872 | tf_op jit(solution)/shard_map/grad_act/pallas_call | solution.py:636
  90.8 24.0 %expert.3 = (bf16[1024,3072]{1,0:T(8,128)(2,1)}, bf16[1024,3072]{1,0:T(8,128)(2,1)}, bf16[768,1024]{1,0:T(8,128)(2,1)}, bf16[1024,768]{1,0:T(8,128)(2,1)}, f32[16,768]{1,0:T(8,128)}, /*index=5*/f32[8,16]{1,0:T(8,128)}) custom-call(s32[1]{0:T(128)} %bitcast.me_ref, bf16[16,768]{1,0:T(8,128)(2,1)} %bitcast.67, f32[8,16]{1,0:T(8,128)} %emb_ref.3, ...), custom_call_target="tpu_custom_call" | custom-call | flops 26449999872 | tf_op jit(solution)/shard_map/expert/pallas_call | solution.py:512
  120.4 23.9 %expert.2 = (bf16[1024,3072]{1,0:T(8,128)(2,1)}, bf16[1024,3072]{1,0:T(8,128)(2,1)}, bf16[768,1024]{1,0:T(8,128)(2,1)}, bf16[1024,768]{1,0:T(8,128)(2,1)}, f32[16,768]{1,0:T(8,128)}, /*index=5*/f32[8,16]{1,0:T(8,128)}) custom-call(s32[1]{0:T(128)} %bitcast.me_ref, bf16[16,768]{1,0:T(8,128)(2,1)} %bitcast.68, f32[8,16]{1,0:T(8,128)} %emb_ref.3, ...), custom_call_target="tpu_custom_call" | custom-call | flops 26449999872 | tf_op jit(solution)/shard_map/expert/pallas_call | solution.py:512
  151.9 19.6 %early_grads.1 = bf16[4,1024,768]{2,1,0:T(8,128)(2,1)} custom-call(bf16[768,1024]{1,0:T(8,128)(2,1)} %get-tuple-element.111.gta_ref, bf16[768,1024]{1,0:T(8,128)(2,1)} %get-tuple-element.112.gtb_ref, bf16[768,1024]{1,0:T(8,128)(2,1)} %get-tuple-element.113.xta_ref, bf16[768,1024]{1,0:T(8,128)(2,1)} %get-tuple-element.114.xtb_ref, ...), custom_call_target="tpu_custom_call" | custom-call | flops 11500000256 | tf_op jit(solution)/shard_map/early_grads/pallas_call | solution.py:574
  172.4 10.1 %combine_back.1 = (f32[1024,768]{1,0:T(8,128)}, bf16[1024,768]{1,0:T(8,128)(2,1)}, f32[1,768]{1,0:T(1,128)}) custom-call(s32[1,1024]{1,0:T(1,128)} %get-tuple-element.90.keyr_ref, f32[1024,768]{1,0:T(8,128)} %get-tuple-element.96.res_ref, bf16[1024,768]{1,0:T(8,128)(2,1)} %cot_ref.3, f32[768]{0:T(1024)} %gf_ref.3, bf16[1024,768]{1,0:T(8,128)(2,1)} %bitcast.47, ...), custom_call_target="tpu_custom_call" | custom-call | flops 115000000512 | tf_op jit(solution)/shard_map/combine_back/pallas_call | solution.py:767
  182.4 14.3 %attend_back.3 = (bf16[4,768,128]{2,1,0:T(8,128)(2,1)}, bf16[4,768,128]{2,1,0:T(8,128)(2,1)}, bf16[3,1024,256]{2,1,0:T(8,128)(2,1)}) custom-call(s32[1]{0:T(128)S(6)} %and.13.core_ref, s32[1,1024]{1,0:T(1,128)} %segr_ref.7, bf16[1024,768]{1,0:T(8,128)(2,1)} %get-tuple-element.91.q_ref, bf16[1024,768]{1,0:T(8,128)(2,1)} %get-tuple-element.92.k_ref, ...), custom_call_target="tpu_custom_call" | custom-call | flops 2300000000 | tf_op jit(solution)/shard_map/attend_back/pallas_call | solution.py:349
  197.2 14.2 %attend_back.4 = (bf16[4,768,128]{2,1,0:T(8,128)(2,1)}, bf16[4,768,128]{2,1,0:T(8,128)(2,1)}, bf16[3,1024,256]{2,1,0:T(8,128)(2,1)}) custom-call(s32[1]{0:T(128)S(6)} %and.13.core_ref, s32[1,1024]{1,0:T(1,128)} %segr_ref.7, bf16[1024,768]{1,0:T(8,128)(2,1)} %get-tuple-element.91.q_ref, bf16[1024,768]{1,0:T(8,128)(2,1)} %get-tuple-element.92.k_ref, ...), custom_call_target="tpu_custom_call" | custom-call | flops 2300000000 | tf_op jit(solution)/shard_map/attend_back/pallas_call | solution.py:349
  220.7 14.2 %attend_back.5 = (bf16[4,768,128]{2,1,0:T(8,128)(2,1)}, bf16[4,768,128]{2,1,0:T(8,128)(2,1)}, bf16[3,1024,256]{2,1,0:T(8,128)(2,1)}) custom-call(s32[1]{0:T(128)S(6)} %and.13.core_ref, s32[1,1024]{1,0:T(1,128)} %segr_ref.7, bf16[1024,768]{1,0:T(8,128)(2,1)} %get-tuple-element.91.q_ref, bf16[1024,768]{1,0:T(8,128)(2,1)} %get-tuple-element.92.k_ref, ...), custom_call_target="tpu_custom_call" | custom-call | flops 11500000256 | tf_op jit(solution)/shard_map/attend_back/pallas_call | solution.py:349
  245.0 15.1 %expert_out.1 = bf16[8,2,128,768]{3,2,1,0:T(8,128)(2,1)} custom-call(bf16[1024,3072]{1,0:T(8,128)(2,1)} %get-tuple-element.115.acta_ref, bf16[1024,3072]{1,0:T(8,128)(2,1)} %get-tuple-element.143.actb_ref, bf16[1,3072,768]{2,1,0:T(8,128)(2,1)} %wout_ref.5), custom_call_target="tpu_custom_call" | custom-call | flops 16099999744 | tf_op jit(solution)/shard_map/expert_out/pallas_call | solution.py:679
  269.8 11.6 %late_grads.1 = bf16[4,512,768]{2,1,0:T(8,128)(2,1)} custom-call(bf16[768,1024]{1,0:T(8,128)(2,1)} %get-tuple-element.113.xta_ref, bf16[768,1024]{1,0:T(8,128)(2,1)} %get-tuple-element.114.xtb_ref, bf16[1024,3072]{1,0:T(8,128)(2,1)} %get-tuple-element.117.gpa_ref, bf16[1024,3072]{1,0:T(8,128)(2,1)} %get-tuple-element.147.gpb_ref), custom_call_target="tpu_custom_call" | custom-call | flops 11500000256 | tf_op jit(solution)/shard_map/late_grads/pallas_call | solution.py:609
  281.4 9.2 %grad_tokens.1 = f32[1024,768]{1,0:T(8,128)} custom-call(bf16[1024,768]{1,0:T(8,128)(2,1)} %tok_ref.3, f32[1024,768]{1,0:T(8,128)} %get-tuple-element.148.gres_ref, f32[768]{0:T(1024)} %ga_ref.5, bf16[768,2304]{1,0:T(8,128)(2,1)} %w_ref.3, bf16[3,1024,256]{2,1,0:T(8,128)(2,1)} %get-tuple-element.123.rest_0_, ...), custom_call_target="tpu_custom_call" | custom-call | flops 10350000128 | tf_op jit(solution)/shard_map/grad_tokens/pallas_call | solution.py:391
  290.6 5.7 %collective-permute-done.5 = bf16[584,128]{1,0:T(8,128)(2,1)S(1)} collective-permute-done((bf16[584,128]{1,0:T(8,128)(2,1)S(1)}, bf16[584,128]{1,0:T(8,128)(2,1)S(1)}, u32[]{:S(2)}, u32[]{:S(2)}) %collective-permute-start.5) | collective-permute-done | bytes 149536 | tf_op jit(solution)/shard_map/ppermute | solution.py:940
  296.4 6.3 %all-to-all-done.7 = bf16[8,256,768]{2,1,0:T(8,128)(2,1)} async-done(((bf16[8,256,768]{2,1,0:T(8,128)(2,1)}), bf16[8,256,768]{2,1,0:T(8,128)(2,1)}, u32[]{:S(2)}, u32[]{:S(2)}) %all-to-all-start.7) | async-done | bytes 3145760 | tf_op jit(solution)/shard_map/all_to_all | solution.py:914
  307.7 5.4 %collective-permute-done.9 = bf16[584,128]{1,0:T(8,128)(2,1)S(1)} collective-permute-done((bf16[584,128]{1,0:T(8,128)(2,1)S(1)}, bf16[584,128]{1,0:T(8,128)(2,1)S(1)}, u32[]{:S(2)}, u32[]{:S(2)}) %collective-permute-start.9) | collective-permute-done | bytes 149536 | tf_op jit(solution)/shard_map/ppermute | solution.py:940
  313.1 14.3 %collective-permute-done.8 = bf16[584,128]{1,0:T(8,128)(2,1)S(1)} collective-permute-done((bf16[584,128]{1,0:T(8,128)(2,1)S(1)}, bf16[584,128]{1,0:T(8,128)(2,1)S(1)}, u32[]{:S(2)}, u32[]{:S(2)}) %collective-permute-start.8) | collective-permute-done | bytes 149536 | tf_op jit(solution)/shard_map/ppermute | solution.py:940
  327.8 7.5 %collective-permute-start.12 = (bf16[2336,128]{1,0:T(8,128)(2,1)S(1)}, bf16[2336,128]{1,0:T(8,128)(2,1)S(1)}, u32[]{:S(2)}, u32[]{:S(2)}) collective-permute-start(bf16[2336,128]{1,0:T(8,128)(2,1)S(1)} %bitcast.54), channel_id=1, source_target_pairs={{0,6},{1,7},{2,4},{3,5},{4,2},{5,3},{6,0},{7,1},{8,14},{9,15},{10,... | collective-permute-start | bytes 1794056 | tf_op jit(solution)/shard_map/ppermute | solution.py:940
  342.8 7.9 %combine.1 = bf16[1024,768]{1,0:T(8,128)(2,1)} custom-call(s32[1,1024]{1,0:T(1,128)} %get-tuple-element.151.keyn_ref, f32[1024,768]{1,0:T(8,128)} %get-tuple-element.96.res_ref, bf16[2048,768]{1,0:T(8,128)(2,1)} %bitcast.21.rows_ref), custom_call_target="tpu_custom_call" | custom-call | flops 5750000128 | tf_op jit(solution)/shard_map/combine/pallas_call | solution.py:796
  350.6 6.4 %collective-permute-done.11.rest_2_ = bf16[2336,128]{1,0:T(8,128)(2,1)S(1)} collective-permute-done((bf16[2336,128]{1,0:T(8,128)(2,1)S(1)}, bf16[2336,128]{1,0:T(8,128)(2,1)S(1)}, u32[]{:S(2)}, u32[]{:S(2)}) %collective-permute-start.11) | collective-permute-done | bytes 598048 | tf_op jit(solution)/shard_map/ppermute | solution.py:940
  363.2 9.7 %shared_sums.1 = (f32[768,2304]{1,0:T(8,128)}, f32[768,768]{1,0:T(8,128)}, f32[768]{0:T(1024)}, f32[768]{0:T(1024)}, f32[16,768]{1,0:T(8,128)}, /*index=5*/f32[8,16]{1,0:T(8,128)}) custom-call(s32[1]{0:T(128)} %bitcast.me_ref, bf16[768,2304]{1,0:T(8,128)(2,1)} %w_ref.3, f32[768]{0:T(1024)} %ga_ref.5, bf16[2336,128]{1,0:T(8,128)(2,1)} %bitcast.58, ...), custom_call_target="tpu_custom_call" | custom-call | flops 2300000000 | tf_op jit(solution)/shard_map/shared_sums/pallas_call | solution.py:879
  (110 shorter events, 71.5 us)
Async XLA Ops:
  14.0 46.5 %all-to-all-start.1 = ((bf16[8,256,768]{2,1,0:T(8,128)(2,1)}), bf16[8,256,768]{2,1,0:T(8,128)(2,1)}, u32[]{:S(2)}, u32[]{:S(2)}) async-start(bf16[8,256,768]{2,1,0:T(8,128)(2,1)} %bitcast.43), calls=%async_computation.1 | async-start | bytes 6291456 | tf_op jit(solution)/shard_map/all_to_all | solution.py:914
  60.5 25.6 %all-to-all-start = ((bf16[8,128,768]{2,1,0:T(8,128)(2,1)}), bf16[8,128,768]{2,1,0:T(8,128)(2,1)S(1)}, u32[]{:S(2)}, u32[]{:S(2)}) async-start(bf16[8,128,768]{2,1,0:T(8,128)(2,1)} %bitcast.52), calls=%async_computation | async-start | bytes 3145728 | tf_op jit(solution)/shard_map/all_to_all | solution.py:914
  87.2 27.6 %all-to-all-start.2 = ((bf16[8,128,768]{2,1,0:T(8,128)(2,1)}), bf16[8,128,768]{2,1,0:T(8,128)(2,1)S(1)}, u32[]{:S(2)}, u32[]{:S(2)}) async-start(bf16[8,128,768]{2,1,0:T(8,128)(2,1)} %bitcast.7), calls=%async_computation.2 | async-start | bytes 3145728 | tf_op jit(solution)/shard_map/all_to_all | solution.py:914
  116.0 28.3 %all-to-all-start.3 = ((bf16[8,128,768]{2,1,0:T(8,128)(2,1)}), bf16[8,128,768]{2,1,0:T(8,128)(2,1)S(1)}, u32[]{:S(2)}, u32[]{:S(2)}) async-start(bf16[8,128,768]{2,1,0:T(8,128)(2,1)} %bitcast.51), calls=%async_computation.3 | async-start | bytes 3145728 | tf_op jit(solution)/shard_map/all_to_all | solution.py:914
  145.4 26.9 %all-to-all-start.4 = ((bf16[8,128,768]{2,1,0:T(8,128)(2,1)}), bf16[8,128,768]{2,1,0:T(8,128)(2,1)}, u32[]{:S(2)}, u32[]{:S(2)}) async-start(bf16[8,128,768]{2,1,0:T(8,128)(2,1)} %bitcast.48), calls=%async_computation.4 | async-start | bytes 3145728 | tf_op jit(solution)/shard_map/all_to_all | solution.py:914
  149.8 152.9 %reduce-scatter.3.cloned.1.call-start = ((), (), s32[]{:S(2)}) async-start(), calls=%async_computation.10 | async-start | bytes 7864320 | tf_op jit(solution)/shard_map/reduce_scatter | solution.py:1008
  196.7 17.0 %collective-permute-start = (bf16[4,768,128]{2,1,0:T(8,128)(2,1)}, bf16[4,768,128]{2,1,0:T(8,128)(2,1)S(1)}, u32[]{:S(2)}, u32[]{:S(2)}) collective-permute-start(bf16[4,768,128]{2,1,0:T(8,128)(2,1)} %get-tuple-element.126), channel_id=1, source_target_pairs={{0,1},{1,0},{2,3},{3,2},{4,5},{5,4},{6,7},{7,6},{8,9},{9,8},{10,11... | collective-permute-start | bytes 2359304 | tf_op jit(solution)/shard_map/ppermute | solution.py:926
  216.6 24.2 %all-to-all-start.5 = ((bf16[4,1568,128]{2,1,0:T(8,128)(2,1)}), bf16[4,1568,128]{2,1,0:T(8,128)(2,1)S(1)}, u32[]{:S(2)}, u32[]{:S(2)}) async-start(bf16[4,1568,128]{2,1,0:T(8,128)(2,1)} %pad_maximum_fusion), calls=%async_computation.5 | async-start | bytes 3211264 | tf_op jit(solution)/shard_map/all_to_all | solution.py:935
  241.3 18.8 %all-to-all-start.6 = ((bf16[4,768,128]{2,1,0:T(8,128)(2,1)}), bf16[4,768,128]{2,1,0:T(8,128)(2,1)S(1)}, u32[]{:S(2)}, u32[]{:S(2)}) async-start(bf16[4,768,128]{2,1,0:T(8,128)(2,1)} %add_convert_fusion), calls=%async_computation.6 | async-start | bytes 1572864 | tf_op jit(solution)/shard_map/all_to_all | solution.py:935
  260.3 42.4 %all-to-all-start.7 = ((bf16[8,256,768]{2,1,0:T(8,128)(2,1)}), bf16[8,256,768]{2,1,0:T(8,128)(2,1)}, u32[]{:S(2)}, u32[]{:S(2)}) async-start(bf16[8,256,768]{2,1,0:T(8,128)(2,1)} %bitcast.42), calls=%async_computation.7 | async-start | bytes 6291456 | tf_op jit(solution)/shard_map/all_to_all | solution.py:914
  264.8 108.1 %reduce-scatter.5.cloned.1.call-start = ((), (), s32[]{:S(2)}) async-start(), calls=%async_computation.11 | async-start | bytes 3932160 | tf_op jit(solution)/shard_map/reduce_scatter | solution.py:1050
  264.9 25.7 %collective-permute-start.4 = (bf16[584,128]{1,0:T(8,128)(2,1)S(1)}, bf16[584,128]{1,0:T(8,128)(2,1)S(1)}, u32[]{:S(2)}, u32[]{:S(2)}) collective-permute-start(bf16[584,128]{1,0:T(8,128)(2,1)S(1)} %get-tuple-element.170), channel_id=1, source_target_pairs={{0,8},{8,0},{16,24},{24,16},{1,9},{9,1},{17,25},{25,17},{2,10},{10... | collective-permute-start | bytes 448520 | tf_op jit(solution)/shard_map/ppermute | solution.py:940
  267.3 23.3 %collective-permute-start.6 = (bf16[584,128]{1,0:T(8,128)(2,1)S(1)}, bf16[584,128]{1,0:T(8,128)(2,1)S(1)}, u32[]{:S(2)}, u32[]{:S(2)}) collective-permute-start(bf16[584,128]{1,0:T(8,128)(2,1)S(1)} %get-tuple-element.171), channel_id=1, source_target_pairs={{0,24},{8,16},{16,8},{24,0},{1,25},{9,17},{17,9},{25,1},{2,26},{10... | collective-permute-start | bytes 448520 | tf_op jit(solution)/shard_map/ppermute | solution.py:940
  269.8 26.5 %collective-permute-start.5 = (bf16[584,128]{1,0:T(8,128)(2,1)S(1)}, bf16[584,128]{1,0:T(8,128)(2,1)S(1)}, u32[]{:S(2)}, u32[]{:S(2)}) collective-permute-start(bf16[584,128]{1,0:T(8,128)(2,1)S(1)} %get-tuple-element.172), channel_id=1, source_target_pairs={{0,16},{8,24},{16,0},{24,8},{1,17},{9,25},{17,1},{25,9},{2,18},{10... | collective-permute-start | bytes 448520 | tf_op jit(solution)/shard_map/ppermute | solution.py:940
  302.7 10.5 %collective-permute-start.9 = (bf16[584,128]{1,0:T(8,128)(2,1)S(1)}, bf16[584,128]{1,0:T(8,128)(2,1)S(1)}, u32[]{:S(2)}, u32[]{:S(2)}) collective-permute-start(bf16[584,128]{1,0:T(8,128)(2,1)S(1)} %fusion.3), channel_id=1, source_target_pairs={{0,24},{8,16},{16,8},{24,0},{1,25},{9,17},{17,9},{25,1},{2,26},{10... | collective-permute-start | bytes 448520 | tf_op jit(solution)/shard_map/ppermute | solution.py:940
  307.0 20.4 %collective-permute-start.8 = (bf16[584,128]{1,0:T(8,128)(2,1)S(1)}, bf16[584,128]{1,0:T(8,128)(2,1)S(1)}, u32[]{:S(2)}, u32[]{:S(2)}) collective-permute-start(bf16[584,128]{1,0:T(8,128)(2,1)S(1)} %fusion.3), channel_id=1, source_target_pairs={{0,16},{8,24},{16,0},{24,8},{1,17},{9,25},{17,1},{25,9},{2,18},{10... | collective-permute-start | bytes 448520 | tf_op jit(solution)/shard_map/ppermute | solution.py:940
  307.1 20.4 %collective-permute-start.7 = (bf16[584,128]{1,0:T(8,128)(2,1)S(1)}, bf16[584,128]{1,0:T(8,128)(2,1)S(1)}, u32[]{:S(2)}, u32[]{:S(2)}) collective-permute-start(bf16[584,128]{1,0:T(8,128)(2,1)S(1)} %fusion.3), channel_id=1, source_target_pairs={{0,8},{8,0},{16,24},{24,16},{1,9},{9,1},{17,25},{25,17},{2,10},{10... | collective-permute-start | bytes 448520 | tf_op jit(solution)/shard_map/ppermute | solution.py:940
  327.8 22.8 %collective-permute-start.12 = (bf16[2336,128]{1,0:T(8,128)(2,1)S(1)}, bf16[2336,128]{1,0:T(8,128)(2,1)S(1)}, u32[]{:S(2)}, u32[]{:S(2)}) collective-permute-start(bf16[2336,128]{1,0:T(8,128)(2,1)S(1)} %bitcast.54), channel_id=1, source_target_pairs={{0,6},{1,7},{2,4},{3,5},{4,2},{5,3},{6,0},{7,1},{8,14},{9,15},{10,... | collective-permute-start | bytes 1794056 | tf_op jit(solution)/shard_map/ppermute | solution.py:940
  335.4 21.7 %collective-permute-start.11 = (bf16[2336,128]{1,0:T(8,128)(2,1)S(1)}, bf16[2336,128]{1,0:T(8,128)(2,1)S(1)}, u32[]{:S(2)}, u32[]{:S(2)}) collective-permute-start(bf16[2336,128]{1,0:T(8,128)(2,1)S(1)} %bitcast.55), channel_id=1, source_target_pairs={{0,4},{1,5},{2,6},{3,7},{4,0},{5,1},{6,2},{7,3},{8,12},{9,13},{10,... | collective-permute-start | bytes 1794056 | tf_op jit(solution)/shard_map/ppermute | solution.py:940
  339.3 18.5 %collective-permute-start.10 = (bf16[2336,128]{1,0:T(8,128)(2,1)S(1)}, bf16[2336,128]{1,0:T(8,128)(2,1)}, u32[]{:S(2)}, u32[]{:S(2)}) collective-permute-start(bf16[2336,128]{1,0:T(8,128)(2,1)S(1)} %bitcast.56), channel_id=1, source_target_pairs={{0,2},{1,3},{2,0},{3,1},{4,6},{5,7},{6,4},{7,5},{8,10},{9,11},{10,... | collective-permute-start | bytes 1794056 | tf_op jit(solution)/shard_map/ppermute | solution.py:940
  357.7 2.8 collective-permute-start.13
  357.7 3.6 collective-permute-start.14
  358.2 4.1 %collective-permute-start.15 = (bf16[2336,128]{1,0:T(8,128)(2,1)S(1)}, bf16[2336,128]{1,0:T(8,128)(2,1)S(1)}, u32[]{:S(2)}, u32[]{:S(2)}) collective-permute-start(bf16[2336,128]{1,0:T(8,128)(2,1)S(1)} %collective-permute-done.11.rest_2_), channel_id=1, source_target_pairs={{0,1},{1,0},{2,3},{3,2},{4,5},{5,4},{6,7},{7,6},{8,9},{9,8},{10,11... | collective-permute-start | bytes 1794056 | tf_op jit(solution)/shard_map/ppermute | solution.py:926
  358.2 4.9 %collective-permute-start.16 = (bf16[2336,128]{1,0:T(8,128)(2,1)S(1)}, bf16[2336,128]{1,0:T(8,128)(2,1)}, u32[]{:S(2)}, u32[]{:S(2)}) collective-permute-start(bf16[2336,128]{1,0:T(8,128)(2,1)S(1)} %collective-permute-done.12.rest_3_), channel_id=1, source_target_pairs={{0,1},{1,0},{2,3},{3,2},{4,5},{5,4},{6,7},{7,6},{8,9},{9,8},{10,11... | collective-permute-start | bytes 1794056 | tf_op jit(solution)/shard_map/ppermute | solution.py:926
  (20 other events, 106.2 us)
Sparse Core Ops, SparseCore 0:
  171.7 120.8 reduce-scatter.2
  302.8 64.8 reduce-scatter.4
